TPU v7x, 32 devices: a whole 2x2x4 slice. The times are simulated.
32 devices in a mesh: dp: 8 (over z, y), frame: 4 (over x, core).
Axes of the slice: x: 2, y: 2, z: 4, core: 2. Of those that a mesh axis runs over, the one named last changes fastest.
Arguments:
- tokens: bfloat16 [16384, 768], P(('dp', 'frame')), may hold values from -6 to 6
- frames: bfloat16 [256, 1500, 768], P('dp', 'frame'), may hold values from -6 to 6
- cotangent: bfloat16 [16384, 768], P(('dp', 'frame')), may hold values from -6 to 6
- buckets: int32 [256], P('dp'), may hold values from 0 to 7, as said below
- lengths: int32 [256], P('dp'), may hold values from 0 to 448, as said below
- slot_of: int32 [96], replicated, may hold values from 0 to 127, as said below
- master: float32 [128, 128, 768], P('dp', None, 'frame'), may hold values from -3 to 3
- first_moment: float32 [128, 128, 768], P('dp', None, 'frame'), may hold values from -2 to 2
- second_moment: float32 [128, 128, 768], P('dp', None, 'frame'), may hold values from 0.01 to 0.1
- vectors: float32 [19, 768], replicated, may hold values from -3 to 3
- vector_first: float32 [19, 768], replicated, may hold values from -6 to 6
- vector_second: float32 [19, 768], replicated, may hold values from 0.05 to 0.5
Outputs:
- out_tokens: float32 [16384, 768], P(('dp', 'frame'))
- token_grads: float32 [16384, 768], P(('dp', 'frame'))
- matrix_grads: float32 [128, 128, 768], P('dp', None, 'frame')
- matrix_first: float32 [128, 128, 768], P('dp', None, 'frame')
- matrix_second: float32 [128, 128, 768], P('dp', None, 'frame')
- matrix_weights: float32 [128, 128, 768], P('dp', None, 'frame')
- vector_grads: float32 [19, 768], replicated
- vector_first_new: float32 [19, 768], replicated
- vector_second_new: float32 [19, 768], replicated
- vector_weights: float32 [19, 768], replicated
Inputs may be any that keep to these rules, and one draw needn't show every extreme that they name: `buckets`: A device's slots take 8 units or fewer together, and some device takes exactly 8; the first slot of every device is taken; some slot has 7 units. `lengths`: 0 for an empty slot, else more than 64 (b - 1) and at most 64 b for the slot's bucket b; some slot has 448. `slot_of`: distinct slots; slot s belongs to dp index s // 16; some dp index owns 16 panels.
All inputs are finite; a program needn't handle non-finite values.
Results may differ from a plain program's by a relative error of at most 0.025.
The roundings to bfloat16 on the way count: a program that leaves them out, or rounds other values in their place, can miss the bound.
Values may be sent and summed in bfloat16 or wider, within the bound.
No kernel may reach another device: no remote copies, remote signals or barrier semaphores. Data moves between devices by JAX's collectives and lax.ppermute only.
A program may use at most 448 MiB of HBM per device.

v0:
```python
import math

import jax
import jax.numpy as jnp
from jax import lax
from jax.sharding import PartitionSpec as P

D = 768
HEADS = 12
FF = 3072
BLOCK = 64
PANEL = 128
STEP = 4


EPS_NORM = 1e-05
EPS_ADAM = 1e-08
BETA_ONE = 0.5
BETA_TWO = 0.5
RATE_MATRIX = 0.04
RATE_VECTOR = 0.2
DECAY_MATRIX = 0.01
MASKED = -1e30


def joined(part, axis, combine):
    gathered = jax.tree.map(lambda a: lax.all_gather(a, axis), part)

    def take(source):
        return jax.tree.map(lambda a: lax.dynamic_index_in_dim(a, source, 0, False), gathered)

    return lax.fori_loop(
        1, lax.axis_size(axis), lambda source, state: combine(state, take(source)), take(0)
    )


def layer_norm(values, scaling, offset):
    average = jnp.mean(values, axis=-1, keepdims=True)
    centred = values - average
    spread = jnp.mean(centred * centred, axis=-1, keepdims=True)
    return centred * lax.rsqrt(spread + EPS_NORM) * scaling + offset


def mat_dot(operand, factor):
    return jnp.dot(operand, factor, preferred_element_type=jnp.float32)


def row_layout(bucket, length, row_count, block_rows):
    slot_count = bucket.shape[0]
    starts = jnp.cumsum(bucket, dtype=jnp.int32) - bucket
    row_ids = jnp.arange(row_count, dtype=jnp.int32)
    slot_ids = jnp.arange(slot_count, dtype=jnp.int32)
    block_ids = row_ids // block_rows
    inside = (block_ids[:, None] >= starts[None, :]) & (
        block_ids[:, None] < (starts + bucket)[None, :]
    )
    member = jnp.where(
        jnp.any(inside, axis=1),
        jnp.sum(jnp.where(inside, slot_ids[None, :], 0), axis=1, dtype=jnp.int32),
        -1,
    )
    live_rows = jnp.any(
        inside & (row_ids[:, None] - block_rows * starts[None, :] < length[None, :]), axis=1
    )
    block_owner = jnp.maximum(member.reshape(row_count // block_rows, block_rows)[:, 0], 0)
    return (member, live_rows, block_owner)


def adam_update(gradient, first_moment, second_moment, weight, step_rate, decay_rate):
    first_new = BETA_ONE * first_moment + (1.0 - BETA_ONE) * gradient
    second_new = BETA_TWO * second_moment + (1.0 - BETA_TWO) * gradient * gradient
    fix_one = 1.0 - BETA_ONE**STEP
    fix_two = 1.0 - BETA_TWO**STEP
    update = first_new / fix_one / (jnp.sqrt(second_new / fix_two) + EPS_ADAM)
    return (first_new, second_new, weight - step_rate * (update + decay_rate * weight))


def merge_pair(earlier, later):
    out_early, lse_early = earlier
    out_late, lse_late = later
    highest = jnp.maximum(lse_early, lse_late)
    weight_early = jnp.exp(lse_early - highest)
    weight_late = jnp.exp(lse_late - highest)
    summed = weight_early + weight_late
    out_shape = out_early.shape
    head_count = lse_early.shape[-1]
    blended = (
        out_early.reshape(out_shape[0], head_count, -1) * (weight_early / summed)[:, :, None]
        + out_late.reshape(out_shape[0], head_count, -1) * (weight_late / summed)[:, :, None]
    )
    return (blended.reshape(out_shape), highest + jnp.log(summed))


def cross_tables(block_query, owners, key_table, value_table):
    unit_total, row_total, head_total, head_width = block_query.shape
    frame_total = key_table.shape[1]
    block_key = key_table[owners].reshape(unit_total, frame_total, head_total, head_width)
    block_value = value_table[owners].reshape(unit_total, frame_total, head_total, head_width)
    raw_scores = jnp.einsum(
        "bqhd,bfhd->bhqf", block_query, block_key, preferred_element_type=jnp.float32
    )
    return (raw_scores, block_key, block_value)


def cross_forward(block_query, owners, key_table, value_table):
    unit_total, row_total, head_total, head_width = block_query.shape
    block_scores, block_key, block_value = cross_tables(block_query, owners, key_table, value_table)
    highest = jnp.max(block_scores, axis=-1, keepdims=True)
    exponentials = jnp.exp(block_scores - highest)
    summed = jnp.sum(exponentials, axis=-1, keepdims=True)
    block_probs = (exponentials / summed).astype(jnp.bfloat16)
    partial_block = jnp.einsum(
        "bhqf,bfhd->bqhd", block_probs, block_value, preferred_element_type=jnp.float32
    )
    block_lse = (highest + jnp.log(summed))[..., 0].transpose(0, 2, 1)
    return (
        partial_block.reshape(unit_total * row_total, head_total * head_width),
        block_lse.reshape(unit_total * row_total, head_total),
    )


def cross_backward(carried, packed, key_table, value_table):
    key_sum, value_sum = carried
    block_query, block_grad, block_lse, block_delta, owners = packed
    unit_total, row_total, head_total, head_width = block_query.shape
    frame_total = key_table.shape[1]
    block_scores, block_key, block_value = cross_tables(block_query, owners, key_table, value_table)
    block_probs = jnp.exp(block_scores - block_lse.transpose(0, 2, 1)[..., None])
    grad_probs = jnp.einsum(
        "bqhd,bfhd->bhqf", block_grad, block_value, preferred_element_type=jnp.float32
    )
    grad_scores = (block_probs * (grad_probs - block_delta.transpose(0, 2, 1)[..., None])).astype(
        jnp.bfloat16
    )
    grad_query = jnp.einsum(
        "bhqf,bfhd->bqhd", grad_scores, block_key, preferred_element_type=jnp.float32
    )
    grad_key = jnp.einsum(
        "bhqf,bqhd->bfhd", grad_scores, block_query, preferred_element_type=jnp.float32
    ).reshape(unit_total, frame_total, head_total * head_width)
    grad_value = jnp.einsum(
        "bhqf,bqhd->bfhd",
        block_probs.astype(jnp.bfloat16),
        block_grad,
        preferred_element_type=jnp.float32,
    ).reshape(unit_total, frame_total, head_total * head_width)
    key_sum = key_sum.at[owners].add(grad_key)
    value_sum = value_sum.at[owners].add(grad_value)
    return (
        (key_sum, value_sum),
        grad_query.reshape(unit_total * row_total, head_total * head_width),
    )


def body(
    tokens,
    frames,
    cotangent,
    buckets,
    lengths,
    slot_of,
    master,
    first_moment,
    second_moment,
    vectors,
    vector_first,
    vector_second,
):
    row_count = tokens.shape[0]
    group_count = lax.axis_size("dp")
    frame_count = lax.axis_size("frame")
    frame_index = lax.axis_index("frame")
    group_index = lax.axis_index("dp")
    slot_cap = master.shape[0]
    slot_total = slot_cap * group_count
    column_count = master.shape[2]
    panel_total = slot_of.shape[0]
    group_slots = buckets.shape[0]
    slots_device = group_slots // frame_count
    head_size = D // HEADS
    query_scale = head_size ** (-0.5)
    blocks_ff = FF // D
    gathered = lax.all_gather(
        master.astype(jnp.bfloat16)[None], ("dp", "frame"), axis=0, tiled=True
    )
    gathered = gathered.reshape(group_count, frame_count, slot_cap, PANEL, column_count)
    gathered = gathered.transpose(0, 2, 3, 1, 4).reshape(
        slot_total, PANEL, frame_count * column_count
    )
    panels = gathered[slot_of]
    square_count = 8 * D // PANEL
    expand_count = FF // PANEL
    square = panels[:square_count].reshape(8, D, D)
    expand = panels[square_count : square_count + expand_count].reshape(blocks_ff, D, D)
    contract = panels[square_count + expand_count :].reshape(FF, D)
    own_bucket = lax.dynamic_slice_in_dim(buckets, frame_index * slots_device, slots_device)
    own_length = lax.dynamic_slice_in_dim(lengths, frame_index * slots_device, slots_device)
    member, live_rows, own_owner = row_layout(own_bucket, own_length, row_count, BLOCK)
    group_owner = jax.vmap(
        lambda bucket_part, length_part: row_layout(bucket_part, length_part, row_count, BLOCK)[2]
    )(buckets.reshape(frame_count, slots_device), lengths.reshape(frame_count, slots_device))
    group_owner = (
        group_owner + slots_device * jnp.arange(frame_count, dtype=jnp.int32)[:, None]
    ).reshape(-1)
    inputs = tokens.astype(jnp.float32)
    normed = layer_norm(inputs, vectors[0], vectors[1]).astype(jnp.bfloat16)
    self_query = (query_scale * (mat_dot(normed, square[0]) + vectors[2])).astype(jnp.bfloat16)
    self_key = mat_dot(normed, square[1]).astype(jnp.bfloat16)
    self_value = (mat_dot(normed, square[2]) + vectors[3]).astype(jnp.bfloat16)
    query_heads = self_query.reshape(row_count, HEADS, head_size)
    key_heads = self_key.reshape(row_count, HEADS, head_size)
    value_heads = self_value.reshape(row_count, HEADS, head_size)
    row_ids = jnp.arange(row_count, dtype=jnp.int32)
    query_block = min(512, row_count)
    block_starts = jnp.arange(row_count // query_block, dtype=jnp.int32) * query_block

    def self_scores(start):
        block_rows = start + jnp.arange(query_block, dtype=jnp.int32)
        visible = (
            (member[:, None] == member[None, :])
            & (row_ids[None, :] <= block_rows[:, None])
            & (live_rows[None, :] | (row_ids[None, :] == block_rows[:, None]))
        )
        raw_scores = jnp.einsum(
            "qhd,khd->hqk", query_heads, key_heads, preferred_element_type=jnp.float32
        )
        return (jnp.where(visible[None], raw_scores, MASKED), query_heads)

    def self_forward(start):
        block_scores = self_scores(start)[0]
        highest = jnp.max(block_scores, axis=-1, keepdims=True)
        exponentials = jnp.exp(block_scores - highest)
        summed = jnp.sum(exponentials, axis=-1, keepdims=True)
        block_probs = (exponentials / summed).astype(jnp.bfloat16)
        block_out = jnp.einsum(
            "hqk,khd->qhd", block_probs, value_heads, preferred_element_type=jnp.float32
        )
        return (block_out.reshape(query_block, D).astype(jnp.bfloat16), highest + jnp.log(summed))

    attended, self_lse = lax.map(self_forward, block_starts)
    attended = attended.reshape(row_count, D)
    first_sum = inputs + (mat_dot(attended, square[3]) + vectors[4])
    crossed = layer_norm(first_sum, vectors[5], vectors[6]).astype(jnp.bfloat16)
    cross_query = (query_scale * (mat_dot(crossed, square[4]) + vectors[7])).astype(jnp.bfloat16)
    step_units = 8
    query_rows = lax.all_gather(cross_query, "frame", axis=0, tiled=True)
    key_table = jnp.einsum(
        "tfd,de->tfe", frames, square[5], preferred_element_type=jnp.float32
    ).astype(jnp.bfloat16)
    value_table = (
        jnp.einsum("tfd,de->tfe", frames, square[6], preferred_element_type=jnp.float32)
        + vectors[8]
    ).astype(jnp.bfloat16)
    step_count = group_owner.shape[0] // step_units
    query_steps = query_rows.reshape(step_count, step_units, BLOCK, HEADS, head_size)
    owner_steps = group_owner.reshape(step_count, step_units)
    partial_out, partial_lse = lax.map(
        lambda packed: cross_forward(packed[0], packed[1], key_table, value_table),
        (query_steps, owner_steps),
    )
    partial_out = partial_out.reshape(-1, D)
    partial_lse = partial_lse.reshape(-1, HEADS)
    merged_out, merged_lse = joined((partial_out, partial_lse), "frame", merge_pair)
    own_out = lax.dynamic_slice_in_dim(merged_out, frame_index * row_count, row_count)
    cross_out = own_out.astype(jnp.bfloat16)
    second_sum = first_sum + (mat_dot(cross_out, square[7]) + vectors[9])
    mlp_input = layer_norm(second_sum, vectors[10], vectors[11]).astype(jnp.bfloat16)
    hidden_pre = jnp.einsum(
        "rd,cde->rce", mlp_input, expand, preferred_element_type=jnp.float32
    ).reshape(row_count, FF) + vectors[12 : 12 + blocks_ff].reshape(FF)
    activated = jax.nn.gelu(hidden_pre, approximate=False).astype(jnp.bfloat16)
    third_sum = second_sum + (mat_dot(activated, contract) + vectors[12 + blocks_ff])
    live_float = live_rows.astype(jnp.float32)[:, None]
    result, final_back = jax.vjp(
        layer_norm, third_sum, vectors[13 + blocks_ff], vectors[14 + blocks_ff]
    )
    out_tokens = result * live_float
    upstream = cotangent.astype(jnp.float32) * live_float
    grad_third, grad_final_gain, grad_final_shift = final_back(upstream)
    grad_mlp = grad_third.astype(jnp.bfloat16)
    grad_contract_bias = jnp.sum(grad_mlp.astype(jnp.float32), axis=0)
    grad_contract = mat_dot(activated.T, grad_mlp)
    grad_activated = mat_dot(grad_mlp, contract.T)
    gelu_back = jax.vjp(lambda values: jax.nn.gelu(values, approximate=False), hidden_pre)[1]
    grad_hidden = gelu_back(grad_activated)[0].astype(jnp.bfloat16)
    grad_expand_bias = jnp.sum(grad_hidden.astype(jnp.float32), axis=0).reshape(blocks_ff, D)
    hidden_blocks = grad_hidden.reshape(row_count, blocks_ff, D)
    grad_expand = jnp.einsum(
        "rd,rce->cde", mlp_input, hidden_blocks, preferred_element_type=jnp.float32
    )
    grad_mixed = jnp.einsum(
        "rce,cde->rd", hidden_blocks, expand, preferred_element_type=jnp.float32
    )
    norm_three_back = jax.vjp(layer_norm, second_sum, vectors[10], vectors[11])[1]
    grad_second_norm, grad_gain_three, grad_shift_three = norm_three_back(grad_mixed)
    grad_second = grad_third + grad_second_norm
    grad_cross_branch = grad_second.astype(jnp.bfloat16)
    grad_co_bias = jnp.sum(grad_cross_branch.astype(jnp.float32), axis=0)
    grad_co = mat_dot(cross_out.T, grad_cross_branch)
    grad_cross_out = mat_dot(grad_cross_branch, square[7].T).astype(jnp.bfloat16)
    rows_grad_out = lax.all_gather(grad_cross_out, "frame", axis=0, tiled=True)
    rows_delta = jnp.sum(
        (rows_grad_out.astype(jnp.float32) * merged_out).reshape(
            frame_count * row_count, HEADS, head_size
        ),
        axis=-1,
    )
    grad_steps = rows_grad_out.reshape(step_count, step_units, BLOCK, HEADS, head_size)
    lse_steps = merged_lse.reshape(step_count, step_units, BLOCK, HEADS)
    delta_steps = rows_delta.reshape(step_count, step_units, BLOCK, HEADS)
    zeros_frames = jnp.zeros(frames.shape, jnp.float32)
    frame_totals, query_parts = lax.scan(
        lambda carried, packed: cross_backward(carried, packed, key_table, value_table),
        (zeros_frames, zeros_frames),
        (query_steps, grad_steps, lse_steps, delta_steps, owner_steps),
    )
    query_parts = query_parts.reshape(-1, D)
    query_summed = lax.psum(query_parts, "frame")
    own_query_grad = lax.dynamic_slice_in_dim(query_summed, frame_index * row_count, row_count)
    grad_cq = own_query_grad.astype(jnp.bfloat16) * query_scale
    grad_cq_bias = jnp.sum(grad_cq.astype(jnp.float32), axis=0)
    grad_cq_weight = mat_dot(crossed.T, grad_cq)
    grad_crossed = mat_dot(grad_cq, square[4].T)
    key_low = frame_totals[0].astype(jnp.bfloat16)
    value_low = frame_totals[1].astype(jnp.bfloat16)
    grad_ck = jnp.einsum("tfd,tfe->de", frames, key_low, preferred_element_type=jnp.float32)
    grad_cv = jnp.einsum("tfd,tfe->de", frames, value_low, preferred_element_type=jnp.float32)
    grad_cv_bias = jnp.sum(value_low.astype(jnp.float32), axis=(0, 1))
    norm_two_back = jax.vjp(layer_norm, first_sum, vectors[5], vectors[6])[1]
    grad_first_norm, grad_gain_two, grad_shift_two = norm_two_back(grad_crossed)
    grad_first = grad_second + grad_first_norm
    grad_self_branch = grad_first.astype(jnp.bfloat16)
    grad_o_bias = jnp.sum(grad_self_branch.astype(jnp.float32), axis=0)
    grad_o = mat_dot(attended.T, grad_self_branch)
    grad_attended = (
        mat_dot(grad_self_branch, square[3].T)
        .astype(jnp.bfloat16)
        .reshape(row_count, HEADS, head_size)
    )

    def self_backward(carried, packed):
        key_sum, value_sum = carried
        start, block_lse = packed
        block_scores, block_query = self_scores(start)
        block_probs = jnp.exp(block_scores - block_lse)
        grad_probs = jnp.einsum(
            "qhd,khd->hqk", grad_attended, value_heads, preferred_element_type=jnp.float32
        )
        row_delta = jnp.sum(block_probs * grad_probs, axis=-1, keepdims=True)
        grad_scores = (block_probs * (grad_probs - row_delta)).astype(jnp.bfloat16)
        grad_query = jnp.einsum(
            "hqk,khd->qhd", grad_scores, key_heads, preferred_element_type=jnp.float32
        )
        key_sum = key_sum + jnp.einsum(
            "hqk,qhd->khd", grad_scores, block_query, preferred_element_type=jnp.float32
        )
        value_sum = value_sum + jnp.einsum(
            "hqk,qhd->khd",
            block_probs.astype(jnp.bfloat16),
            grad_attended,
            preferred_element_type=jnp.float32,
        )
        return ((key_sum, value_sum), grad_query.reshape(query_block, D))

    zeros_heads = jnp.zeros((row_count, HEADS, head_size), jnp.float32)
    head_totals, query_total = lax.scan(
        self_backward, (zeros_heads, zeros_heads), (block_starts, self_lse)
    )
    grad_query = query_total.reshape(row_count, D).astype(jnp.bfloat16) * query_scale
    grad_key = head_totals[0].reshape(row_count, D).astype(jnp.bfloat16)
    grad_value = head_totals[1].reshape(row_count, D).astype(jnp.bfloat16)
    grad_q_bias = jnp.sum(grad_query.astype(jnp.float32), axis=0)
    grad_v_bias = jnp.sum(grad_value.astype(jnp.float32), axis=0)
    grad_wq = mat_dot(normed.T, grad_query)
    grad_wk = mat_dot(normed.T, grad_key)
    grad_wv = mat_dot(normed.T, grad_value)
    grad_normed = (
        mat_dot(grad_query, square[0].T)
        + mat_dot(grad_key, square[1].T)
        + mat_dot(grad_value, square[2].T)
    )
    norm_one_back = jax.vjp(layer_norm, inputs, vectors[0], vectors[1])[1]
    grad_input_norm, grad_gain_one, grad_shift_one = norm_one_back(grad_normed)
    token_grads = grad_first + grad_input_norm
    grad_square = jnp.stack(
        [grad_wq, grad_wk, grad_wv, grad_o, grad_cq_weight, grad_ck, grad_cv, grad_co]
    )
    grad_panels = jnp.concatenate(
        [
            grad_square.reshape(-1, PANEL, D),
            grad_expand.reshape(-1, PANEL, D),
            grad_contract.reshape(-1, PANEL, D),
        ],
        axis=0,
    )
    grad_vectors = jnp.concatenate(
        [
            jnp.stack(
                [
                    grad_gain_one,
                    grad_shift_one,
                    grad_q_bias,
                    grad_v_bias,
                    grad_o_bias,
                    grad_gain_two,
                    grad_shift_two,
                    grad_cq_bias,
                    grad_cv_bias,
                    grad_co_bias,
                    grad_gain_three,
                    grad_shift_three,
                ]
            ),
            grad_expand_bias,
            jnp.stack([grad_contract_bias, grad_final_gain, grad_final_shift]),
        ],
        axis=0,
    )
    slot_ids = jnp.arange(slot_total, dtype=jnp.int32)
    matches = slot_of[:, None] == slot_ids[None, :]
    panel_of_slot = jnp.sum(
        jnp.where(matches, jnp.arange(panel_total, dtype=jnp.int32)[:, None], 0),
        axis=0,
        dtype=jnp.int32,
    )
    used_slots = jnp.any(matches, axis=0)
    by_quarter = (
        grad_panels.reshape(panel_total, PANEL, frame_count, column_count)
        .transpose(2, 0, 1, 3)
        .reshape(frame_count * panel_total, PANEL, column_count)
    )
    quarter_ids = jnp.arange(frame_count, dtype=jnp.int32)
    picks = (
        quarter_ids[None, :, None] * panel_total + panel_of_slot.reshape(group_count, 1, slot_cap)
    ).reshape(-1)
    owned = lax.psum_scatter(by_quarter[picks], ("dp", "frame"), scatter_dimension=0, tiled=True)
    vector_total = lax.psum(grad_vectors, ("dp", "frame"))
    grad_scale = 1.0 / math.sqrt(row_count * group_count * frame_count)
    own_used = lax.dynamic_slice_in_dim(used_slots, group_index * slot_cap, slot_cap)[:, None, None]
    matrix_grads = jnp.where(own_used, owned * grad_scale, 0.0)
    matrix_first, matrix_second, matrix_weights = adam_update(
        matrix_grads, first_moment, second_moment, master, RATE_MATRIX, DECAY_MATRIX
    )
    matrix_first = jnp.where(own_used, matrix_first, 0.0)
    matrix_second = jnp.where(own_used, matrix_second, 0.0)
    matrix_weights = jnp.where(own_used, matrix_weights, 0.0)
    vector_grads = vector_total * grad_scale
    vector_first_new, vector_second_new, vector_weights = adam_update(
        vector_grads, vector_first, vector_second, vectors, RATE_VECTOR, 0.0
    )
    return (
        out_tokens,
        token_grads,
        matrix_grads,
        matrix_first,
        matrix_second,
        matrix_weights,
        vector_grads,
        vector_first_new,
        vector_second_new,
        vector_weights,
    )


def solution(mesh):
    in_specs = (
        P(("dp", "frame"), None),
        P("dp", "frame", None),
        P(("dp", "frame"), None),
        P("dp"),
        P("dp"),
        P(),
        P("dp", None, "frame"),
        P("dp", None, "frame"),
        P("dp", None, "frame"),
        P(),
        P(),
        P(),
    )
    out_specs = (
        P(("dp", "frame"), None),
        P(("dp", "frame"), None),
        P("dp", None, "frame"),
        P("dp", None, "frame"),
        P("dp", None, "frame"),
        P("dp", None, "frame"),
        P(),
        P(),
        P(),
        P(),
    )
    return jax.shard_map(body, mesh=mesh, in_specs=in_specs, out_specs=out_specs, check_vma=False)
```

profile of v0, /device:TPU:0, one launch (start us, length us, event | category | flops | bytes accessed | tf_op | source)
XLA Modules:
  0.0 2360.5 jit_solution(12863526655799975130)
XLA Ops:
  13.9 155.0 %all-gather.12.cloned.1.call-done = bf16[512,128,192]{1,2,0:T(8,128)(2,1)} async-done(((bf16[16,128,192]{1,2,0:T(8,128)(2,1)}), bf16[512,128,192]{1,2,0:T(8,128)(2,1)}) %all-gather.12.cloned.1.call-update) | async-done | bytes 25165840 | tf_op jit(solution)/shard_map/all_gather | solution.py:183
  168.9 23.0 copy.223
  191.9 17.3 gather_fusion.4
  254.0 55.6 %convert_bitcast_fusion = bf16[32,375,768]{2,1,0:T(8,128)(2,1)} fusion(bf16[768,768,1]{1,0,2:T(8,128)(2,1)S(1)} %bitcast.374, bf16[32,375,768]{2,0,1:T(8,128)(2,1)} %param.19), kind=kOutput, calls=%fused_computation.71 | convolution fusion | flops 14164992000 | bytes 38043648 | tf_op jit(solution)/shard_map/tfd,de->tfe/dot_general | solution.py:247
  310.1 56.2 %fusion.31 = bf16[32,375,768]{2,1,0:T(8,128)(2,1)} fusion(f32[768]{0:T(1024)S(1)} %get-tuple-element.431, bf16[768,768,1]{1,0,2:T(8,128)(2,1)S(1)} %bitcast.373, bf16[32,375,768]{2,0,1:T(8,128)(2,1)} %param.19), kind=kOutput, calls=%fused_computation.68 | convolution fusion | flops 14174208000 | bytes 38046720 | tf_op jit(solution)/shard_map/tfd,de->tfe/dot_general | solution.py:251
  387.7 212.7 %while.14 = (s32[]{:T(128)}, f32[4,512,768]{2,1,0:T(8,128)}, f32[4,512,12]{1,0,2:T(4,128)S(1)}, s32[4,8]{1,0:T(4,128)S(1)}, bf16[32,375,768]{2,1,0:T(8,128)(2,1)...) while((s32[]{:T(128)}, f32[4,512,768]{2,1,0:T(8,128)}, ...), condition=%wide.region_16.17_spmd, body=%wide.region_13.16_spmd.sunk | while | flops 603642880 | bytes 100925760 | solution.py:257
  645.6 110.8 %all-gather.8.cloned.1.call-done = f32[4,2048,768]{2,1,0:T(8,128)} async-done(((f32[1,2048,768]{2,1,0:T(8,128)}), f32[4,2048,768]{2,1,0:T(8,128)}) %all-gather.8.cloned.1.call-update) | async-done | bytes 25165840 | tf_op jit(solution)/shard_map/all_gather | solution.py:27
  769.3 65.6 %while.15 = (s32[]{:T(128)}, f32[2048,768]{0,1:T(8,128)}, f32[2048,12]{0,1:T(8,128)S(1)}, f32[4,2048,12]{1,2,0:T(8,128)S(1)}, f32[4,2048,768]{2,1,0:T(8,128)}, /*index=5*/s32[]{:T(128)}, s32[]{:T(128)}, s32[]{:T(128)}) while((s32[]{:T(128)}, f32[2048,768]{0,1:T(8,128)}, f32[2048,12]{0,1:T(8,128)S(1)}, f32[4,2048,12]{1,2,0:T(8,128)S(1)}, ...), condition=%wide.region_18.19_spmd, body=%wide.region_17.18_spmd.sunk | while | flops 4890629 | bytes 44728456 | solution.py:32
  838.1 19.3 multiply_convert_fusion.2
  913.8 13.3 copy.266
  971.9 12.4 broadcast_in_dim.249
  984.2 12.4 broadcast_in_dim.249.clone
  999.7 535.6 %while.56 = (s32[]{:T(128)}, f32[32,375,768]{2,1,0:T(8,128)}, f32[32,375,768]{2,1,0:T(8,128)}, f32[4,512,768]{2,1,0:T(8,128)}, s32[4,8]{1,0:T(4,128)}, /*index=5...) while((s32[]{:T(128)}, f32[32,375,768]{2,1,0:T(8,128)}, ...), condition=%wide.region_31.32_spmd, body=%wide.region_28.31_spmd.sunk | while | flops 1492993024 | bytes 239423888 | solution.py:312
  1064.9 17.8 scatter_fusion
  1102.0 17.8 scatter_fusion.1
  1198.9 17.8 scatter_fusion
  1235.9 17.6 scatter_fusion.1
  1332.7 16.9 scatter_fusion
  1368.9 17.0 scatter_fusion.1
  1465.0 18.5 scatter_fusion
  1502.8 18.3 scatter_fusion.1
  1535.4 111.6 %all-reduce.1 = bf16[2048,768]{1,0:T(8,128)(2,1)} all-reduce(f32[2048,768]{1,0:T(8,128)} %bitcast.334), channel_id=1, replica_groups=mesh['dp'=8,'frame'=4] {'frame'}, use_global_device_ids=true, to_apply=%region_32.33 | all-reduce | flops 1572864 | bytes 9437184 | tf_op jit(solution)/shard_map/psum | solution.py:318
  1700.2 34.6 %bitcast_dynamic-update-slice_fusion.1 = f32[8,768,768]{2,1,0:T(8,128)} fusion(f32[8,768,768]{2,1,0:T(8,128)} %bitcast_dynamic-update-slice_fusion.3, bf16[32,375,768]{2,0,1:T(8,128)(2,1)} %param.19, f32[32,375,768]{2,1,0:T(8,128)} %get-tuple-element.308), kind=kOutput, calls=%fused_computation.125 | convolution fusion | flops 14164992000 | bytes 57753600 | tf_op jit(solution)/shard_map/tfd,tfe->de/dot_general | solution.py:326
  1734.8 34.5 %bitcast_dynamic-update-slice_fusion = f32[8,768,768]{2,1,0:T(8,128)} fusion(f32[8,768,768]{2,1,0:T(8,128)} %bitcast_dynamic-update-slice_fusion.1, bf16[32,375,768]{2,0,1:T(8,128)(2,1)} %param.19, f32[32,375,768]{2,1,0:T(8,128)} %get-tuple-element.309), kind=kOutput, calls=%fused_computation.124 | convolution fusion | flops 14164992000 | bytes 57753600 | tf_op jit(solution)/shard_map/tfd,tfe->de/dot_general | solution.py:327
  1772.9 19.1 copy.264
  1792.1 19.6 concatenate.13
  1811.7 26.4 %maximum_bitcast_fusion = f32[4,96,128,192]{2,1,3,0:T(8,128)} fusion(f32[24,128,4,192]{1,0,3,2:T(8,128)} %bitcast.332, f32[24,128,4,192]{1,0,3,2:T(8,128)} %concatenate.14, f32[48,128,4,192]{1,0,3,2:T(8,128)} %concatenate.13), kind=kLoop, calls=%fused_computation.65 | loop fusion | flops 18874368 | bytes 75497472 | tf_op jit(solution)/shard_map/transpose | solution.py:429
  1838.1 35.8 %copy.268 = f32[4,96,128,192]{2,3,1,0:T(8,128)} copy(f32[4,96,128,192]{2,1,3,0:T(8,128)} %maximum_bitcast_fusion) | data formatting | bytes 75497472 | tf_op jit(solution)/shard_map/transpose | solution.py:429
  1873.9 35.7 %gather_fusion.5 = f32[512,128,192]{1,2,0:T(8,128)} fusion(f32[384,128,192]{1,2,0:T(8,128)} %bitcast.325, s32[1024]{0:T(1024)S(1)} %copy-done.88), kind=kCustom, calls=%fused_computation.5 | custom fusion | bytes 100665344 | tf_op jit(solution)/shard_map/gather | solution.py:436
  1918.9 20.1 convert_reduce_fusion
  1939.1 45.2 %psum.15 = f32[19,768]{1,0:T(8,128)S(1)} all-reduce(f32[19,768]{1,0:T(8,128)S(1)} %concatenate.17), channel_id=1, replica_groups=mesh['dp'=8,'frame'=4] {'dp','frame'}, use_global_device_ids=true, to_apply=%region_57.58 | all-reduce | flops 14592 | bytes 116736 | tf_op jit(solution)/shard_map/psum | solution.py:437
  1988.8 357.1 %reduce-scatter.2.cloned.1.call-done = f32[16,128,192]{1,2,0:T(8,128)} async-done(((f32[512,128,192]{1,2,0:T(8,128)}), f32[16,128,192]{1,2,0:T(8,128)}) %reduce-scatter.2.cloned.1.call-update) | async-done | bytes 1572880 | tf_op jit(solution)/shard_map/reduce_scatter | solution.py:436
  (584 shorter events, 987.0 us)
Async XLA Ops:
  7.2 161.6 %all-gather.12.cloned.1.call-start = ((), (), s32[]{:S(2)}) async-start(), calls=%async_computation.5 | async-start | bytes 25952256 | tf_op jit(solution)/shard_map/all_gather | solution.py:183
  9.8 356.5 %all-gather.6.cloned.1.call-start = ((), (), s32[]{:S(2)}) async-start(), calls=%async_computation.1 | async-start | bytes 3932160 | tf_op jit(solution)/shard_map/all_gather | solution.py:246
  12.2 179.7 %copy-start.92 = (pred[512]{0:T(512)(128)(4,1)}, pred[512]{0:T(512)(128)(4,1)S(1)}, u32[]{:S(2)}) copy-start(pred[512]{0:T(512)(128)(4,1)S(1)} %get-tuple-element.438) | copy-start | bytes 1540
  12.9 216.5 %copy-start.58 = (f32[768]{0:T(1024)}, f32[768]{0:T(1024)S(1)}, u32[]{:S(2)}) copy-start(f32[768]{0:T(1024)S(1)} %get-tuple-element.436) | copy-start | bytes 9220
  12.9 216.5 %copy-start.100 = (f32[768]{0:T(1024)}, f32[768]{0:T(1024)S(1)}, u32[]{:S(2)}) copy-start(f32[768]{0:T(1024)S(1)} %get-tuple-element.435) | copy-start | bytes 9220
  12.9 238.5 %copy-start.84 = (f32[768]{0:T(1024)}, f32[768]{0:T(1024)S(1)}, u32[]{:S(2)}) copy-start(f32[768]{0:T(1024)S(1)} %get-tuple-element.430) | copy-start | bytes 9220
  12.9 238.5 %copy-start.98 = (f32[768]{0:T(1024)}, f32[768]{0:T(1024)S(1)}, u32[]{:S(2)}) copy-start(f32[768]{0:T(1024)S(1)} %get-tuple-element.429) | copy-start | bytes 9220
  13.1 216.3 %copy-start.61 = (f32[512]{0:T(512)}, f32[512]{0:T(512)S(1)}, u32[]{:S(2)}) copy-start(f32[512]{0:T(512)S(1)} %broadcast_multiply_fusion.4) | copy-start | bytes 6148
  13.5 178.4 %copy-start.73 = (f32[512]{0:T(512)}, f32[512]{0:T(512)S(1)}, u32[]{:S(2)}) copy-start(f32[512]{0:T(512)S(1)} %fusion.72) | copy-start | bytes 6148
  13.5 215.9 %copy-start.66 = (f32[512]{0:T(512)}, f32[512]{0:T(512)S(1)}, u32[]{:S(2)}) copy-start(f32[512]{0:T(512)S(1)} %fusion.97) | copy-start | bytes 6148
  13.8 229.3 %copy-start.14 = (pred[512,512]{0,1:T(8,128)(4,1)}, pred[512,512]{0,1:T(8,128)(4,1)S(1)}, u32[]{:S(2)}) copy-start(pred[512,512]{0,1:T(8,128)(4,1)S(1)} %fusion.83) | copy-start | bytes 786436
  222.8 20.4 copy-start.26
  253.3 503.1 %all-gather.8.cloned.1.call-start = ((), (), s32[]{:S(2)}) async-start(), calls=%async_computation.2 | async-start | bytes 31457280 | tf_op jit(solution)/shard_map/all_gather | solution.py:27
  253.9 55.6 %copy-start.23 = (bf16[6,128,768]{1,2,0:T(8,128)(2,1)S(1)}, bf16[6,128,768]{1,2,0:T(8,128)(2,1)}, u32[]{:S(2)}) copy-start(bf16[6,128,768]{1,2,0:T(8,128)(2,1)} %get-tuple-element.524) | copy-start | bytes 3538948
  601.0 338.4 %all-gather.10.cloned.1.call-start = ((), (), s32[]{:S(2)}) async-start(), calls=%async_computation.3 | async-start | bytes 3932160 | tf_op jit(solution)/shard_map/all_gather | solution.py:301
  769.3 65.6 %copy-start.17 = (f32[512,768]{1,0:T(8,128)S(1)}, f32[512,768]{1,0:T(8,128)}, u32[]{:S(2)}) copy-start(f32[512,768]{1,0:T(8,128)} %copy-done.16) | copy-start | bytes 4718596
  769.3 65.6 %copy-start.104 = (f32[768]{0:T(1024)S(1)}, f32[768]{0:T(1024)}, u32[]{:S(2)}) copy-start(f32[768]{0:T(1024)} %get-tuple-element.427) | copy-start | bytes 9220
  834.9 22.5 slice-start.7
  838.1 19.3 slice-start.8
  889.6 1456.3 %reduce-scatter.2.cloned.1.call-start = ((), (), s32[]{:S(2)}) async-start(), calls=%async_computation.4 | async-start | bytes 51904512 | tf_op jit(solution)/shard_map/reduce_scatter | solution.py:436
  1535.3 113.6 %copy-start.18 = (f32[512,768]{1,0:T(8,128)S(1)}, f32[512,768]{1,0:T(8,128)}, u32[]{:S(2)}) copy-start(f32[512,768]{1,0:T(8,128)} %copy-done.16) | copy-start | bytes 4718596
  1535.3 113.6 %copy-start.38 = (bf16[6,128,768]{2,1,0:T(8,128)(2,1)S(1)}, bf16[6,128,768]{2,1,0:T(8,128)(2,1)}, u32[]{:S(2)}) copy-start(bf16[6,128,768]{2,1,0:T(8,128)(2,1)} %copy.234) | copy-start | bytes 3538948
  1535.3 113.6 %copy-start.70 = (f32[512]{0:T(512)S(1)}, f32[512]{0:T(512)}, u32[]{:S(2)}) copy-start(f32[512]{0:T(512)} %copy-done.69) | copy-start | bytes 6148
  1535.3 113.6 %copy-start.85 = (f32[768]{0:T(1024)S(1)}, f32[768]{0:T(1024)}, u32[]{:S(2)}) copy-start(f32[768]{0:T(1024)} %copy-done.84) | copy-start | bytes 9220
  1535.4 113.6 %copy-start.90 = (f32[512]{0:T(512)S(1)}, f32[512]{0:T(512)}, u32[]{:S(2)}) copy-start(f32[512]{0:T(512)} %copy-done.89) | copy-start | bytes 6148
  1838.1 35.8 %copy-start.88 = (s32[1024]{0:T(1024)S(1)}, s32[1024]{0:T(1024)}, u32[]{:S(2)}) copy-start(s32[1024]{0:T(1024)} %get-tuple-element.550) | copy-start | bytes 12292
  1918.9 65.5 %copy-start.53 = (f32[19,768]{1,0:T(8,128)S(1)}, f32[19,768]{1,0:T(8,128)}, u32[]{:S(2)}) copy-start(f32[19,768]{1,0:T(8,128)} %param.27) | copy-start | bytes 175108
  1918.9 65.5 %copy-start.56 = (f32[19,768]{1,0:T(8,128)S(1)}, f32[19,768]{1,0:T(8,128)}, u32[]{:S(2)}) copy-start(f32[19,768]{1,0:T(8,128)} %param.29) | copy-start | bytes 175108
  1918.9 65.5 %copy-start.57 = (f32[19,768]{1,0:T(8,128)S(1)}, f32[19,768]{1,0:T(8,128)}, u32[]{:S(2)}) copy-start(f32[19,768]{1,0:T(8,128)} %param.28) | copy-start | bytes 175108
  1918.9 66.2 %copy-start.72 = (f32[512]{0:T(512)S(1)}, f32[512]{0:T(512)}, u32[]{:S(2)}) copy-start(f32[512]{0:T(512)} %copy-done.71) | copy-start | bytes 6148
  1988.8 362.5 %copy-start.19 = (f32[16,128,192]{1,2,0:T(8,128)S(1)}, f32[16,128,192]{1,2,0:T(8,128)}, u32[]{:S(2)}) copy-start(f32[16,128,192]{1,2,0:T(8,128)} %param.25) | copy-start | bytes 4718596
  1988.8 362.5 %copy-start.20 = (f32[16,128,192]{1,2,0:T(8,128)S(1)}, f32[16,128,192]{1,2,0:T(8,128)}, u32[]{:S(2)}) copy-start(f32[16,128,192]{1,2,0:T(8,128)} %param.26) | copy-start | bytes 4718596
  (102 other events, 467.9 us)
Sparse Core Ops, SparseCore 0:
  11.5 157.3 all-gather.11
  253.4 26.6 all-gather.5
  600.6 155.7 all-gather.7
  889.7 28.5 all-gather.9
  1909.7 436.1 reduce-scatter.1
where the time goes:
time: 2380 us; the launch traced here: 2360 us
  local copies, waits for them, and re-layouts  797 us (33%)
  waiting for transfers between devices  623 us (26%)
  matrix products  483 us (20%)
  other arithmetic  273 us (11%)
  blocking collectives  167 us (7%)
    reduce_scatter x1, waiting for transfers between devices, body(): lax.psum_scatter(by_quarter[picks], ('dp', 'frame'), scatter_dimension=0,...  357 us
    all_gather x1, waiting for transfers between devices, body(): lax.all_gather(master.astype(jnp.bfloat16)[None], ('dp', 'frame'), axis=0...  155 us
    gather x16, local copies, waits for them, and re-layouts, cross_tables(): key_table[owners].reshape(unit_total, frame_total, head_total, head_width)  127 us
    gather x16, local copies, waits for them, and re-layouts, cross_tables(): value_table[owners].reshape(unit_total, frame_total, head_total, head_width)  127 us
    psum x1, blocking collectives, body(): query_summed = lax.psum(query_parts, 'frame')  112 us
    all_gather x1, waiting for transfers between devices, joined(): gathered = jax.tree.map(lambda a: lax.all_gather(a, axis), part)  111 us
    dynamic_update_slice x28, local copies, waits for them, and re-layouts, body(): lax.map(lambda packed: cross_forward(packed[0], packed[1], key_table, val...  73.9 us
    scatter-add x4, other arithmetic, cross_backward(): key_sum = key_sum.at[owners].add(grad_key)  71 us
  transfers between devices with their start and end apart: 5, of which 3 were waited for; matrix products, arithmetic and copies ran while one was open for 10% of the time, Pallas kernels for 0%

commit v1 on v0

v1 whole, which is shorter than its diff:
```python
import functools
import math

import jax
import jax.numpy as jnp
from jax import lax
from jax.experimental import pallas as pl
from jax.experimental.pallas import tpu as pltpu
from jax.sharding import PartitionSpec as P

D = 768
HEADS = 12
HEAD = 64
FF = 3072
BLOCK = 64
PANEL = 128
STEP = 4
WIDE = 256
GROUPS = D // WIDE
ROWS = 6
MATS = 16
PARTIAL = 544
PACKED = 560

EPS_NORM = 1e-05
EPS_ADAM = 1e-08
BETA_ONE = 0.5
BETA_TWO = 0.5
RATE_MATRIX = 0.04
RATE_VECTOR = 0.2
DECAY_MATRIX = 0.01
MASKED = -1e30
SCALE = HEAD**-0.5

BF = jnp.bfloat16
F32 = jnp.float32
VMEM_LIMIT = 60 * 1024 * 1024


def dot_nt(a, b):
    return lax.dot_general(a, b, (((1,), (1,)), ((), ())), preferred_element_type=F32)


def dot_nn(a, b):
    return lax.dot_general(a, b, (((1,), (0,)), ((), ())), preferred_element_type=F32)


def eye():
    return (
        lax.broadcasted_iota(jnp.int32, (WIDE, WIDE), 0)
        == lax.broadcasted_iota(jnp.int32, (WIDE, WIDE), 1)
    ).astype(BF)


def turned(x, unit):
    parts = [
        dot_nt(unit, x[:, s : s + WIDE]).astype(BF) for s in range(0, x.shape[1], WIDE)
    ]
    return parts[0] if len(parts) == 1 else jnp.concatenate(parts, axis=0)


def head_mask():
    return (
        lax.broadcasted_iota(jnp.int32, (WIDE, WIDE), 0) >> 6
        == lax.broadcasted_iota(jnp.int32, (WIDE, WIDE), 1) >> 6
    )


def row_pick():
    return (
        lax.broadcasted_iota(jnp.int32, (HEAD, WIDE), 0)
        == lax.broadcasted_iota(jnp.int32, (HEAD, WIDE), 1) & (HEAD - 1)
    ).astype(BF)


def thirds(x):
    high = x.astype(BF)
    rest = x - high.astype(F32)
    middle = rest.astype(BF)
    return high, middle, (rest - middle.astype(F32)).astype(BF)


def norm_parts(v):
    average = jnp.mean(v, axis=-1, keepdims=True)
    centred = v - average
    inverse = lax.rsqrt(jnp.mean(centred * centred, axis=-1, keepdims=True) + EPS_NORM)
    return centred * inverse, inverse


def norm_back(e, unit_rows, inverse, gain):
    f = e * gain
    lean = jnp.mean(f, axis=-1, keepdims=True)
    slant = jnp.mean(f * unit_rows, axis=-1, keepdims=True)
    return (f - lean - unit_rows * slant) * inverse


def column_sum(x):
    return jnp.sum(x, axis=0, keepdims=True)


def matrix_copies(tiles, where, matrix, target, sem):
    copies = []
    for r in range(ROWS):
        for f in range(4):
            copies.append(
                pltpu.make_async_copy(
                    tiles.at[where[(matrix * ROWS + r) * 4 + f]],
                    target.at[pl.ds(f * 192, 192), pl.ds(r * PANEL, PANEL)],
                    sem,
                )
            )
    return copies


def gradient_copies(staged, keep, send, slot, me, sem):
    copies = []
    for relative in range(4):
        f = relative ^ me
        target = send if relative & 1 else keep
        for r in range(ROWS):
            copies.append(
                pltpu.make_async_copy(
                    staged.at[pl.ds(pl.multiple_of(f * 192, 64), 192), pl.ds(r * PANEL, PANEL)],
                    target.at[relative >> 1, slot * ROWS + r],
                    sem,
                )
            )
    return copies


def start_all(copies):
    for copy in copies:
        copy.start()


def wait_all(copies):
    for copy in copies:
        copy.wait()


def front_kernel(
    where, tokens, vectors, member_column, live_column, member_row, tiles,
    sum_one, cross_query, query, key, value, attended, lse,
    weights, bias, sems,
):
    loads = [
        matrix_copies(tiles, where, i, weights.at[i], sems.at[i]) for i in range(5)
    ]
    for load in loads:
        start_all(load)
    unit = eye()
    count = tokens.shape[0]
    key_ids = lax.broadcasted_iota(jnp.int32, (count, count), 0)
    row_ids = lax.broadcasted_iota(jnp.int32, (count, count), 1)
    seen = (
        (member_column[...] == member_row[...])
        & (key_ids <= row_ids)
        & ((live_column[...] > 0) | (key_ids == row_ids))
    )
    bias[...] = jnp.where(seen, 0.0, MASKED)
    x = tokens[...].astype(F32)
    a = (norm_parts(x)[0] * vectors[0:1] + vectors[1:2]).astype(BF)
    wait_all(loads[0])
    query[...] = (SCALE * (dot_nt(a, weights[0]) + vectors[2:3])).astype(BF)
    wait_all(loads[1])
    key[...] = dot_nt(a, weights[1]).astype(BF)
    wait_all(loads[2])
    value[...] = (dot_nt(a, weights[2]) + vectors[3:4]).astype(BF)
    lanes = lax.broadcasted_iota(jnp.int32, (1, WIDE), 1) >> 6
    lse[...] = jnp.zeros_like(lse)
    for g in range(GROUPS):
        cols = pl.ds(g * WIDE, WIDE)
        q, k = query[:, cols], key[:, cols]
        v_turned = turned(value[:, cols], unit)
        outs = []
        for h in range(4):
            masked_q = jnp.where(lanes == h, q, jnp.zeros_like(q))
            scores = dot_nt(k, masked_q) + bias[...]
            top = jnp.max(scores, axis=0, keepdims=True)
            p = jnp.exp(scores - top)
            total = jnp.sum(p, axis=0, keepdims=True)
            out = dot_nn(v_turned[h * HEAD : (h + 1) * HEAD], p.astype(BF))
            outs.append((out * (1.0 / total)).astype(BF))
            lse[g * 4 + h : g * 4 + h + 1] = top + jnp.log(total)
        attended[:, cols] = turned(jnp.concatenate(outs, axis=0), unit)
    wait_all(loads[3])
    h1 = x + (dot_nt(attended[...], weights[3]) + vectors[4:5])
    sum_one[...] = h1
    c = (norm_parts(h1)[0] * vectors[5:6] + vectors[6:7]).astype(BF)
    wait_all(loads[4])
    cross_query[...] = (SCALE * (dot_nt(c, weights[4]) + vectors[7:8])).astype(BF)


def tables_kernel(act, where, frames, vectors, tiles, key_table, value_table, weights, sems):
    step = pl.program_id(0)

    @pl.when(step == 0)
    def _():
        loads = [
            matrix_copies(tiles, where, 5 + i, weights.at[i], sems.at[i]) for i in range(2)
        ]
        for load in loads:
            start_all(load)
        for load in loads:
            wait_all(load)

    @pl.when(step < act[0])
    def _():
        f = frames[0]
        key_table[0] = dot_nt(f, weights[0]).astype(BF)
        value_table[0] = (dot_nt(f, weights[1]) + vectors[8:9]).astype(BF)


def pad_rows(scores, fill):
    half = scores.shape[0] // 2
    odd = lax.broadcasted_iota(jnp.int32, (16, 1), 0) + (half - 16) >= 375
    parts = []
    for s in (0, half):
        parts.append(scores[s : s + half - 16])
        parts.append(jnp.where(odd, fill, scores[s + half - 16 : s + half]))
    return jnp.concatenate(parts, axis=0)


def each_unit(info, body):
    step = pl.program_id(0)
    first, mine = info[10 + step], info[18 + step]
    rest = jnp.where(step == 0, 8 - info[1], 0)

    def one(j, state):
        body(jnp.where(j < mine, first + j, info[1] + j - mine))
        return state

    lax.fori_loop(0, mine + rest, one, 0)


def spread_heads(x, mask):
    return jnp.where(mask, jnp.concatenate([x] * 4, axis=0), jnp.zeros((), x.dtype))


def cross_forward_kernel(info, query, key_table, value_table, out, value_turned, lse):
    step = pl.program_id(0)

    @pl.when(step < info[0])
    def _():
        unit, mask, pick = eye(), head_mask(), row_pick()
        for g in range(GROUPS):
            cols = pl.ds(g * WIDE, WIDE)
            value_turned[g] = turned(value_table[0, :, cols], unit)

        def body(u):
            rows = pl.ds(pl.multiple_of(u * BLOCK, BLOCK), BLOCK)
            for g in range(GROUPS):
                cols = pl.ds(g * WIDE, WIDE)
                wide_q = spread_heads(query[rows, cols], mask)
                scores = pad_rows(dot_nt(key_table[0, :, cols], wide_q), MASKED)
                top = jnp.max(scores, axis=0, keepdims=True)
                p = jnp.exp(scores - top)
                total = jnp.sum(p, axis=0, keepdims=True)
                o = dot_nn(value_turned[g], p.astype(BF)) * (1.0 / total)
                o = jnp.where(mask, o, 0.0).astype(BF)
                out[rows, cols] = dot_nt(pick, o).astype(BF)
                lse[pl.ds(u, 1), cols] = top + jnp.log(total)

        each_unit(info, body)

    @pl.when(step == pl.num_programs(0) - 1)
    def _():
        parts = [t.astype(F32) for t in thirds(lse[...])]
        parts.append(jnp.zeros_like(parts[0]))
        out[512:PARTIAL] = jnp.concatenate(parts, axis=0).astype(BF)


def cross_backward_kernel(
    info, query, packed, key_table, value_table, frames, grad_key_in, grad_value_in, bias_in,
    grad_query, grad_key, grad_value, bias_grad,
    key_turned, key_sum, value_sum, lse, delta,
):
    step = pl.program_id(0)

    @pl.when(step == 0)
    def _():
        grad_key[...] = grad_key_in[...]
        grad_value[...] = grad_value_in[...]
        bias_grad[...] = bias_in[...]
        extra = packed[512:PACKED].astype(F32)
        lse[...] = extra[0:8] + extra[8:16] + extra[16:24]
        delta[...] = extra[24:32] + extra[32:40] + extra[40:48]

    @pl.when(step < info[0])
    def _():
        unit, mask, pick = eye(), head_mask(), row_pick()
        for g in range(GROUPS):
            cols = pl.ds(g * WIDE, WIDE)
            key_turned[g] = turned(key_table[0, :, cols], unit)
        key_sum[...] = jnp.zeros_like(key_sum)
        value_sum[...] = jnp.zeros_like(value_sum)

        def body(u):
            rows = pl.ds(pl.multiple_of(u * BLOCK, BLOCK), BLOCK)
            for g in range(GROUPS):
                cols = pl.ds(g * WIDE, WIDE)
                wide_q = spread_heads(query[rows, cols], mask)
                wide_o = spread_heads(packed[rows, cols], mask)
                scores = dot_nt(key_table[0, :, cols], wide_q)
                p = pad_rows(jnp.exp(scores - lse[pl.ds(u, 1), cols]), 0.0)
                dp = dot_nt(value_table[0, :, cols], wide_o)
                ds = (p * (dp - delta[pl.ds(u, 1), cols])).astype(BF)
                value_sum[:, cols] += dot_nn(p.astype(BF), wide_o)
                key_sum[:, cols] += dot_nn(ds, wide_q)
                dq = jnp.where(mask, dot_nn(key_turned[g], ds), 0.0).astype(BF)
                grad_query[rows, cols] = dot_nt(pick, dq).astype(BF)

        each_unit(info, body)
        f = frames[0]
        for g in range(GROUPS):
            cols = pl.ds(g * WIDE, WIDE)
            grad_key[cols, :] += dot_nn(turned(key_sum[:, cols].astype(BF), unit), f)
            low = value_sum[:, cols].astype(BF)
            grad_value[cols, :] += dot_nn(turned(low, unit), f)
            bias_grad[0:1, cols] += column_sum(low.astype(F32))


def middle_kernel(
    where, me, sum_one, own, other, vectors, live, cotangent, tiles,
    out_tokens, grad_two, packed, vector_grads, keep, send,
    weights, hidden, act, staged, third, merged, sems, out_sem,
):
    count = sum_one.shape[0]
    loads = {
        m: matrix_copies(tiles, where, m, weights.at[m - 7], sems.at[m - 7]) for m in range(7, 16)
    }
    for load in loads.values():
        start_all(load)
    unit, mask, pick = eye(), head_mask(), row_pick()
    lse_own = own[512:536].astype(F32)
    lse_other = other[512:536].astype(F32)
    lse_own = lse_own[0:8] + lse_own[8:16] + lse_own[16:24]
    lse_other = lse_other[0:8] + lse_other[8:16] + lse_other[16:24]
    top = jnp.maximum(lse_own, lse_other)
    weight_own = jnp.exp(lse_own - top)
    weight_other = jnp.exp(lse_other - top)
    total = weight_own + weight_other
    share = weight_own / total
    lse = top + jnp.log(total)
    for u in range(count // BLOCK):
        rows = pl.ds(u * BLOCK, BLOCK)
        for g in range(GROUPS):
            cols = pl.ds(g * WIDE, WIDE)
            part = share[u : u + 1, g * WIDE : (g + 1) * WIDE]
            high = part.astype(BF)
            low = (part - high.astype(F32)).astype(BF)
            none = jnp.zeros((), BF)
            factor = dot_nt(pick, jnp.where(mask, high, none)) + dot_nt(
                pick, jnp.where(mask, low, none)
            )
            first, second = own[rows, cols].astype(F32), other[rows, cols].astype(F32)
            merged[rows, cols] = second + factor * (first - second)
    cross_out = merged[...].astype(BF)
    wait_all(loads[7])
    h2 = sum_one[...] + (dot_nt(cross_out, weights[0]) + vectors[9:10])
    unit_three, inverse_three = norm_parts(h2)
    m = (unit_three * vectors[10:11] + vectors[11:12]).astype(BF)
    third[...] = h2 + vectors[16:17]
    for c in range(4):
        wait_all(loads[8 + c])
        wait_all(loads[12 + c])

    def ahead(c, state):
        u = dot_nt(m, weights[1 + c]) + vectors[pl.ds(12 + c, 1)]
        hidden[c] = u
        g = (u * (0.5 * (1.0 + lax.erf(u * math.sqrt(0.5))))).astype(BF)
        act[c] = g
        third[...] += dot_nt(g, weights[5 + c])
        return state

    lax.fori_loop(0, 4, ahead, 0)
    unit_last, inverse_last = norm_parts(third[...])
    alive = live[...]
    out_tokens[...] = (unit_last * vectors[17:18] + vectors[18:19]) * alive
    e = cotangent[...].astype(F32) * alive
    vector_grads[...] = jnp.zeros_like(vector_grads)
    vector_grads[8:9] = column_sum(e * unit_last)
    vector_grads[9:10] = column_sum(e)
    dh3 = norm_back(e, unit_last, inverse_last, vectors[17:18])
    third[...] = dh3
    e3 = dh3.astype(BF)
    vector_grads[7:8] = column_sum(e3.astype(F32))
    e3_turned = turned(e3, unit)
    grad_two[...] = jnp.zeros_like(grad_two)

    def back(c, state):
        staged[5 + c] = dot_nn(e3_turned, act[c]).astype(BF)
        start_all(gradient_copies(staged.at[5 + c], keep, send, 5 + c, me[0], out_sem))
        u = hidden[c]
        slope = 0.5 * (1.0 + lax.erf(u * math.sqrt(0.5))) + u * (
            jnp.exp(-0.5 * u * u) * (1.0 / math.sqrt(2.0 * math.pi))
        )
        du = (dot_nn(e3, weights[5 + c]) * slope).astype(BF)
        vector_grads[pl.ds(3 + c, 1)] = column_sum(du.astype(F32))
        staged[1 + c] = dot_nn(turned(du, unit), m).astype(BF)
        start_all(gradient_copies(staged.at[1 + c], keep, send, 1 + c, me[0], out_sem))
        grad_two[...] += dot_nn(du, weights[1 + c])
        return state

    lax.fori_loop(0, 4, back, 0)
    dm = grad_two[...]
    vector_grads[1:2] = column_sum(dm * unit_three)
    vector_grads[2:3] = column_sum(dm)
    dh2 = third[...] + norm_back(dm, unit_three, inverse_three, vectors[10:11])
    grad_two[...] = dh2
    e2 = dh2.astype(BF)
    vector_grads[0:1] = column_sum(e2.astype(F32))
    staged[0] = dot_nn(turned(e2, unit), cross_out).astype(BF)
    start_all(gradient_copies(staged.at[0], keep, send, 0, me[0], out_sem))
    packed[0:512] = dot_nn(e2, weights[0]).astype(BF)
    ones = jnp.ones((8, WIDE), BF)
    deltas = []
    for u in range(count // BLOCK):
        rows = pl.ds(u * BLOCK, BLOCK)
        line = []
        for g in range(GROUPS):
            cols = pl.ds(g * WIDE, WIDE)
            product = packed[rows, cols].astype(F32) * merged[rows, cols]
            high, middle, low = (spread_heads(t, mask) for t in thirds(product))
            line.append((dot_nt(ones, high) + dot_nt(ones, middle) + dot_nt(ones, low))[0:1])
        deltas.append(jnp.concatenate(line, axis=1))
    delta = jnp.concatenate(deltas, axis=0)
    extra = [t.astype(F32) for t in thirds(lse)] + [t.astype(F32) for t in thirds(delta)]
    packed[512:PACKED] = jnp.concatenate(extra, axis=0).astype(BF)
    for i in range(9):
        wait_all(gradient_copies(staged.at[i], keep, send, i, me[0], out_sem))


def last_kernel(
    where, me, tokens, sum_one, grad_two, query, key, value, attended, lse, own, other, vectors,
    member_column, live_column, member_row, tiles,
    token_grads, vector_grads, keep, send,
    weights, staged, bias, grad_att, grad_q, grad_q_turned, grad_k, grad_v, sems, out_sem,
):
    order = (4, 3, 0, 1, 2)
    loads = [
        matrix_copies(tiles, where, m, weights.at[i], sems.at[i]) for i, m in enumerate(order)
    ]
    for load in loads:
        start_all(load)
    unit = eye()
    count = tokens.shape[0]
    key_ids = lax.broadcasted_iota(jnp.int32, (count, count), 0)
    row_ids = lax.broadcasted_iota(jnp.int32, (count, count), 1)
    seen = (
        (member_column[...] == member_row[...])
        & (key_ids <= row_ids)
        & ((live_column[...] > 0) | (key_ids == row_ids))
    )
    bias[...] = jnp.where(seen, 0.0, MASKED)

    def put(slot, value_):
        staged[slot] = value_.astype(BF)
        start_all(gradient_copies(staged.at[slot], keep, send, slot, me[0], out_sem))

    ecq = (own[...].astype(F32) + other[...].astype(F32)).astype(BF) * jnp.asarray(SCALE, BF)
    vector_grads[...] = jnp.zeros_like(vector_grads)
    vector_grads[7:8] = column_sum(ecq.astype(F32))
    unit_two, inverse_two = norm_parts(sum_one[...])
    c = (unit_two * vectors[5:6] + vectors[6:7]).astype(BF)
    put(0, dot_nn(turned(ecq, unit), c))
    wait_all(loads[0])
    dc = dot_nn(ecq, weights[0])
    vector_grads[5:6] = column_sum(dc * unit_two)
    vector_grads[6:7] = column_sum(dc)
    dh1 = grad_two[...] + norm_back(dc, unit_two, inverse_two, vectors[5:6])
    token_grads[...] = dh1
    e1 = dh1.astype(BF)
    vector_grads[4:5] = column_sum(e1.astype(F32))
    put(1, dot_nn(turned(e1, unit), attended[...]))
    wait_all(loads[1])
    grad_att[...] = dot_nn(e1, weights[1]).astype(BF)
    lanes = lax.broadcasted_iota(jnp.int32, (1, WIDE), 1) >> 6
    for g in range(GROUPS):
        cols = pl.ds(g * WIDE, WIDE)
        q, k, v, do = query[:, cols], key[:, cols], value[:, cols], grad_att[:, cols]
        k_turned = turned(k, unit)
        dk = jnp.zeros((count, WIDE), F32)
        dv = jnp.zeros((count, WIDE), F32)
        for h in range(4):
            none = jnp.zeros_like(q)
            masked_q = jnp.where(lanes == h, q, none)
            masked_o = jnp.where(lanes == h, do, none)
            scores = dot_nt(k, masked_q) + bias[...]
            p = jnp.exp(scores - lse[g * 4 + h : g * 4 + h + 1])
            dp = dot_nt(v, masked_o)
            drift = jnp.sum(p * dp, axis=0, keepdims=True)
            ds = (p * (dp - drift)).astype(BF)
            dv = dv + dot_nn(p.astype(BF), masked_o)
            dk = dk + dot_nn(ds, masked_q)
            dq = dot_nn(k_turned[h * HEAD : (h + 1) * HEAD], ds).astype(BF)
            spot = g * WIDE + h * HEAD
            grad_q_turned[spot : spot + HEAD] = dq * jnp.asarray(SCALE, BF)
        grad_k[:, cols] = dk.astype(BF)
        grad_v[:, cols] = dv.astype(BF)
        grad_q[:, cols] = turned(grad_q_turned[cols, :], unit)
    x = tokens[...].astype(F32)
    unit_one, inverse_one = norm_parts(x)
    a = (unit_one * vectors[0:1] + vectors[1:2]).astype(BF)
    vector_grads[2:3] = column_sum(grad_q[...].astype(F32))
    vector_grads[3:4] = column_sum(grad_v[...].astype(F32))
    put(2, dot_nn(grad_q_turned[...], a))
    put(3, dot_nn(turned(grad_k[...], unit), a))
    put(4, dot_nn(turned(grad_v[...], unit), a))
    wait_all(loads[2])
    wait_all(loads[3])
    wait_all(loads[4])
    da = (
        dot_nn(grad_q[...], weights[2])
        + dot_nn(grad_k[...], weights[3])
        + dot_nn(grad_v[...], weights[4])
    )
    vector_grads[0:1] = column_sum(da * unit_one)
    vector_grads[1:2] = column_sum(da)
    token_grads[...] += norm_back(da, unit_one, inverse_one, vectors[0:1])
    for i in range(5):
        wait_all(gradient_copies(staged.at[i], keep, send, i, me[0], out_sem))


SMEM = pl.BlockSpec(memory_space=pltpu.SMEM)
WHOLE = pl.BlockSpec(memory_space=pltpu.VMEM)
AWAY = pl.BlockSpec(memory_space=pl.ANY)
PARAMS = pltpu.CompilerParams(vmem_limit_bytes=VMEM_LIMIT)


def shape(*dims, dtype=BF):
    return jax.ShapeDtypeStruct(dims, dtype)


def call_front(where, tokens, vectors, layout, tiles):
    count = tokens.shape[0]
    return pl.pallas_call(
        front_kernel,
        out_shape=(
            shape(count, D, dtype=F32),
            *(shape(count, D) for _ in range(5)),
            shape(16, count, dtype=F32),
        ),
        in_specs=[SMEM, WHOLE, WHOLE, WHOLE, WHOLE, WHOLE, AWAY],
        out_specs=(WHOLE,) * 7,
        scratch_shapes=[
            pltpu.VMEM((5, D, D), BF),
            pltpu.VMEM((count, count), F32),
            pltpu.SemaphoreType.DMA((5,)),
        ],
        compiler_params=PARAMS,
        name="front",
    )(where, tokens, vectors, *layout, tiles)


def call_tables(act, where, frames, vectors, tiles):
    slots, extent, _ = frames.shape

    def place(i, act, where):
        return (act[1 + i], 0, 0)

    block = pl.BlockSpec((1, extent, D), place)
    return pl.pallas_call(
        tables_kernel,
        out_shape=(shape(slots, extent, D),) * 2,
        grid_spec=pltpu.PrefetchScalarGridSpec(
            num_scalar_prefetch=2,
            grid=(slots,),
            in_specs=[block, WHOLE, AWAY],
            out_specs=(block, block),
            scratch_shapes=[pltpu.VMEM((2, D, D), BF), pltpu.SemaphoreType.DMA((2,))],
        ),
        compiler_params=PARAMS,
        name="tables",
    )(act, where, frames, vectors, tiles)


def whole_spec(*dims):
    return pl.BlockSpec(dims, lambda i, info: (0,) * len(dims))


def call_cross_forward(info, query, key_table, value_table, base):
    count, extent = query.shape[0], key_table.shape[1]
    slots = 8
    block = pl.BlockSpec((1, extent, D), lambda i, info: (base + info[2 + i], 0, 0))
    return pl.pallas_call(
        cross_forward_kernel,
        out_shape=shape(PARTIAL, D),
        grid_spec=pltpu.PrefetchScalarGridSpec(
            num_scalar_prefetch=1,
            grid=(slots,),
            in_specs=[whole_spec(count, D), block, block],
            out_specs=whole_spec(PARTIAL, D),
            scratch_shapes=[
                pltpu.VMEM((GROUPS, WIDE, extent), BF),
                pltpu.VMEM((8, D), F32),
            ],
        ),
        compiler_params=PARAMS,
        name="cross_forward",
    )(info, query, key_table, value_table)


def call_cross_backward(info, query, packed, key_table, value_table, frames, sums, base):
    count, extent = query.shape[0], key_table.shape[1]
    slots = 8
    block = pl.BlockSpec((1, extent, D), lambda i, info: (base + info[2 + i], 0, 0))
    return pl.pallas_call(
        cross_backward_kernel,
        out_shape=(
            shape(count, D),
            shape(D, D, dtype=F32),
            shape(D, D, dtype=F32),
            shape(8, D, dtype=F32),
        ),
        grid_spec=pltpu.PrefetchScalarGridSpec(
            num_scalar_prefetch=1,
            grid=(slots,),
            in_specs=[
                whole_spec(count, D),
                whole_spec(PACKED, D),
                block,
                block,
                block,
                whole_spec(D, D),
                whole_spec(D, D),
                whole_spec(8, D),
            ],
            out_specs=(
                whole_spec(count, D),
                whole_spec(D, D),
                whole_spec(D, D),
                whole_spec(8, D),
            ),
            scratch_shapes=[
                pltpu.VMEM((GROUPS, WIDE, extent), BF),
                pltpu.VMEM((extent, D), F32),
                pltpu.VMEM((extent, D), F32),
                pltpu.VMEM((8, D), F32),
                pltpu.VMEM((8, D), F32),
            ],
        ),
        compiler_params=PARAMS,
        name="cross_backward",
    )(info, query, packed, key_table, value_table, frames, *sums)


def call_middle(where, me, sum_one, own, other, vectors, live, cotangent, tiles):
    count = sum_one.shape[0]
    part = shape(2, 9 * ROWS, 192, PANEL)
    return pl.pallas_call(
        middle_kernel,
        out_shape=(
            shape(count, D, dtype=F32),
            shape(count, D, dtype=F32),
            shape(PACKED, D),
            shape(16, D, dtype=F32),
            part,
            part,
        ),
        in_specs=[SMEM, SMEM, WHOLE, WHOLE, WHOLE, WHOLE, WHOLE, WHOLE, AWAY],
        out_specs=(WHOLE, WHOLE, WHOLE, WHOLE, AWAY, AWAY),
        scratch_shapes=[
            pltpu.VMEM((9, D, D), BF),
            pltpu.VMEM((4, count, D), F32),
            pltpu.VMEM((4, count, D), BF),
            pltpu.VMEM((9, D, D), BF),
            pltpu.VMEM((count, D), F32),
            pltpu.VMEM((count, D), F32),
            pltpu.SemaphoreType.DMA((9,)),
            pltpu.SemaphoreType.DMA,
        ],
        compiler_params=PARAMS,
        name="middle",
    )(where, me, sum_one, own, other, vectors, live, cotangent, tiles)


def call_last(where, me, tokens, sum_one, grad_two, saved, own, other, vectors, layout, tiles):
    count = tokens.shape[0]
    part = shape(2, 5 * ROWS, 192, PANEL)
    return pl.pallas_call(
        last_kernel,
        out_shape=(shape(count, D, dtype=F32), shape(8, D, dtype=F32), part, part),
        in_specs=[SMEM, SMEM] + [WHOLE] * 14 + [AWAY],
        out_specs=(WHOLE, WHOLE, AWAY, AWAY),
        scratch_shapes=[
            pltpu.VMEM((5, D, D), BF),
            pltpu.VMEM((5, D, D), BF),
            pltpu.VMEM((count, count), F32),
            pltpu.VMEM((count, D), BF),
            pltpu.VMEM((count, D), BF),
            pltpu.VMEM((D, count), BF),
            pltpu.VMEM((count, D), BF),
            pltpu.VMEM((count, D), BF),
            pltpu.SemaphoreType.DMA((5,)),
            pltpu.SemaphoreType.DMA,
        ],
        compiler_params=PARAMS,
        name="last",
    )(where, me, tokens, sum_one, grad_two, *saved, own, other, vectors, *layout, tiles)


def row_layout(bucket, length, row_count):
    starts = jnp.cumsum(bucket, dtype=jnp.int32) - bucket
    row_ids = jnp.arange(row_count, dtype=jnp.int32)
    slot_ids = jnp.arange(bucket.shape[0], dtype=jnp.int32)
    block_ids = row_ids // BLOCK
    inside = (block_ids[:, None] >= starts[None, :]) & (
        block_ids[:, None] < (starts + bucket)[None, :]
    )
    member = jnp.where(
        jnp.any(inside, axis=1),
        jnp.sum(jnp.where(inside, slot_ids[None, :], 0), axis=1, dtype=jnp.int32),
        -1,
    )
    live = jnp.any(
        inside & (row_ids[:, None] - BLOCK * starts[None, :] < length[None, :]), axis=1
    )
    return member, live


def packed_slots(bucket):
    count = bucket.shape[0]
    ids = jnp.arange(count, dtype=jnp.int32)
    taken = bucket > 0
    number = jnp.sum(taken, dtype=jnp.int32)
    rank = jnp.cumsum(taken, dtype=jnp.int32) - 1
    step = jnp.minimum(ids, number - 1)
    hit = (rank[None, :] == step[:, None]) & taken[None, :]

    def pick(values):
        return jnp.sum(jnp.where(hit, values[None, :], 0), axis=1, dtype=jnp.int32)

    starts = jnp.cumsum(bucket, dtype=jnp.int32) - bucket
    return number, pick(ids), pick(starts), pick(bucket)


def adam_update(gradient, first_moment, second_moment, weight, step_rate, decay_rate):
    first_new = BETA_ONE * first_moment + (1.0 - BETA_ONE) * gradient
    second_new = BETA_TWO * second_moment + (1.0 - BETA_TWO) * gradient * gradient
    fix_one = 1.0 - BETA_ONE**STEP
    fix_two = 1.0 - BETA_TWO**STEP
    update = first_new / fix_one / (jnp.sqrt(second_new / fix_two) + EPS_ADAM)
    return (first_new, second_new, weight - step_rate * (update + decay_rate * weight))


def swap(x, bit):
    return lax.ppermute(x, "frame", [(i, i ^ bit) for i in range(4)])


def reduced(keep, send):
    mine = (keep.astype(F32) + swap(send, 1).astype(F32)).astype(BF)
    quarter = (mine[0].astype(F32) + swap(mine[1], 2).astype(F32)).astype(BF)
    return lax.psum(quarter, "dp")


def body(
    tokens, frames, cotangent, buckets, lengths, slot_of, master, first_moment, second_moment,
    vectors, vector_first, vector_second,
):
    row_count = tokens.shape[0]
    group_count = lax.axis_size("dp")
    frame_count = lax.axis_size("frame")
    me = lax.axis_index("frame")
    group_index = lax.axis_index("dp")
    cap = master.shape[0]
    panel_total = slot_of.shape[0]
    slots = buckets.shape[0] // frame_count
    extent = frames.shape[1]

    tiles = lax.all_gather(
        master.astype(BF).transpose(0, 2, 1)[None], ("dp", "frame"), axis=0, tiled=True
    )
    tiles = tiles.reshape(group_count * frame_count * cap, master.shape[2], PANEL)
    quarter_ids = jnp.arange(frame_count, dtype=jnp.int32)
    where = (
        ((slot_of // cap)[:, None] * frame_count + quarter_ids[None, :]) * cap
        + (slot_of % cap)[:, None]
    ).reshape(-1)

    core, far = me & 1, me >> 1
    room = (extent + 15) // 16 * 16
    by_buffer = frames.reshape(2, 2, slots, extent, D)

    def halves(bit):
        part = lax.dynamic_index_in_dim(by_buffer, bit, 1, False)
        first = lax.dynamic_index_in_dim(part, far, 0, False)
        second = lax.dynamic_index_in_dim(part, 1 - far, 0, False)
        return jnp.pad(
            jnp.concatenate([first, second], axis=0), ((0, 0), (0, room - extent), (0, 0))
        )

    all_frames = jnp.concatenate([halves(core), swap(halves(1 - core), 1)], axis=1)

    by_device = buckets.reshape(frame_count, slots)
    own_bucket = lax.dynamic_index_in_dim(by_device, me, 0, False)
    far_bucket = lax.dynamic_index_in_dim(by_device, me ^ 2, 0, False)
    own_length = lax.dynamic_index_in_dim(lengths.reshape(frame_count, slots), me, 0, False)
    infos = []
    for bucket in (own_bucket, far_bucket):
        number, places, starts, units = packed_slots(bucket)
        infos.append(
            jnp.concatenate([jnp.stack([number, jnp.sum(bucket)]), places, starts, units])
        )
    both = packed_slots(jnp.concatenate([own_bucket, far_bucket]))
    act = jnp.concatenate([both[0][None], both[1]])
    member, live = row_layout(own_bucket, own_length, row_count)
    layout = (member[:, None], live.astype(jnp.int32)[:, None], member[None, :])

    key_table, value_table = call_tables(act, where, all_frames, vectors, tiles)
    sum_one, cross_query, *saved = call_front(where, tokens, vectors, layout, tiles)
    far_query = swap(cross_query, 2)
    own_part = call_cross_forward(infos[0], cross_query, key_table, value_table, 0)
    far_part = call_cross_forward(infos[1], far_query, key_table, value_table, slots)
    other_part = swap(far_part, 2)
    place = me[None].astype(jnp.int32)
    out_tokens, grad_two, packed, vectors_mid, keep_mid, send_mid = call_middle(
        where, place, sum_one, own_part, other_part, vectors, live.astype(F32)[:, None],
        cotangent, tiles,
    )
    far_packed = swap(packed, 2)
    zeros = (jnp.zeros((D, D), F32), jnp.zeros((D, D), F32), jnp.zeros((8, D), F32))
    own_grad, *sums = call_cross_backward(
        infos[0], cross_query, packed, key_table, value_table, all_frames, zeros, 0
    )
    far_grad, grad_ck, grad_cv, bias_cv = call_cross_backward(
        infos[1], far_query, far_packed, key_table, value_table, all_frames, sums, slots
    )
    other_grad = swap(far_grad, 2)
    token_grads, vectors_last, keep_last, send_last = call_last(
        where, place, tokens, sum_one, grad_two, saved, own_grad, other_grad, vectors, layout, tiles
    )

    def split(grad):
        parts = (
            grad.astype(BF).reshape(4, 192, ROWS, PANEL).transpose(0, 2, 1, 3)
        )
        pieces = [lax.dynamic_index_in_dim(parts, me ^ i, 0, False) for i in range(4)]
        return jnp.stack([pieces[0], pieces[2]]), jnp.stack([pieces[1], pieces[3]])

    keep_k, send_k = split(grad_ck)
    keep_v, send_v = split(grad_cv)
    early = reduced(keep_mid, send_mid)
    late = reduced(
        jnp.concatenate([keep_k, keep_v, keep_last], axis=1),
        jnp.concatenate([send_k, send_v, send_last], axis=1),
    )
    at = {m: i for i, m in enumerate((7, *range(8, 16), 5, 6, 4, 3, 0, 1, 2))}
    spots = jnp.asarray([at[p // ROWS] * ROWS + p % ROWS for p in range(panel_total)], jnp.int32)
    slot_ids = group_index * cap + jnp.arange(cap, dtype=jnp.int32)
    matches = slot_of[:, None] == slot_ids[None, :]
    spot = jnp.sum(jnp.where(matches, spots[:, None], 0), axis=0, dtype=jnp.int32)
    used = jnp.any(matches, axis=0)[:, None, None]
    owned = jnp.concatenate([early, late], axis=0)[spot].transpose(0, 2, 1)
    grad_vectors = jnp.concatenate(
        [vectors_last[0:8], bias_cv[0:1], vectors_mid[0:10]], axis=0
    )
    vector_total = lax.psum(grad_vectors, ("dp", "frame"))
    grad_scale = 1.0 / math.sqrt(row_count * group_count * frame_count)
    matrix_grads = jnp.where(used, owned.astype(F32) * grad_scale, 0.0)
    matrix_first, matrix_second, matrix_weights = adam_update(
        matrix_grads, first_moment, second_moment, master, RATE_MATRIX, DECAY_MATRIX
    )
    matrix_first = jnp.where(used, matrix_first, 0.0)
    matrix_second = jnp.where(used, matrix_second, 0.0)
    matrix_weights = jnp.where(used, matrix_weights, 0.0)
    vector_grads = vector_total * grad_scale
    vector_first_new, vector_second_new, vector_weights = adam_update(
        vector_grads, vector_first, vector_second, vectors, RATE_VECTOR, 0.0
    )
    return (
        out_tokens,
        token_grads,
        matrix_grads,
        matrix_first,
        matrix_second,
        matrix_weights,
        vector_grads,
        vector_first_new,
        vector_second_new,
        vector_weights,
    )


def solution(mesh):
    in_specs = (
        P(("dp", "frame"), None),
        P("dp", "frame", None),
        P(("dp", "frame"), None),
        P("dp"),
        P("dp"),
        P(),
        P("dp", None, "frame"),
        P("dp", None, "frame"),
        P("dp", None, "frame"),
        P(),
        P(),
        P(),
    )
    out_specs = (
        P(("dp", "frame"), None),
        P(("dp", "frame"), None),
        P("dp", None, "frame"),
        P("dp", None, "frame"),
        P("dp", None, "frame"),
        P("dp", None, "frame"),
        P(),
        P(),
        P(),
        P(),
    )
    return jax.shard_map(body, mesh=mesh, in_specs=in_specs, out_specs=out_specs, check_vma=False)
```

time: 2380 us -> 793 us (0.33)
  local copies, waits for them, and re-layouts: 797 us -> 49.6 us
  matrix products: 483 us -> 0 us
  waiting for transfers between devices: 623 us -> 344 us
  Pallas kernels: 0 us -> 256 us
  other arithmetic: 273 us -> 66 us
  blocking collectives: 167 us -> 57.2 us
    dot_general x62 -> x0, matrix products: 483 us -> none  [the longest x21 57.1 us: mat_dot(): return jnp.dot(operand, factor, preferred_element_type=jnp.float32)]
    reduce_scatter x1 -> x0, waiting for transfers between devices: 357 us -> none  [body(): lax.psum_scatter(by_quarter[picks], ('dp', 'frame'), scatter_dimension=0,...]
    gather x34 -> x1, local copies, waits for them, and re-layouts: 307 us -> 3.86 us  [body(): owned = jnp.concatenate([early, late], axis=0)[spot].transpose(0, 2, 1)]
    pallas_call x0 -> x8, Pallas kernels: none -> 256 us  [the longest x2 96 us: call_cross_backward(): pl.pallas_call(cross_backward_kernel, out_shape=(shape(count, D), shape(D...]
    all_gather x4 -> x1, waiting for transfers between devices: 266 us -> 109 us  [body(): lax.all_gather(master.astype(BF).transpose(0, 2, 1)[None], ('dp', 'frame'...]
    scatter-add x8 -> x0, other arithmetic: 142 us -> none  [the longest x4 71 us: cross_backward(): key_sum = key_sum.at[owners].add(grad_key)]
    psum x0 -> x1, waiting for transfers between devices: none -> 124 us  [reduced(): return lax.psum(quarter, 'dp')]
    ppermute x0 -> x9, waiting for transfers between devices: none -> 112 us  [swap(): return lax.ppermute(x, 'frame', [(i, i ^ bit) for i in range(4)])]
  transfers between devices with their start and end apart: 5 -> 11, of which waited for: 3 -> 5; matrix products, arithmetic and copies ran while one was open for 10% -> 11% of each run, Pallas kernels for 0% -> 24%
where the time goes in v1:
time: 793 us; the launch traced here: 796 us
  waiting for transfers between devices  344 us (43%)
  Pallas kernels  256 us (32%)
  other arithmetic  66 us (8%)
  blocking collectives  57.2 us (7%)
  local copies, waits for them, and re-layouts  49.6 us (6%)
  between operations  16.7 us (2%)
    psum x1, waiting for transfers between devices, reduced(): return lax.psum(quarter, 'dp')  124 us
    ppermute x9, waiting for transfers between devices, swap(): return lax.ppermute(x, 'frame', [(i, i ^ bit) for i in range(4)])  112 us
    all_gather x1, waiting for transfers between devices, body(): lax.all_gather(master.astype(BF).transpose(0, 2, 1)[None], ('dp', 'frame'...  109 us
    pallas_call x2, Pallas kernels, call_cross_backward(): pl.pallas_call(cross_backward_kernel, out_shape=(shape(count, D), shape(D...  96 us
    psum x1, blocking collectives, body(): vector_total = lax.psum(grad_vectors, ('dp', 'frame'))  57.2 us
    pallas_call x2, Pallas kernels, call_cross_forward(): pl.pallas_call(cross_forward_kernel, out_shape=shape(PARTIAL, D), grid_sp...  56.5 us
    pallas_call x1, Pallas kernels, call_middle(): pl.pallas_call(middle_kernel, out_shape=(shape(count, D, dtype=F32), shap...  34 us
    pallas_call x1, Pallas kernels, call_tables(): pl.pallas_call(tables_kernel, out_shape=(shape(slots, extent, D),) * 2, g...  28.2 us
  transfers between devices with their start and end apart: 11, of which 5 were waited for; matrix products, arithmetic and copies ran while one was open for 11% of the time, Pallas kernels for 24%

profile of v1, /device:TPU:0, one launch (start us, length us, event | category | flops | bytes accessed | tf_op | source)
XLA Modules:
  0.0 796.2 jit_solution(12322604869534050264)
XLA Ops:
  7.2 2.4 convert_bitcast_fusion
  9.7 13.6 %constant_dynamic-slice_fusion.11 = (bf16[1,1,8,375,768]{4,2,1,0,3:T(8,128)(2,1)}, bf16[1,1,8,375,768]{4,2,1,0,3:T(8,128)(2,1)}, bf16[1,1,8,375,768]{4,2,1,0,3:T(8,128)(2,1)}, bf16[1,1,8,375,768]{4,2,1,0,3:T(8,128)(2,1)}) fusion(bf16[2,2,8,375,768]{4,2,1,0,3:T(8,128)(2,1)} %bitcast.100, s32[]{:T(128)S(6)} %select_n.163, s32[]{:T(128)S(6)} %select_n.165, ...), kind=kLoop, calls=%fused_computation.81 | loop fusion | bytes 36864016 | tf_op jit(solution)/shard_map/jit(dynamic_index_in_dim)/dynamic_slice | solution.py:787
  23.4 5.7 copy_bitcast_fusion
  29.2 5.6 fusion.5
  44.5 1.9 concatenate.58.info
  47.9 6.2 copy_bitcast_fusion.2
  54.1 6.0 fusion.4
  60.2 108.8 %all-gather.3.cloned.1.call-done.tiles = bf16[512,192,128]{2,1,0:T(8,128)(2,1)} async-done(((bf16[16,192,128]{2,1,0:T(8,128)(2,1)}), bf16[512,192,128]{2,1,0:T(8,128)(2,1)}) %all-gather.3.cloned.1.call-update) | async-done | bytes 25165840 | tf_op jit(solution)/shard_map/all_gather | solution.py:771
  169.0 15.9 %front.1 = (f32[512,768]{1,0:T(8,128)}, bf16[512,768]{1,0:T(8,128)(2,1)}, bf16[512,768]{1,0:T(8,128)(2,1)}, bf16[512,768]{1,0:T(8,128)(2,1)}, bf16[512,768]{1,0:...) custom-call(s32[384]{0:T(512)} %add.200.where, bf16[512,768]{1,0:T(8,128)(2,1)} %tokens.3, f32[19,768]{1,0:T(8,128)} %vectors.7, ...), custom_call_target="tpu_custom_call" | custom-call | tf_op jit(solution)/shard_map/front/pallas_call | solution.py:537
  186.3 14.8 %pad_maximum_fusion.frames = bf16[16,768,768]{2,1,0:T(8,128)(2,1)} fusion(bf16[16,384,768]{2,1,0:T(8,128)(2,1)} %collective-permute-done, bf16[16,384,768]{2,1,0:T(8,128)(2,1)} %fusion.4), kind=kLoop, calls=%fused_computation.6 | loop fusion | flops 37748736 | bytes 37748736 | tf_op jit(solution)/shard_map/concatenate | solution.py:793
  201.1 28.2 %tables.1 = (bf16[16,768,768]{2,1,0:T(8,128)(2,1)}, bf16[16,768,768]{2,1,0:T(8,128)(2,1)}) custom-call(s32[17]{0:T(128)} %pad_add_fusion.act, s32[384]{0:T(512)} %add.200.where, bf16[16,768,768]{2,1,0:T(8,128)(2,1)} %pad_maximum_fusion.frames, f32[19,768]{1,0:T(8,128)} %vectors.7, bf16[512,192,128]{2,1,0:T(8,128)(2,1)} %all-gather.3.cloned.1.call-done.tiles), custom_call_target="tpu_custom_call" | custom-call | tf_op jit(solution)/shard_map/tables/pallas_call | solution.py:563
  230.3 34.3 %cross_forward.3 = bf16[544,768]{1,0:T(8,128)(2,1)} custom-call(s32[26]{0:T(128)} %concatenate.58.info, bf16[512,768]{1,0:T(8,128)(2,1)} %copy-done.4, bf16[16,768,768]{2,1,0:T(8,128)(2,1)} %get-tuple-element.39.key_table, bf16[16,768,768]{2,1,0:T(8,128)(2,1)} %get-tuple-element.40.value_table), custom_call_target="tpu_custom_call" | custom-call | tf_op jit(solution)/shard_map/cross_forward/pallas_call | solution.py:586
  265.6 1.9 concatenate.50.info
  267.5 22.2 %cross_forward.2.own = bf16[544,768]{1,0:T(8,128)(2,1)} custom-call(s32[26]{0:T(128)} %concatenate.50.info, bf16[512,768]{1,0:T(8,128)(2,1)} %get-tuple-element.38.query, bf16[16,768,768]{2,1,0:T(8,128)(2,1)} %get-tuple-element.39.key_table, bf16[16,768,768]{2,1,0:T(8,128)(2,1)} %get-tuple-element.40.value_table), custom_call_target="tpu_custom_call" | custom-call | tf_op jit(solution)/shard_map/cross_forward/pallas_call | solution.py:586
  290.6 34.0 %middle.1 = (f32[512,768]{1,0:T(8,128)}, f32[512,768]{1,0:T(8,128)}, bf16[560,768]{1,0:T(8,128)(2,1)}, f32[16,768]{1,0:T(8,128)}, bf16[2,54,192,128]{3,2,1,0:T(8,128)(2,1)}, /*index=5*/bf16[2,54,192,128]{3,2,1,0:T(8,128)(2,1)}) custom-call(s32[384]{0:T(512)} %add.200.where, s32[1]{0:T(128)} %bitcast.me, f32[512,768]{1,0:T(8,128)} %get-tuple-element.37.sum_one, ...), custom_call_target="tpu_custom_call" | custom-call | tf_op jit(solution)/shard_map/middle/pallas_call | solution.py:651
  325.3 1.8 collective-permute-start.3
  329.3 46.9 %cross_backward.2 = (bf16[512,768]{1,0:T(8,128)(2,1)}, f32[768,768]{1,0:T(8,128)}, f32[768,768]{1,0:T(8,128)}, f32[8,768]{1,0:T(8,128)}) custom-call(s32[26]{0:T(128)} %concatenate.50.info, bf16[512,768]{1,0:T(8,128)(2,1)} %get-tuple-element.38.query, bf16[560,768]{1,0:T(8,128)(2,1)} %get-tuple-element.48.packed, ...), custom_call_target="tpu_custom_call" | custom-call | tf_op jit(solution)/shard_map/cross_backward/pallas_call | solution.py:608
  377.1 49.1 %cross_backward.3 = (bf16[512,768]{1,0:T(8,128)(2,1)}, f32[768,768]{1,0:T(8,128)}, f32[768,768]{1,0:T(8,128)}, f32[8,768]{1,0:T(8,128)}) custom-call(s32[26]{0:T(128)} %concatenate.58.info, bf16[512,768]{1,0:T(8,128)(2,1)} %copy-done.4, bf16[560,768]{1,0:T(8,128)(2,1)} %copy-done.10, bf16[16,768,768]{2,1,0:T(8,128)(2,1)} %get-tuple-element.39.key_table, ...), custom_call_target="tpu_custom_call" | custom-call | tf_op jit(solution)/shard_map/cross_backward/pallas_call | solution.py:608
  433.4 12.7 %collective-permute-done.4.other = bf16[512,768]{1,0:T(8,128)(2,1)} collective-permute-done((bf16[512,768]{1,0:T(8,128)(2,1)}, bf16[512,768]{1,0:T(8,128)(2,1)}, u32[]{:S(2)}, u32[]{:S(2)}) %collective-permute-start.4) | collective-permute-done | bytes 786464 | tf_op jit(solution)/shard_map/ppermute | solution.py:748
  446.1 25.9 %last.1 = (f32[512,768]{1,0:T(8,128)}, f32[8,768]{1,0:T(8,128)}, bf16[2,30,192,128]{3,2,1,0:T(8,128)(2,1)}, bf16[2,30,192,128]{3,2,1,0:T(8,128)(2,1)}) custom-call(s32[384]{0:T(512)} %add.200.where, s32[1]{0:T(128)} %bitcast.me, bf16[512,768]{1,0:T(8,128)(2,1)} %tokens.3, f32[512,768]{1,0:T(8,128)} %get-tuple-element.37.sum_one, ...), custom_call_target="tpu_custom_call" | custom-call | tf_op jit(solution)/shard_map/last/pallas_call | solution.py:681
  472.1 3.8 pad_maximum_fusion.2
  476.9 4.8 add_convert_fusion
  483.5 3.1 add_convert_fusion.1
  487.3 98.1 %collective-permute-done.8 = bf16[42,192,128]{2,1,0:T(8,128)(2,1)S(1)} collective-permute-done((bf16[42,192,128]{2,1,0:T(8,128)(2,1)S(1)}, bf16[42,192,128]{2,1,0:T(8,128)(2,1)S(1)}, u32[]{:S(2)}, u32[]{:S(2)}) %collective-permute-start.8) | collective-permute-done | bytes 2064416 | tf_op jit(solution)/shard_map/ppermute | solution.py:748
  585.4 2.1 fusion.7
  587.5 2.5 fusion.6
  591.8 57.2 %psum.23 = f32[19,768]{1,0:T(8,128)S(1)} all-reduce(f32[19,768]{1,0:T(8,128)S(1)} %pad_maximum_fusion.3), channel_id=1, replica_groups=mesh['dp'=8,'frame'=4] {'dp','frame'}, use_global_device_ids=true, to_apply=%region_24.25 | all-reduce | flops 14592 | bytes 116736 | tf_op jit(solution)/shard_map/psum | solution.py:858
  649.8 123.8 %all-reduce.5.cloned.1.call-done = (bf16[42,192,128]{2,1,0:T(8,128)(2,1)}, bf16[54,192,128]{2,1,0:T(8,128)(2,1)}) async-done(((bf16[42,192,128]{2,1,0:T(8,128)(2,1)}, bf16[54,192,128]{2,1,0:T(8,128)(2,1)}), (bf16[42,192,128]{2,1,0:T(8,128)(2,1)}, bf16[54,192,128]{2,1,0:T(8,128)(2,1)})) %all-reduce.5.cloned.1.call-update) | async-done | bytes 4718608 | tf_op jit(solution)/shard_map/psum | solution.py:754
  773.5 5.1 pad_maximum_fusion.1
  778.6 3.9 gather_fusion
  782.4 4.4 subtract_select_fusion
  786.9 2.2 broadcast_select_fusion
  (130 shorter events, 30.6 us)
Async XLA Ops:
  7.2 161.8 %all-gather.3.cloned.1.call-start = ((), (), s32[]{:S(2)}) async-start(), calls=%async_computation | async-start | bytes 25952256 | tf_op jit(solution)/shard_map/all_gather | solution.py:771
  9.7 763.8 %all-reduce.5.cloned.1.call-start = ((), (), s32[]{:S(2)}) async-start(), calls=%async_computation.1 | async-start | bytes 9437184 | tf_op jit(solution)/shard_map/psum | solution.py:754
  29.1 6.0 copy-start.19
  29.1 6.8 copy-start.17
  29.1 6.9 copy-start.18
  34.7 151.6 %collective-permute-start = (bf16[16,384,768]{2,1,0:T(8,128)(2,1)}, bf16[16,384,768]{2,1,0:T(8,128)(2,1)}, u32[]{:S(2)}, u32[]{:S(2)}) collective-permute-start(bf16[16,384,768]{2,1,0:T(8,128)(2,1)} %fusion.5), channel_id=1, source_target_pairs={{0,1},{1,0},{2,3},{3,2},{4,5},{5,4},{6,7},{7,6},{8,9},{9,8},{10,11... | collective-permute-start | bytes 28311560 | tf_op jit(solution)/shard_map/ppermute | solution.py:748
  37.1 17.0 %copy-start.15 = (s32[512]{0:T(512)}, s32[512]{0:T(512)S(1)}, u32[]{:S(2)}) copy-start(s32[512]{0:T(512)S(1)} %broadcast_select_fusion.2) | copy-start | bytes 6148
  184.8 44.5 %collective-permute-start.1 = (bf16[512,768]{1,0:T(8,128)(2,1)}, bf16[512,768]{1,0:T(8,128)(2,1)S(1)}, u32[]{:S(2)}, u32[]{:S(2)}) collective-permute-start(bf16[512,768]{1,0:T(8,128)(2,1)} %get-tuple-element.38.query), channel_id=1, source_target_pairs={{0,2},{1,3},{2,0},{3,1},{4,6},{5,7},{6,4},{7,5},{8,10},{9,11},{10,... | collective-permute-start | bytes 2359304 | tf_op jit(solution)/shard_map/ppermute | solution.py:748
  229.4 0.9 copy-start.4
  264.6 25.1 %collective-permute-start.2 = (bf16[544,768]{1,0:T(8,128)(2,1)}, bf16[544,768]{1,0:T(8,128)(2,1)S(1)}, u32[]{:S(2)}, u32[]{:S(2)}) collective-permute-start(bf16[544,768]{1,0:T(8,128)(2,1)} %cross_forward.3), channel_id=1, source_target_pairs={{0,2},{1,3},{2,0},{3,1},{4,6},{5,7},{6,4},{7,5},{8,10},{9,11},{10,... | collective-permute-start | bytes 2506760 | tf_op jit(solution)/shard_map/ppermute | solution.py:748
  324.6 151.5 %collective-permute-start.5 = (bf16[2,54,192,128]{3,2,1,0:T(8,128)(2,1)}, bf16[2,54,192,128]{3,2,1,0:T(8,128)(2,1)}, u32[]{:S(2)}, u32[]{:S(2)}) collective-permute-start(bf16[2,54,192,128]{3,2,1,0:T(8,128)(2,1)} %get-tuple-element.56), channel_id=1, source_target_pairs={{0,1},{1,0},{2,3},{3,2},{4,5},{5,4},{6,7},{7,6},{8,9},{9,8},{10,11... | collective-permute-start | bytes 15925256 | tf_op jit(solution)/shard_map/ppermute | solution.py:748
  325.3 50.8 %collective-permute-start.3 = (bf16[560,768]{1,0:T(8,128)(2,1)}, bf16[560,768]{1,0:T(8,128)(2,1)S(1)}, u32[]{:S(2)}, u32[]{:S(2)}) collective-permute-start(bf16[560,768]{1,0:T(8,128)(2,1)} %get-tuple-element.48.packed), channel_id=1, source_target_pairs={{0,2},{1,3},{2,0},{3,1},{4,6},{5,7},{6,4},{7,5},{8,10},{9,11},{10,... | collective-permute-start | bytes 2580488 | tf_op jit(solution)/shard_map/ppermute | solution.py:748
  376.2 0.9 copy-start.10
  426.2 19.9 %collective-permute-start.4 = (bf16[512,768]{1,0:T(8,128)(2,1)}, bf16[512,768]{1,0:T(8,128)(2,1)}, u32[]{:S(2)}, u32[]{:S(2)}) collective-permute-start(bf16[512,768]{1,0:T(8,128)(2,1)} %get-tuple-element.53), channel_id=1, source_target_pairs={{0,2},{1,3},{2,0},{3,1},{4,6},{5,7},{6,4},{7,5},{8,10},{9,11},{10,... | collective-permute-start | bytes 2359304 | tf_op jit(solution)/shard_map/ppermute | solution.py:748
  429.6 1.8 copy-start.6
  446.1 25.9 %copy-start.8 = (bf16[1,192,6,128]{3,1,2,0:T(8,128)(2,1)S(1)}, bf16[1,192,6,128]{3,1,2,0:T(8,128)(2,1)}, u32[]{:S(2)}) copy-start(bf16[1,192,6,128]{3,1,2,0:T(8,128)(2,1)} %copy.106) | copy-start | bytes 884740
  446.1 25.9 %copy-start.9 = (bf16[1,192,6,128]{3,1,2,0:T(8,128)(2,1)S(1)}, bf16[1,192,6,128]{3,1,2,0:T(8,128)(2,1)}, u32[]{:S(2)}) copy-start(bf16[1,192,6,128]{3,1,2,0:T(8,128)(2,1)} %copy.107) | copy-start | bytes 884740
  472.0 4.1 slice-start
  472.1 4.9 slice-start.1
  475.9 7.4 collective-permute-start.7
  481.7 1.8 copy-start.5
  481.9 105.5 %collective-permute-start.6 = (bf16[54,192,128]{2,1,0:T(8,128)(2,1)S(1)}, bf16[54,192,128]{2,1,0:T(8,128)(2,1)S(1)}, u32[]{:S(2)}, u32[]{:S(2)}) collective-permute-start(bf16[54,192,128]{2,1,0:T(8,128)(2,1)S(1)} %slice_bitcast_fusion), channel_id=1, source_target_pairs={{0,2},{1,3},{2,0},{3,1},{4,6},{5,7},{6,4},{7,5},{8,10},{9,11},{10,... | collective-permute-start | bytes 7962632 | tf_op jit(solution)/shard_map/ppermute | solution.py:748
  486.8 98.6 %collective-permute-start.8 = (bf16[42,192,128]{2,1,0:T(8,128)(2,1)S(1)}, bf16[42,192,128]{2,1,0:T(8,128)(2,1)S(1)}, u32[]{:S(2)}, u32[]{:S(2)}) collective-permute-start(bf16[42,192,128]{2,1,0:T(8,128)(2,1)S(1)} %slice_bitcast_fusion.2), channel_id=1, source_target_pairs={{0,2},{1,3},{2,0},{3,1},{4,6},{5,7},{6,4},{7,5},{8,10},{9,11},{10,... | collective-permute-start | bytes 6193160 | tf_op jit(solution)/shard_map/ppermute | solution.py:748
  590.0 1.8 copy-start.14
  590.0 1.8 copy-start.16
  590.0 59.0 %copy-start.7 = (f32[19,768]{1,0:T(8,128)S(1)}, f32[19,768]{1,0:T(8,128)}, u32[]{:S(2)}) copy-start(f32[19,768]{1,0:T(8,128)} %vectors.7) | copy-start | bytes 175108
  590.0 59.0 %copy-start.12 = (f32[19,768]{1,0:T(8,128)S(1)}, f32[19,768]{1,0:T(8,128)}, u32[]{:S(2)}) copy-start(f32[19,768]{1,0:T(8,128)} %param.24) | copy-start | bytes 175108
  590.0 59.0 %copy-start.13 = (f32[19,768]{1,0:T(8,128)S(1)}, f32[19,768]{1,0:T(8,128)}, u32[]{:S(2)}) copy-start(f32[19,768]{1,0:T(8,128)} %param.23) | copy-start | bytes 175108
  773.5 8.9 %copy-start = (f32[16,128,192]{1,2,0:T(8,128)S(1)}, f32[16,128,192]{1,2,0:T(8,128)}, u32[]{:S(2)}) copy-start(f32[16,128,192]{1,2,0:T(8,128)} %param.19) | copy-start | bytes 4718596
  773.5 8.9 %copy-start.1 = (f32[16,128,192]{1,2,0:T(8,128)S(1)}, f32[16,128,192]{1,2,0:T(8,128)}, u32[]{:S(2)}) copy-start(f32[16,128,192]{1,2,0:T(8,128)} %param.20) | copy-start | bytes 4718596
  782.4 4.4 copy-start.2
  786.9 2.2 copy-start.3
  (2 other events, 1.6 us)
Sparse Core Ops, SparseCore 0:
  11.5 157.4 all-gather.2
  590.1 183.3 all-reduce.4

commit v2 on v1

--- a/solution.py
+++ b/solution.py
@@ -138,6 +138,17 @@
         copy.wait()
 
 
+def seen_bias(count, member_column, live_column, member_row):
+    key_ids = lax.broadcasted_iota(jnp.int32, (count, count), 0)
+    row_ids = lax.broadcasted_iota(jnp.int32, (count, count), 1)
+    seen = (
+        (member_column[...] == member_row[...])
+        & (key_ids <= row_ids)
+        & ((live_column[...] > 0) | (key_ids == row_ids))
+    )
+    return jnp.where(seen, 0.0, MASKED)
+
+
 def front_kernel(
     where, tokens, vectors, member_column, live_column, member_row, tiles,
     sum_one, cross_query, query, key, value, attended, lse,
@@ -150,14 +161,7 @@
         start_all(load)
     unit = eye()
     count = tokens.shape[0]
-    key_ids = lax.broadcasted_iota(jnp.int32, (count, count), 0)
-    row_ids = lax.broadcasted_iota(jnp.int32, (count, count), 1)
-    seen = (
-        (member_column[...] == member_row[...])
-        & (key_ids <= row_ids)
-        & ((live_column[...] > 0) | (key_ids == row_ids))
-    )
-    bias[...] = jnp.where(seen, 0.0, MASKED)
+    bias[...] = seen_bias(count, member_column, live_column, member_row)
     x = tokens[...].astype(F32)
     a = (norm_parts(x)[0] * vectors[0:1] + vectors[1:2]).astype(BF)
     wait_all(loads[0])
@@ -271,17 +275,15 @@
 
 
 def cross_backward_kernel(
-    info, query, packed, key_table, value_table, frames, grad_key_in, grad_value_in, bias_in,
-    grad_query, grad_key, grad_value, bias_grad,
+    info, query, packed, key_table, value_table, earlier, also_earlier,
+    grad_query, key_out, value_out, bias_grad,
     key_turned, key_sum, value_sum, lse, delta,
 ):
     step = pl.program_id(0)
 
     @pl.when(step == 0)
     def _():
-        grad_key[...] = grad_key_in[...]
-        grad_value[...] = grad_value_in[...]
-        bias_grad[...] = bias_in[...]
+        bias_grad[...] = jnp.zeros_like(bias_grad)
         extra = packed[512:PACKED].astype(F32)
         lse[...] = extra[0:8] + extra[8:16] + extra[16:24]
         delta[...] = extra[24:32] + extra[32:40] + extra[40:48]
@@ -311,13 +313,46 @@
                 grad_query[rows, cols] = dot_nt(pick, dq).astype(BF)
 
         each_unit(info, body)
-        f = frames[0]
         for g in range(GROUPS):
             cols = pl.ds(g * WIDE, WIDE)
-            grad_key[cols, :] += dot_nn(turned(key_sum[:, cols].astype(BF), unit), f)
             low = value_sum[:, cols].astype(BF)
-            grad_value[cols, :] += dot_nn(turned(low, unit), f)
             bias_grad[0:1, cols] += column_sum(low.astype(F32))
+            key_out[0, cols, :] = turned(key_sum[:, cols].astype(BF), unit)
+            value_out[0, cols, :] = turned(low, unit)
+
+
+def table_gradient_kernel(
+    info_own, info_far, me, key_own, value_own, frames_own, key_far, value_far, frames_far,
+    earlier,
+    keep, send, grad_key, grad_value, staged, sem,
+):
+    step = pl.program_id(0)
+
+    @pl.when(step == 0)
+    def _():
+        grad_key[...] = jnp.zeros_like(grad_key)
+        grad_value[...] = jnp.zeros_like(grad_value)
+
+    for info, key, value, frames in (
+        (info_own, key_own, value_own, frames_own),
+        (info_far, key_far, value_far, frames_far),
+    ):
+
+        @pl.when(step < info[0])
+        def _():
+            f = frames[0]
+            grad_key[...] += dot_nn(key[0], f)
+            grad_value[...] += dot_nn(value[0], f)
+
+    @pl.when(step == pl.num_programs(0) - 1)
+    def _():
+        staged[0] = grad_key[...].astype(BF)
+        staged[1] = grad_value[...].astype(BF)
+        copies = [gradient_copies(staged.at[i], keep, send, i, me[0], sem) for i in range(2)]
+        for copy in copies:
+            start_all(copy)
+        for copy in copies:
+            wait_all(copy)
 
 
 def middle_kernel(
@@ -431,50 +466,58 @@
         wait_all(gradient_copies(staged.at[i], keep, send, i, me[0], out_sem))
 
 
-def last_kernel(
-    where, me, tokens, sum_one, grad_two, query, key, value, attended, lse, own, other, vectors,
-    member_column, live_column, member_row, tiles,
-    token_grads, vector_grads, keep, send,
-    weights, staged, bias, grad_att, grad_q, grad_q_turned, grad_k, grad_v, sems, out_sem,
+def cross_back_kernel(
+    where, me, sum_one, grad_two, attended, own, other, vectors, tiles, earlier, also_earlier,
+    grad_one, grad_att, vector_grads, keep, send,
+    weights, staged, sems, out_sem,
 ):
-    order = (4, 3, 0, 1, 2)
-    loads = [
-        matrix_copies(tiles, where, m, weights.at[i], sems.at[i]) for i, m in enumerate(order)
-    ]
+    loads = [matrix_copies(tiles, where, m, weights.at[i], sems.at[i]) for i, m in enumerate((4, 3))]
     for load in loads:
         start_all(load)
     unit = eye()
-    count = tokens.shape[0]
-    key_ids = lax.broadcasted_iota(jnp.int32, (count, count), 0)
-    row_ids = lax.broadcasted_iota(jnp.int32, (count, count), 1)
-    seen = (
-        (member_column[...] == member_row[...])
-        & (key_ids <= row_ids)
-        & ((live_column[...] > 0) | (key_ids == row_ids))
-    )
-    bias[...] = jnp.where(seen, 0.0, MASKED)
-
-    def put(slot, value_):
-        staged[slot] = value_.astype(BF)
+
+    def put(slot, grad):
+        staged[slot] = grad.astype(BF)
         start_all(gradient_copies(staged.at[slot], keep, send, slot, me[0], out_sem))
 
     ecq = (own[...].astype(F32) + other[...].astype(F32)).astype(BF) * jnp.asarray(SCALE, BF)
     vector_grads[...] = jnp.zeros_like(vector_grads)
-    vector_grads[7:8] = column_sum(ecq.astype(F32))
+    vector_grads[3:4] = column_sum(ecq.astype(F32))
     unit_two, inverse_two = norm_parts(sum_one[...])
     c = (unit_two * vectors[5:6] + vectors[6:7]).astype(BF)
     put(0, dot_nn(turned(ecq, unit), c))
     wait_all(loads[0])
     dc = dot_nn(ecq, weights[0])
-    vector_grads[5:6] = column_sum(dc * unit_two)
-    vector_grads[6:7] = column_sum(dc)
+    vector_grads[1:2] = column_sum(dc * unit_two)
+    vector_grads[2:3] = column_sum(dc)
     dh1 = grad_two[...] + norm_back(dc, unit_two, inverse_two, vectors[5:6])
-    token_grads[...] = dh1
+    grad_one[...] = dh1
     e1 = dh1.astype(BF)
-    vector_grads[4:5] = column_sum(e1.astype(F32))
+    vector_grads[0:1] = column_sum(e1.astype(F32))
     put(1, dot_nn(turned(e1, unit), attended[...]))
     wait_all(loads[1])
     grad_att[...] = dot_nn(e1, weights[1]).astype(BF)
+    for i in range(2):
+        wait_all(gradient_copies(staged.at[i], keep, send, i, me[0], out_sem))
+
+
+def last_kernel(
+    where, me, tokens, grad_one, grad_att, query, key, value, lse, vectors,
+    member_column, live_column, member_row, tiles, earlier,
+    token_grads, vector_grads, keep, send,
+    weights, staged, bias, grad_q, grad_q_turned, grad_k, grad_v, sems, out_sem,
+):
+    loads = [matrix_copies(tiles, where, i, weights.at[i], sems.at[i]) for i in range(3)]
+    for load in loads:
+        start_all(load)
+    unit = eye()
+    count = tokens.shape[0]
+    bias[...] = seen_bias(count, member_column, live_column, member_row)
+
+    def put(slot, grad):
+        staged[slot] = grad.astype(BF)
+        start_all(gradient_copies(staged.at[slot], keep, send, slot, me[0], out_sem))
+
     lanes = lax.broadcasted_iota(jnp.int32, (1, WIDE), 1) >> 6
     for g in range(GROUPS):
         cols = pl.ds(g * WIDE, WIDE)
@@ -502,30 +545,90 @@
     x = tokens[...].astype(F32)
     unit_one, inverse_one = norm_parts(x)
     a = (unit_one * vectors[0:1] + vectors[1:2]).astype(BF)
+    vector_grads[...] = jnp.zeros_like(vector_grads)
     vector_grads[2:3] = column_sum(grad_q[...].astype(F32))
     vector_grads[3:4] = column_sum(grad_v[...].astype(F32))
-    put(2, dot_nn(grad_q_turned[...], a))
-    put(3, dot_nn(turned(grad_k[...], unit), a))
-    put(4, dot_nn(turned(grad_v[...], unit), a))
-    wait_all(loads[2])
-    wait_all(loads[3])
-    wait_all(loads[4])
+    put(0, dot_nn(grad_q_turned[...], a))
+    put(1, dot_nn(turned(grad_k[...], unit), a))
+    put(2, dot_nn(turned(grad_v[...], unit), a))
+    for load in loads:
+        wait_all(load)
     da = (
-        dot_nn(grad_q[...], weights[2])
-        + dot_nn(grad_k[...], weights[3])
-        + dot_nn(grad_v[...], weights[4])
+        dot_nn(grad_q[...], weights[0])
+        + dot_nn(grad_k[...], weights[1])
+        + dot_nn(grad_v[...], weights[2])
     )
     vector_grads[0:1] = column_sum(da * unit_one)
     vector_grads[1:2] = column_sum(da)
-    token_grads[...] += norm_back(da, unit_one, inverse_one, vectors[0:1])
-    for i in range(5):
+    token_grads[...] = grad_one[...] + norm_back(da, unit_one, inverse_one, vectors[0:1])
+    for i in range(3):
         wait_all(gradient_copies(staged.at[i], keep, send, i, me[0], out_sem))
+
+
+def panel_copies(place, early, late, target, sem):
+    cap = target.shape[0]
+    count = early.shape[0] // 192
+
+    def rows(i):
+        return pl.ds(pl.multiple_of(i * 192, 192), 192)
+
+    def start(i, state):
+        @pl.when(place[i] < count)
+        def _():
+            pltpu.make_async_copy(early.at[rows(place[i])], target.at[i], sem).start()
+
+        @pl.when(place[i] >= count)
+        def _():
+            pltpu.make_async_copy(late.at[rows(place[i] - count)], target.at[i], sem).start()
+
+        return state
+
+    def wait(i, state):
+        pltpu.make_async_copy(early.at[pl.ds(0, 192)], target.at[i], sem).wait()
+        return state
+
+    lax.fori_loop(0, cap, start, 0)
+    lax.fori_loop(0, cap, wait, 0)
+
+
+def pick_kernel(place, early, late, earlier, out, sem):
+    del earlier
+    panel_copies(place, early, late, out, sem)
+
+
+def update_kernel_of(
+    row_total, place, source, early, late, got, master, first_moment, second_moment,
+    grad_out, first_out, second_out, weight_out, own, sem,
+):
+    cap = got.shape[0]
+    panel_copies(place, early, late, own, sem)
+
+    def one(i, state):
+        used = source[i] < 2
+        low = jnp.where(source[i] == 0, own[i], got[i])
+        grad = jnp.where(used, low.astype(F32) * (1.0 / math.sqrt(row_total)), 0.0)
+        first, second, weight = adam_update(
+            grad, first_moment[i], second_moment[i], master[i], RATE_MATRIX, DECAY_MATRIX
+        )
+        grad_out[i] = grad
+        first_out[i] = jnp.where(used, first, 0.0)
+        second_out[i] = jnp.where(used, second, 0.0)
+        weight_out[i] = jnp.where(used, weight, 0.0)
+        return state
+
+    lax.fori_loop(0, cap, one, 0)
 
 
 SMEM = pl.BlockSpec(memory_space=pltpu.SMEM)
 WHOLE = pl.BlockSpec(memory_space=pltpu.VMEM)
 AWAY = pl.BlockSpec(memory_space=pl.ANY)
 PARAMS = pltpu.CompilerParams(vmem_limit_bytes=VMEM_LIMIT)
+
+
+def cost(microseconds):
+    return pl.CostEstimate(
+        flops=int(microseconds * 1e9), bytes_accessed=1 << 20, transcendentals=0
+    )
 
 
 def shape(*dims, dtype=BF):
@@ -549,6 +652,7 @@
             pltpu.SemaphoreType.DMA((5,)),
         ],
         compiler_params=PARAMS,
+        cost_estimate=cost(16),
         name="front",
     )(where, tokens, vectors, *layout, tiles)
 
@@ -571,6 +675,7 @@
             scratch_shapes=[pltpu.VMEM((2, D, D), BF), pltpu.SemaphoreType.DMA((2,))],
         ),
         compiler_params=PARAMS,
+        cost_estimate=cost(30),
         name="tables",
     )(act, where, frames, vectors, tiles)
 
@@ -597,41 +702,29 @@
             ],
         ),
         compiler_params=PARAMS,
+        cost_estimate=cost(23),
         name="cross_forward",
     )(info, query, key_table, value_table)
 
 
-def call_cross_backward(info, query, packed, key_table, value_table, frames, sums, base):
+def call_cross_backward(info, query, packed, key_table, value_table, earlier, base):
     count, extent = query.shape[0], key_table.shape[1]
     slots = 8
     block = pl.BlockSpec((1, extent, D), lambda i, info: (base + info[2 + i], 0, 0))
+    block_out = pl.BlockSpec((1, D, extent), lambda i, info: (info[2 + i], 0, 0))
     return pl.pallas_call(
         cross_backward_kernel,
         out_shape=(
             shape(count, D),
-            shape(D, D, dtype=F32),
-            shape(D, D, dtype=F32),
+            shape(slots, D, extent),
+            shape(slots, D, extent),
             shape(8, D, dtype=F32),
         ),
         grid_spec=pltpu.PrefetchScalarGridSpec(
             num_scalar_prefetch=1,
             grid=(slots,),
-            in_specs=[
-                whole_spec(count, D),
-                whole_spec(PACKED, D),
-                block,
-                block,
-                block,
-                whole_spec(D, D),
-                whole_spec(D, D),
-                whole_spec(8, D),
-            ],
-            out_specs=(
-                whole_spec(count, D),
-                whole_spec(D, D),
-                whole_spec(D, D),
-                whole_spec(8, D),
-            ),
+            in_specs=[whole_spec(count, D), whole_spec(PACKED, D), block, block, AWAY, AWAY],
+            out_specs=(whole_spec(count, D), block_out, block_out, whole_spec(8, D)),
             scratch_shapes=[
                 pltpu.VMEM((GROUPS, WIDE, extent), BF),
                 pltpu.VMEM((extent, D), F32),
@@ -641,8 +734,40 @@
             ],
         ),
         compiler_params=PARAMS,
+        cost_estimate=cost(40),
         name="cross_backward",
-    )(info, query, packed, key_table, value_table, frames, *sums)
+    )(info, query, packed, key_table, value_table, *earlier)
+
+
+def call_table_gradient(infos, me, own, far, frames, earlier):
+    slots, extent = own[0].shape[0], frames.shape[1]
+
+    def block(part, base, *dims):
+        return pl.BlockSpec((1, *dims), lambda i, *infos: (base + infos[part][2 + i], 0, 0))
+
+    specs = []
+    for part in range(2):
+        specs += [block(part, 0, D, extent)] * 2 + [block(part, part * slots, extent, D)]
+    part = shape(2, 2 * ROWS, 192, PANEL)
+    return pl.pallas_call(
+        table_gradient_kernel,
+        out_shape=(part, part),
+        grid_spec=pltpu.PrefetchScalarGridSpec(
+            num_scalar_prefetch=3,
+            grid=(slots,),
+            in_specs=[*specs, AWAY],
+            out_specs=(AWAY, AWAY),
+            scratch_shapes=[
+                pltpu.VMEM((D, D), F32),
+                pltpu.VMEM((D, D), F32),
+                pltpu.VMEM((2, D, D), BF),
+                pltpu.SemaphoreType.DMA,
+            ],
+        ),
+        compiler_params=PARAMS,
+        cost_estimate=cost(20),
+        name="table_gradient",
+    )(*infos, me, *own, frames, *far, frames, earlier)
 
 
 def call_middle(where, me, sum_one, own, other, vectors, live, cotangent, tiles):
@@ -671,33 +796,82 @@
             pltpu.SemaphoreType.DMA,
         ],
         compiler_params=PARAMS,
+        cost_estimate=cost(34),
         name="middle",
     )(where, me, sum_one, own, other, vectors, live, cotangent, tiles)
 
 
-def call_last(where, me, tokens, sum_one, grad_two, saved, own, other, vectors, layout, tiles):
+def call_cross_back(where, me, sum_one, grad_two, attended, own, other, vectors, tiles, earlier):
+    count = sum_one.shape[0]
+    part = shape(2, 2 * ROWS, 192, PANEL)
+    return pl.pallas_call(
+        cross_back_kernel,
+        out_shape=(shape(count, D, dtype=F32), shape(count, D), shape(8, D, dtype=F32), part, part),
+        in_specs=[SMEM, SMEM] + [WHOLE] * 6 + [AWAY] * 3,
+        out_specs=(WHOLE, WHOLE, WHOLE, AWAY, AWAY),
+        scratch_shapes=[
+            pltpu.VMEM((2, D, D), BF),
+            pltpu.VMEM((2, D, D), BF),
+            pltpu.SemaphoreType.DMA((2,)),
+            pltpu.SemaphoreType.DMA,
+        ],
+        compiler_params=PARAMS,
+        cost_estimate=cost(8),
+        name="cross_back",
+    )(where, me, sum_one, grad_two, attended, own, other, vectors, tiles, *earlier)
+
+
+def call_last(where, me, tokens, grad_one, grad_att, saved, vectors, layout, tiles, earlier):
     count = tokens.shape[0]
-    part = shape(2, 5 * ROWS, 192, PANEL)
+    part = shape(2, 3 * ROWS, 192, PANEL)
     return pl.pallas_call(
         last_kernel,
         out_shape=(shape(count, D, dtype=F32), shape(8, D, dtype=F32), part, part),
-        in_specs=[SMEM, SMEM] + [WHOLE] * 14 + [AWAY],
+        in_specs=[SMEM, SMEM] + [WHOLE] * 11 + [AWAY] * 2,
         out_specs=(WHOLE, WHOLE, AWAY, AWAY),
         scratch_shapes=[
-            pltpu.VMEM((5, D, D), BF),
-            pltpu.VMEM((5, D, D), BF),
+            pltpu.VMEM((3, D, D), BF),
+            pltpu.VMEM((3, D, D), BF),
             pltpu.VMEM((count, count), F32),
-            pltpu.VMEM((count, D), BF),
             pltpu.VMEM((count, D), BF),
             pltpu.VMEM((D, count), BF),
             pltpu.VMEM((count, D), BF),
             pltpu.VMEM((count, D), BF),
-            pltpu.SemaphoreType.DMA((5,)),
+            pltpu.SemaphoreType.DMA((3,)),
             pltpu.SemaphoreType.DMA,
         ],
         compiler_params=PARAMS,
+        cost_estimate=cost(20),
         name="last",
-    )(where, me, tokens, sum_one, grad_two, *saved, own, other, vectors, *layout, tiles)
+    )(where, me, tokens, grad_one, grad_att, *saved, vectors, *layout, tiles, earlier)
+
+
+def call_pick(place, early, late, earlier):
+    cap = place.shape[0]
+    return pl.pallas_call(
+        pick_kernel,
+        out_shape=shape(cap, 192, PANEL),
+        in_specs=[SMEM, AWAY, AWAY, AWAY],
+        out_specs=WHOLE,
+        scratch_shapes=[pltpu.SemaphoreType.DMA],
+        compiler_params=PARAMS,
+        cost_estimate=cost(3),
+        name="pick",
+    )(place, early, late, earlier)
+
+
+def call_update(row_total, place, source, early, late, got, weights):
+    cap = got.shape[0]
+    return pl.pallas_call(
+        functools.partial(update_kernel_of, row_total),
+        out_shape=(shape(cap, 192, PANEL, dtype=F32),) * 4,
+        in_specs=[SMEM, SMEM, AWAY, AWAY] + [WHOLE] * 4,
+        out_specs=(WHOLE,) * 4,
+        scratch_shapes=[pltpu.VMEM((cap, 192, PANEL), BF), pltpu.SemaphoreType.DMA],
+        compiler_params=PARAMS,
+        cost_estimate=cost(6),
+        name="update",
+    )(place, source, early, late, got, *weights)
 
 
 def row_layout(bucket, length, row_count):
@@ -748,10 +922,49 @@
     return lax.ppermute(x, "frame", [(i, i ^ bit) for i in range(4)])
 
 
-def reduced(keep, send):
-    mine = (keep.astype(F32) + swap(send, 1).astype(F32)).astype(BF)
-    quarter = (mine[0].astype(F32) + swap(mine[1], 2).astype(F32)).astype(BF)
-    return lax.psum(quarter, "dp")
+def over_dp(x, bit):
+    size = lax.axis_size("dp")
+    return lax.ppermute(x, "dp", [(i, i ^ bit) for i in range(size)])
+
+
+def added(a, b):
+    return (a.astype(F32) + b.astype(F32)).astype(BF)
+
+
+def frame_sum(keep, send):
+    mine = added(keep, swap(send, 1))
+    return added(mine[0], swap(mine[1], 2))
+
+
+def dp_bits():
+    size, bits = lax.axis_size("dp"), []
+    while 2 ** len(bits) < size:
+        bits.append(2 ** len(bits))
+    return bits
+
+
+def half_sum(x, bit):
+    half = x.shape[0] // 2
+    upper = (lax.axis_index("dp") // bit) & 1
+    kept = lax.dynamic_slice_in_dim(x, upper * half, half)
+    sent = lax.dynamic_slice_in_dim(x, (1 - upper) * half, half)
+    return added(kept, over_dp(sent, bit))
+
+
+def both_halves(x, bit):
+    upper = (lax.axis_index("dp") // bit) & 1
+    got = over_dp(x, bit)
+    return jnp.where(
+        upper == 0, jnp.concatenate([x, got], axis=0), jnp.concatenate([got, x], axis=0)
+    )
+
+
+def total_sum(x):
+    for bit in (1, 2):
+        x = x + swap(x, bit)
+    for bit in dp_bits():
+        x = x + over_dp(x, bit)
+    return x
 
 
 def body(
@@ -819,52 +1032,104 @@
         cotangent, tiles,
     )
     far_packed = swap(packed, 2)
-    zeros = (jnp.zeros((D, D), F32), jnp.zeros((D, D), F32), jnp.zeros((8, D), F32))
-    own_grad, *sums = call_cross_backward(
-        infos[0], cross_query, packed, key_table, value_table, all_frames, zeros, 0
-    )
-    far_grad, grad_ck, grad_cv, bias_cv = call_cross_backward(
-        infos[1], far_query, far_packed, key_table, value_table, all_frames, sums, slots
-    )
+    pair_mid = added(keep_mid, swap(send_mid, 1))
+    cuts = (0, 3 * ROWS, 9 * ROWS)
+
+    def across(part):
+        mine = pair_mid[:, cuts[part] : cuts[part + 1]]
+        return added(mine[0], swap(mine[1], 2))
+
+    own_grad, *own_sums, own_bias = call_cross_backward(
+        infos[0], cross_query, packed, key_table, value_table, (pair_mid, pair_mid), 0
+    )
+    early_one = across(0)
+    far_grad, *far_sums, far_bias = call_cross_backward(
+        infos[1], far_query, far_packed, key_table, value_table, (own_grad, early_one), slots
+    )
+    early_two = across(1)
+    early = jnp.concatenate([early_one, early_two], axis=0).reshape(-1, PANEL)
+    bits = dp_bits()
     other_grad = swap(far_grad, 2)
+    keep_table, send_table = call_table_gradient(
+        infos, place, own_sums, far_sums, all_frames, early_two
+    )
+    *saved_heads, attended, lse = saved
+    early = half_sum(early, bits[0])
+    grad_one, grad_att, vectors_cross, keep_cross, send_cross = call_cross_back(
+        where, place, sum_one, grad_two, attended, own_grad, other_grad, vectors, tiles,
+        (keep_table, early),
+    )
+    early = half_sum(early, bits[1])
+    pair_cross = added(
+        jnp.concatenate([keep_table, keep_cross], axis=1),
+        swap(jnp.concatenate([send_table, send_cross], axis=1), 1),
+    )
     token_grads, vectors_last, keep_last, send_last = call_last(
-        where, place, tokens, sum_one, grad_two, saved, own_grad, other_grad, vectors, layout, tiles
-    )
-
-    def split(grad):
-        parts = (
-            grad.astype(BF).reshape(4, 192, ROWS, PANEL).transpose(0, 2, 1, 3)
+        where, place, tokens, grad_one, grad_att, [*saved_heads, lse], vectors, layout, tiles,
+        pair_cross,
+    )
+    late = jnp.concatenate(
+        [added(pair_cross[0], swap(pair_cross[1], 2)), frame_sum(keep_last, send_last)], axis=0
+    ).reshape(-1, PANEL)
+    late = half_sum(late, bits[0])
+    for bit in bits[2:]:
+        early = half_sum(early, bit)
+    for bit in bits[1:]:
+        late = half_sum(late, bit)
+    for bit in reversed(bits[1:]):
+        early = both_halves(early, bit)
+        late = both_halves(late, bit)
+    grad_vectors = jnp.concatenate(
+        [
+            vectors_last[0:4],
+            vectors_cross[0:4],
+            own_bias[0:1] + far_bias[0:1],
+            vectors_mid[0:10],
+            jnp.zeros((5, D), F32),
+        ],
+        axis=0,
+    )
+    vector_total = total_sum(grad_vectors)[0 : vectors.shape[0]]
+    held = ((7, *range(8, 16)), (5, 6, 4, 3, 0, 1, 2))
+    halves_of, places_of = {}, {}
+    base = 0
+    for matrices in held:
+        middle = len(matrices) * ROWS // 2
+        for i in range(2 * middle):
+            panel = matrices[i // ROWS] * ROWS + i % ROWS
+            halves_of[panel] = i // middle
+            places_of[panel] = base + i % middle
+        base += middle
+    panel_half = jnp.asarray([halves_of[p] for p in range(panel_total)], jnp.int32)
+    panel_place = jnp.asarray([places_of[p] for p in range(panel_total)], jnp.int32)
+
+    def slots_of(group):
+        slot_ids = group * cap + jnp.arange(cap, dtype=jnp.int32)
+        matches = slot_of[:, None] == slot_ids[None, :]
+        half, place_ = (
+            jnp.sum(jnp.where(matches, values[:, None], 0), axis=0, dtype=jnp.int32)
+            for values in (panel_half, panel_place)
         )
-        pieces = [lax.dynamic_index_in_dim(parts, me ^ i, 0, False) for i in range(4)]
-        return jnp.stack([pieces[0], pieces[2]]), jnp.stack([pieces[1], pieces[3]])
-
-    keep_k, send_k = split(grad_ck)
-    keep_v, send_v = split(grad_cv)
-    early = reduced(keep_mid, send_mid)
-    late = reduced(
-        jnp.concatenate([keep_k, keep_v, keep_last], axis=1),
-        jnp.concatenate([send_k, send_v, send_last], axis=1),
-    )
-    at = {m: i for i, m in enumerate((7, *range(8, 16), 5, 6, 4, 3, 0, 1, 2))}
-    spots = jnp.asarray([at[p // ROWS] * ROWS + p % ROWS for p in range(panel_total)], jnp.int32)
-    slot_ids = group_index * cap + jnp.arange(cap, dtype=jnp.int32)
-    matches = slot_of[:, None] == slot_ids[None, :]
-    spot = jnp.sum(jnp.where(matches, spots[:, None], 0), axis=0, dtype=jnp.int32)
-    used = jnp.any(matches, axis=0)[:, None, None]
-    owned = jnp.concatenate([early, late], axis=0)[spot].transpose(0, 2, 1)
-    grad_vectors = jnp.concatenate(
-        [vectors_last[0:8], bias_cv[0:1], vectors_mid[0:10]], axis=0
-    )
-    vector_total = lax.psum(grad_vectors, ("dp", "frame"))
-    grad_scale = 1.0 / math.sqrt(row_count * group_count * frame_count)
-    matrix_grads = jnp.where(used, owned.astype(F32) * grad_scale, 0.0)
-    matrix_first, matrix_second, matrix_weights = adam_update(
-        matrix_grads, first_moment, second_moment, master, RATE_MATRIX, DECAY_MATRIX
-    )
-    matrix_first = jnp.where(used, matrix_first, 0.0)
-    matrix_second = jnp.where(used, matrix_second, 0.0)
-    matrix_weights = jnp.where(used, matrix_weights, 0.0)
-    vector_grads = vector_total * grad_scale
+        return half, place_, jnp.any(matches, axis=0)
+
+    upper = (group_index // bits[0]) & 1
+    half, own_place, used = slots_of(group_index)
+    far_place = slots_of(group_index ^ bits[0])[1]
+    got = over_dp(call_pick(far_place, early, late, vector_total), bits[0])
+    row_total = row_count * group_count * frame_count
+    updates = call_update(
+        row_total,
+        own_place,
+        jnp.where(used, jnp.where(half == upper, 0, 1), 2),
+        early,
+        late,
+        got,
+        [w.transpose(0, 2, 1) for w in (master, first_moment, second_moment)],
+    )
+    matrix_grads, matrix_first, matrix_second, matrix_weights = (
+        u.transpose(0, 2, 1) for u in updates
+    )
+    vector_grads = vector_total * (1.0 / math.sqrt(row_total))
     vector_first_new, vector_second_new, vector_weights = adam_update(
         vector_grads, vector_first, vector_second, vectors, RATE_VECTOR, 0.0
     )

time: 793 us -> 661 us (0.83); the launches traced: 796 us -> 656 us
  waiting for transfers between devices: 344 us -> 234 us
  blocking collectives: 57.2 us -> 0 us
  Pallas kernels: 256 us -> 276 us
  starting transfers between devices: 5.76 us -> 19 us
    psum x1 -> x0, waiting for transfers between devices: 124 us -> none  [reduced(): return lax.psum(quarter, 'dp')]
    ppermute x0 -> x14, waiting for transfers between devices: none -> 85.1 us  [over_dp(): return lax.ppermute(x, 'dp', [(i, i ^ bit) for i in range(size)])]
    ppermute x9 -> x14, waiting for transfers between devices: 112 us -> 54.6 us  [swap(): return lax.ppermute(x, 'frame', [(i, i ^ bit) for i in range(4)])]
    psum x1 -> x0, blocking collectives: 57.2 us -> none  [body(): vector_total = lax.psum(grad_vectors, ('dp', 'frame'))]
    pallas_call x2 -> x6, Pallas kernels: 96 us -> 124 us  [the longest x2 70.9 us: call_cross_backward(): pl.pallas_call(cross_backward_kernel, out_shape=(shape(count, D), shape(s...]
    all_gather x1, waiting for transfers between devices: 109 us -> 93.9 us  [body(): lax.all_gather(master.astype(BF).transpose(0, 2, 1)[None], ('dp', 'frame'...]
    pallas_call x2, Pallas kernels: 56.5 us -> 46 us  [call_cross_forward(): pl.pallas_call(cross_forward_kernel, out_shape=shape(PARTIAL, D), grid_sp...]
    convert_element_type x6 -> x13, other arithmetic: 14.3 us -> 23.2 us  [added(): return (a.astype(F32) + b.astype(F32)).astype(BF)]
  transfers between devices with their start and end apart: 11 -> 29, of which waited for: 5 -> 14; matrix products, arithmetic and copies ran while one was open for 11% -> 15% of each run, Pallas kernels for 24% -> 24%
where the time goes in v2:
time: 661 us; the launch traced here: 656 us
  Pallas kernels  276 us (42%)
  waiting for transfers between devices  234 us (35%)
  other arithmetic  64.1 us (10%)
  local copies, waits for them, and re-layouts  46.9 us (7%)
  starting transfers between devices  19 us (3%)
  between operations  16.9 us (3%)
    all_gather x1, waiting for transfers between devices, body(): lax.all_gather(master.astype(BF).transpose(0, 2, 1)[None], ('dp', 'frame'...  93.9 us
    ppermute x14, waiting for transfers between devices, over_dp(): return lax.ppermute(x, 'dp', [(i, i ^ bit) for i in range(size)])  85.1 us
    pallas_call x2, Pallas kernels, call_cross_backward(): pl.pallas_call(cross_backward_kernel, out_shape=(shape(count, D), shape(s...  70.9 us
    ppermute x14, waiting for transfers between devices, swap(): return lax.ppermute(x, 'frame', [(i, i ^ bit) for i in range(4)])  54.6 us
    pallas_call x2, Pallas kernels, call_cross_forward(): pl.pallas_call(cross_forward_kernel, out_shape=shape(PARTIAL, D), grid_sp...  46 us
    pallas_call x1, Pallas kernels, call_middle(): pl.pallas_call(middle_kernel, out_shape=(shape(count, D, dtype=F32), shap...  34.4 us
    pallas_call x1, Pallas kernels, call_table_gradient(): pl.pallas_call(table_gradient_kernel, out_shape=(part, part), grid_spec=p...  32.6 us
    pallas_call x1, Pallas kernels, call_tables(): pl.pallas_call(tables_kernel, out_shape=(shape(slots, extent, D),) * 2, g...  32.2 us
  transfers between devices with their start and end apart: 29, of which 14 were waited for; matrix products, arithmetic and copies ran while one was open for 15% of the time, Pallas kernels for 24%

profile of v2, /device:TPU:0, one launch (start us, length us, event | category | flops | bytes accessed | tf_op | source)
XLA Modules:
  0.0 656.2 jit_solution(9193002515797757053)
XLA Ops:
  9.7 13.6 %constant_dynamic-slice_fusion.9 = (bf16[1,1,8,375,768]{4,2,1,0,3:T(8,128)(2,1)}, bf16[1,1,8,375,768]{4,2,1,0,3:T(8,128)(2,1)}, bf16[1,1,8,375,768]{4,2,1,0,3:T(8,128)(2,1)}, bf16[1,1,8,375,768]{4,2,1,0,3:T(8,128)(2,1)}) fusion(bf16[2,2,8,375,768]{4,2,1,0,3:T(8,128)(2,1)} %bitcast.92, s32[]{:T(128)S(6)} %select_n.222, s32[]{:T(128)S(6)} %select_n.224, ...), kind=kLoop, calls=%fused_computation.74 | loop fusion | bytes 36864016 | tf_op jit(solution)/shard_map/jit(dynamic_index_in_dim)/dynamic_slice | solution.py:1000
  23.3 5.7 copy_bitcast_fusion
  29.1 5.7 fusion.5
  50.8 5.5 copy_bitcast_fusion.2
  56.3 3.7 fusion.4
  60.0 14.8 %pad_maximum_fusion.frames.frames_own.frames_far = bf16[16,768,768]{2,1,0:T(8,128)(2,1)} fusion(bf16[16,384,768]{2,1,0:T(8,128)(2,1)} %collective-permute-done, bf16[16,384,768]{2,1,0:T(8,128)(2,1)S(1)} %fusion.4), kind=kLoop, calls=%fused_computation.5 | loop fusion | flops 37748736 | bytes 37748736 | tf_op jit(solution)/shard_map/concatenate | solution.py:1006
  74.9 93.9 %all-gather.3.cloned.1.call-done.tiles = bf16[512,192,128]{2,1,0:T(8,128)(2,1)} async-done(((bf16[16,192,128]{2,1,0:T(8,128)(2,1)}), bf16[512,192,128]{2,1,0:T(8,128)(2,1)}) %all-gather.3.cloned.1.call-update) | async-done | bytes 25165840 | tf_op jit(solution)/shard_map/all_gather | solution.py:984
  168.8 15.9 %front.1 = (f32[512,768]{1,0:T(8,128)}, bf16[512,768]{1,0:T(8,128)(2,1)}, bf16[512,768]{1,0:T(8,128)(2,1)}, bf16[512,768]{1,0:T(8,128)(2,1)}, bf16[512,768]{1,0:...) custom-call(s32[384]{0:T(512)} %add.250.where, bf16[512,768]{1,0:T(8,128)(2,1)} %tokens.3, f32[19,768]{1,0:T(8,128)} %vectors.9, ...), custom_call_target="tpu_custom_call" | custom-call | flops 16000000000 | bytes 1048576 | tf_op jit(solution)/shard_map/front/pallas_call | solution.py:640
  186.2 32.2 %tables.1 = (bf16[16,768,768]{2,1,0:T(8,128)(2,1)}, bf16[16,768,768]{2,1,0:T(8,128)(2,1)}) custom-call(s32[17]{0:T(128)} %pad_add_fusion.act, s32[384]{0:T(512)} %add.250.where, bf16[16,768,768]{2,1,0:T(8,128)(2,1)} %pad_maximum_fusion.frames.frames_own.frames_far, f32[19,768]{1,0:T(8,128)} %vectors.9, bf16[512,192,128]{2,1,0:T(8,128)(2,1)} %all-gather.3.cloned.1.call-done.tiles), custom_call_target="tpu_custom_call" | custom-call | flops 30000001024 | bytes 1048576 | tf_op jit(solution)/shard_map/tables/pallas_call | solution.py:667
  219.3 22.9 %cross_forward.3 = bf16[544,768]{1,0:T(8,128)(2,1)} custom-call(s32[26]{0:T(128)} %concatenate.85.info.info_far, bf16[512,768]{1,0:T(8,128)(2,1)} %copy-done.25, bf16[16,768,768]{2,1,0:T(8,128)(2,1)} %get-tuple-element.50.key_table, bf16[16,768,768]{2,1,0:T(8,128)(2,1)} %get-tuple-element.51.value_table), custom_call_target="tpu_custom_call" | custom-call | flops 23000000512 | bytes 1048576 | tf_op jit(solution)/shard_map/cross_forward/pallas_call | solution.py:691
  243.5 23.2 %cross_forward.2.own = bf16[544,768]{1,0:T(8,128)(2,1)} custom-call(s32[26]{0:T(128)} %concatenate.77.info.info_own, bf16[512,768]{1,0:T(8,128)(2,1)} %get-tuple-element.49.query, bf16[16,768,768]{2,1,0:T(8,128)(2,1)} %get-tuple-element.50.key_table, bf16[16,768,768]{2,1,0:T(8,128)(2,1)} %get-tuple-element.51.value_table), custom_call_target="tpu_custom_call" | custom-call | flops 23000000512 | bytes 1048576 | tf_op jit(solution)/shard_map/cross_forward/pallas_call | solution.py:691
  267.6 34.4 %middle.1 = (f32[512,768]{1,0:T(8,128)}, f32[512,768]{1,0:T(8,128)}, bf16[560,768]{1,0:T(8,128)(2,1)}, f32[16,768]{1,0:T(8,128)}, bf16[2,54,192,128]{3,2,1,0:T(8,128)(2,1)}, /*index=5*/bf16[2,54,192,128]{3,2,1,0:T(8,128)(2,1)}) custom-call(s32[384]{0:T(512)} %add.250.where, s32[1]{0:T(128)} %bitcast.me, f32[512,768]{1,0:T(8,128)} %get-tuple-element.48.sum_one, ...), custom_call_target="tpu_custom_call" | custom-call | flops 33999998976 | bytes 1048576 | tf_op jit(solution)/shard_map/middle/pallas_call | solution.py:776
  303.2 8.0 %collective-permute-done.3 = bf16[2,54,192,128]{3,2,1,0:T(8,128)(2,1)} collective-permute-done((bf16[2,54,192,128]{3,2,1,0:T(8,128)(2,1)}, bf16[2,54,192,128]{3,2,1,0:T(8,128)(2,1)}, u32[]{:S(2)}, u32[]{:S(2)}) %collective-permute-start.3) | collective-permute-done | bytes 5308448 | tf_op jit(solution)/shard_map/ppermute | solution.py:922
  311.1 6.4 add_convert_fusion.earlier.also_earlier
  321.6 36.3 %cross_backward.2 = (bf16[512,768]{1,0:T(8,128)(2,1)}, bf16[8,768,768]{2,1,0:T(8,128)(2,1)}, bf16[8,768,768]{2,1,0:T(8,128)(2,1)}, f32[8,768]{1,0:T(8,128)}) custom-call(s32[26]{0:T(128)} %concatenate.77.info.info_own, bf16[512,768]{1,0:T(8,128)(2,1)} %get-tuple-element.49.query, bf16[560,768]{1,0:T(8,128)(2,1)} %get-tuple-element.55.packed, ...), custom_call_target="tpu_custom_call" | custom-call | flops 40000000000 | bytes 1048576 | tf_op jit(solution)/shard_map/cross_backward/pallas_call | solution.py:715
  362.2 34.6 %cross_backward.3 = (bf16[512,768]{1,0:T(8,128)(2,1)}, bf16[8,768,768]{2,1,0:T(8,128)(2,1)}, bf16[8,768,768]{2,1,0:T(8,128)(2,1)}, f32[8,768]{1,0:T(8,128)}) custom-call(s32[26]{0:T(128)} %concatenate.85.info.info_far, bf16[512,768]{1,0:T(8,128)(2,1)} %copy-done.25, bf16[560,768]{1,0:T(8,128)(2,1)} %collective-permute-done.4.packed, ...), custom_call_target="tpu_custom_call" | custom-call | flops 40000000000 | bytes 1048576 | tf_op jit(solution)/shard_map/cross_backward/pallas_call | solution.py:715
  396.8 3.6 collective-permute-start.6
  405.5 32.6 %table_gradient.1 = (bf16[2,12,192,128]{3,2,1,0:T(8,128)(2,1)}, bf16[2,12,192,128]{3,2,1,0:T(8,128)(2,1)}) custom-call(s32[26]{0:T(128)} %concatenate.77.info.info_own, s32[26]{0:T(128)} %concatenate.85.info.info_far, s32[1]{0:T(128)} %bitcast.me, bf16[8,768,768]{2,1,0:T(8,128)(2,1)} %get-tuple-element.60.key_own, ...), custom_call_target="tpu_custom_call" | custom-call | flops 20000000000 | bytes 1048576 | tf_op jit(solution)/shard_map/table_gradient/pallas_call | solution.py:752
  441.0 9.5 %cross_back.1 = (f32[512,768]{1,0:T(8,128)}, bf16[512,768]{1,0:T(8,128)(2,1)}, f32[8,768]{1,0:T(8,128)}, bf16[2,12,192,128]{3,2,1,0:T(8,128)(2,1)}, bf16[2,12,192,128]{3,2,1,0:T(8,128)(2,1)}) custom-call(s32[384]{0:T(512)} %add.250.where, s32[1]{0:T(128)} %bitcast.me, f32[512,768]{1,0:T(8,128)} %get-tuple-element.48.sum_one, ...), custom_call_target="tpu_custom_call" | custom-call | flops 8000000000 | bytes 1048576 | tf_op jit(solution)/shard_map/cross_back/pallas_call | solution.py:807
  452.2 4.5 collective-permute-done.9
  459.0 22.8 %last.1 = (f32[512,768]{1,0:T(8,128)}, f32[8,768]{1,0:T(8,128)}, bf16[2,18,192,128]{3,2,1,0:T(8,128)(2,1)}, bf16[2,18,192,128]{3,2,1,0:T(8,128)(2,1)}) custom-call(s32[384]{0:T(512)} %add.250.where, s32[1]{0:T(128)} %bitcast.me, bf16[512,768]{1,0:T(8,128)(2,1)} %tokens.3, f32[512,768]{1,0:T(8,128)} %get-tuple-element.65.grad_one, ...), custom_call_target="tpu_custom_call" | custom-call | flops 20000000000 | bytes 1048576 | tf_op jit(solution)/shard_map/last/pallas_call | solution.py:827
  488.7 23.5 %collective-permute-done.14 = bf16[24,192,128]{2,1,0:T(8,128)(2,1)} collective-permute-done((bf16[24,192,128]{2,1,0:T(8,128)(2,1)}, bf16[24,192,128]{2,1,0:T(8,128)(2,1)}, u32[]{:S(2)}, u32[]{:S(2)}) %collective-permute-start.14) | collective-permute-done | bytes 1179680 | tf_op jit(solution)/shard_map/ppermute | solution.py:922
  514.2 16.4 %collective-permute-done.16 = bf16[18,192,128]{2,1,0:T(8,128)(2,1)} collective-permute-done((bf16[18,192,128]{2,1,0:T(8,128)(2,1)}, bf16[18,192,128]{2,1,0:T(8,128)(2,1)}, u32[]{:S(2)}, u32[]{:S(2)}) %collective-permute-start.16) | collective-permute-done | bytes 884768 | tf_op jit(solution)/shard_map/ppermute | solution.py:922
  534.7 23.2 %collective-permute-done.17 = bf16[4032,128]{1,0:T(8,128)(2,1)} collective-permute-done((bf16[4032,128]{1,0:T(8,128)(2,1)}, bf16[4032,128]{1,0:T(8,128)(2,1)}, u32[]{:S(2)}, u32[]{:S(2)}) %collective-permute-start.17) | collective-permute-done | bytes 1032224 | tf_op jit(solution)/shard_map/ppermute | solution.py:927
  560.9 18.3 %collective-permute-done.18 = bf16[2016,128]{1,0:T(8,128)(2,1)S(1)} collective-permute-done((bf16[2016,128]{1,0:T(8,128)(2,1)S(1)}, bf16[2016,128]{1,0:T(8,128)(2,1)S(1)}, u32[]{:S(2)}, u32[]{:S(2)}) %collective-permute-start.18) | collective-permute-done | bytes 516128 | tf_op jit(solution)/shard_map/ppermute | solution.py:927
  580.0 10.0 %collective-permute-done.19 = bf16[1008,128]{1,0:T(8,128)(2,1)S(1)} collective-permute-done((bf16[1008,128]{1,0:T(8,128)(2,1)S(1)}, bf16[1008,128]{1,0:T(8,128)(2,1)S(1)}, u32[]{:S(2)}, u32[]{:S(2)}) %collective-permute-start.19) | collective-permute-done | bytes 258080 | tf_op jit(solution)/shard_map/ppermute | solution.py:927
  591.5 3.1 collective-permute-done.24
  594.6 2.7 collective-permute-start.25
  598.1 7.7 %collective-permute-done.25 = f32[24,768]{1,0:T(8,128)S(1)} collective-permute-done((f32[24,768]{1,0:T(8,128)S(1)}, f32[24,768]{1,0:T(8,128)S(1)}, u32[]{:S(2)}, u32[]{:S(2)}) %collective-permute-start.25) | collective-permute-done | bytes 73760 | tf_op jit(solution)/shard_map/ppermute | solution.py:927
  612.6 6.6 %collective-permute-done.21 = bf16[2016,128]{1,0:T(8,128)(2,1)S(1)} collective-permute-done((bf16[2016,128]{1,0:T(8,128)(2,1)S(1)}, bf16[2016,128]{1,0:T(8,128)(2,1)S(1)}, u32[]{:S(2)}, u32[]{:S(2)}) %collective-permute-start.21) | collective-permute-done | bytes 516128 | tf_op jit(solution)/shard_map/ppermute | solution.py:927
  624.7 15.2 %collective-permute-done.27.got = bf16[16,192,128]{2,1,0:T(8,128)(2,1)S(1)} collective-permute-done((bf16[16,192,128]{2,1,0:T(8,128)(2,1)}, bf16[16,192,128]{2,1,0:T(8,128)(2,1)S(1)}, u32[]{:S(2)}, u32[]{:S(2)}) %collective-permute-start.27) | collective-permute-done | bytes 786464 | tf_op jit(solution)/shard_map/ppermute | solution.py:927
  640.7 8.4 %update.1 = (f32[16,192,128]{2,1,0:T(8,128)}, f32[16,192,128]{2,1,0:T(8,128)}, f32[16,192,128]{2,1,0:T(8,128)}, f32[16,192,128]{2,1,0:T(8,128)}) custom-call(s32[16]{0:T(128)} %get-tuple-element.95.place, s32[16]{0:T(128)} %fusion.22.source, bf16[5184,128]{1,0:T(8,128)(2,1)} %maximum_select_fusion.early, bf16[4032,128]{1,0:T(8,128)(2,1)} %maximum_select_fusion.1.late, ...), custom_call_target="tpu_custom_call" | custom-call | flops 6000000000 | bytes 1048576 | tf_op jit(solution)/shard_map/update/pallas_call | solution.py:865
  (184 shorter events, 74.3 us)
Async XLA Ops:
  7.2 161.6 %all-gather.3.cloned.1.call-start = ((), (), s32[]{:S(2)}) async-start(), calls=%async_computation | async-start | bytes 25952256 | tf_op jit(solution)/shard_map/all_gather | solution.py:984
  34.8 25.3 %collective-permute-start = (bf16[16,384,768]{2,1,0:T(8,128)(2,1)}, bf16[16,384,768]{2,1,0:T(8,128)(2,1)}, u32[]{:S(2)}, u32[]{:S(2)}) collective-permute-start(bf16[16,384,768]{2,1,0:T(8,128)(2,1)} %fusion.5), channel_id=1, source_target_pairs={{0,1},{1,0},{2,3},{3,2},{4,5},{5,4},{6,7},{7,6},{8,9},{9,8},{10,11... | collective-permute-start | bytes 28311560 | tf_op jit(solution)/shard_map/ppermute | solution.py:922
  184.7 33.7 %collective-permute-start.1 = (bf16[512,768]{1,0:T(8,128)(2,1)}, bf16[512,768]{1,0:T(8,128)(2,1)S(1)}, u32[]{:S(2)}, u32[]{:S(2)}) collective-permute-start(bf16[512,768]{1,0:T(8,128)(2,1)} %get-tuple-element.49.query), channel_id=1, source_target_pairs={{0,2},{1,3},{2,0},{3,1},{4,6},{5,7},{6,4},{7,5},{8,10},{9,11},{10,... | collective-permute-start | bytes 2359304 | tf_op jit(solution)/shard_map/ppermute | solution.py:922
  242.2 24.4 %collective-permute-start.2 = (bf16[544,768]{1,0:T(8,128)(2,1)}, bf16[544,768]{1,0:T(8,128)(2,1)S(1)}, u32[]{:S(2)}, u32[]{:S(2)}) collective-permute-start(bf16[544,768]{1,0:T(8,128)(2,1)} %cross_forward.3), channel_id=1, source_target_pairs={{0,2},{1,3},{2,0},{3,1},{4,6},{5,7},{6,4},{7,5},{8,10},{9,11},{10,... | collective-permute-start | bytes 2506760 | tf_op jit(solution)/shard_map/ppermute | solution.py:922
  302.0 9.2 %collective-permute-start.3 = (bf16[2,54,192,128]{3,2,1,0:T(8,128)(2,1)}, bf16[2,54,192,128]{3,2,1,0:T(8,128)(2,1)}, u32[]{:S(2)}, u32[]{:S(2)}) collective-permute-start(bf16[2,54,192,128]{3,2,1,0:T(8,128)(2,1)} %get-tuple-element.57), channel_id=1, source_target_pairs={{0,1},{1,0},{2,3},{3,2},{4,5},{5,4},{6,7},{7,6},{8,9},{9,8},{10,11... | collective-permute-start | bytes 15925256 | tf_op jit(solution)/shard_map/ppermute | solution.py:922
  302.1 60.1 %collective-permute-start.4 = (bf16[560,768]{1,0:T(8,128)(2,1)}, bf16[560,768]{1,0:T(8,128)(2,1)}, u32[]{:S(2)}, u32[]{:S(2)}) collective-permute-start(bf16[560,768]{1,0:T(8,128)(2,1)} %get-tuple-element.55.packed), channel_id=1, source_target_pairs={{0,2},{1,3},{2,0},{3,1},{4,6},{5,7},{6,4},{7,5},{8,10},{9,11},{10,... | collective-permute-start | bytes 2580488 | tf_op jit(solution)/shard_map/ppermute | solution.py:922
  320.8 38.8 %collective-permute-start.5 = (bf16[18,192,128]{2,1,0:T(8,128)(2,1)}, bf16[18,192,128]{2,1,0:T(8,128)(2,1)}, u32[]{:S(2)}, u32[]{:S(2)}) collective-permute-start(bf16[18,192,128]{2,1,0:T(8,128)(2,1)} %slice_bitcast_fusion.6), channel_id=1, source_target_pairs={{0,2},{1,3},{2,0},{3,1},{4,6},{5,7},{6,4},{7,5},{8,10},{9,11},{10,... | collective-permute-start | bytes 2654216 | tf_op jit(solution)/shard_map/ppermute | solution.py:922
  359.5 40.9 %collective-permute-start.7 = (bf16[36,192,128]{2,1,0:T(8,128)(2,1)S(1)}, bf16[36,192,128]{2,1,0:T(8,128)(2,1)S(1)}, u32[]{:S(2)}, u32[]{:S(2)}) collective-permute-start(bf16[36,192,128]{2,1,0:T(8,128)(2,1)S(1)} %slice_bitcast_fusion), channel_id=1, source_target_pairs={{0,2},{1,3},{2,0},{3,1},{4,6},{5,7},{6,4},{7,5},{8,10},{9,11},{10,... | collective-permute-start | bytes 5308424 | tf_op jit(solution)/shard_map/ppermute | solution.py:922
  396.8 44.1 %collective-permute-start.6 = (bf16[512,768]{1,0:T(8,128)(2,1)}, bf16[512,768]{1,0:T(8,128)(2,1)}, u32[]{:S(2)}, u32[]{:S(2)}) collective-permute-start(bf16[512,768]{1,0:T(8,128)(2,1)} %get-tuple-element.59), channel_id=1, source_target_pairs={{0,2},{1,3},{2,0},{3,1},{4,6},{5,7},{6,4},{7,5},{8,10},{9,11},{10,... | collective-permute-start | bytes 2359304 | tf_op jit(solution)/shard_map/ppermute | solution.py:922
  405.5 32.7 %collective-permute-start.8 = (bf16[5184,128]{1,0:T(8,128)(2,1)S(1)}, bf16[5184,128]{1,0:T(8,128)(2,1)}, u32[]{:S(2)}, u32[]{:S(2)}) collective-permute-start(bf16[5184,128]{1,0:T(8,128)(2,1)S(1)} %constant_dynamic-slice_fusion.5), channel_id=1, source_target_pairs={{0,4},{4,0},{8,12},{12,8},{16,20},{20,16},{24,28},{28,24},{1,5},{5... | collective-permute-start | bytes 3981320 | tf_op jit(solution)/shard_map/ppermute | solution.py:927
  452.1 4.6 collective-permute-start.9
  481.8 4.0 collective-permute-start.15
  483.1 29.1 %collective-permute-start.14 = (bf16[24,192,128]{2,1,0:T(8,128)(2,1)}, bf16[24,192,128]{2,1,0:T(8,128)(2,1)}, u32[]{:S(2)}, u32[]{:S(2)}) collective-permute-start(bf16[24,192,128]{2,1,0:T(8,128)(2,1)} %slice_bitcast_fusion.2), channel_id=1, source_target_pairs={{0,2},{1,3},{2,0},{3,1},{4,6},{5,7},{6,4},{7,5},{8,10},{9,11},{10,... | collective-permute-start | bytes 3538952 | tf_op jit(solution)/shard_map/ppermute | solution.py:922
  487.4 43.2 %collective-permute-start.16 = (bf16[18,192,128]{2,1,0:T(8,128)(2,1)}, bf16[18,192,128]{2,1,0:T(8,128)(2,1)}, u32[]{:S(2)}, u32[]{:S(2)}) collective-permute-start(bf16[18,192,128]{2,1,0:T(8,128)(2,1)} %slice_bitcast_fusion.4), channel_id=1, source_target_pairs={{0,2},{1,3},{2,0},{3,1},{4,6},{5,7},{6,4},{7,5},{8,10},{9,11},{10,... | collective-permute-start | bytes 2654216 | tf_op jit(solution)/shard_map/ppermute | solution.py:922
  488.7 44.5 %collective-permute-start.10 = (bf16[2592,128]{1,0:T(8,128)(2,1)}, bf16[2592,128]{1,0:T(8,128)(2,1)}, u32[]{:S(2)}, u32[]{:S(2)}) collective-permute-start(bf16[2592,128]{1,0:T(8,128)(2,1)} %constant_dynamic-slice_fusion.4), channel_id=1, source_target_pairs={{0,8},{4,12},{8,0},{12,4},{16,24},{20,28},{24,16},{28,20},{1,9},{5... | collective-permute-start | bytes 1990664 | tf_op jit(solution)/shard_map/ppermute | solution.py:927
  533.3 24.6 %collective-permute-start.17 = (bf16[4032,128]{1,0:T(8,128)(2,1)}, bf16[4032,128]{1,0:T(8,128)(2,1)}, u32[]{:S(2)}, u32[]{:S(2)}) collective-permute-start(bf16[4032,128]{1,0:T(8,128)(2,1)} %constant_dynamic-slice_fusion.2), channel_id=1, source_target_pairs={{0,4},{4,0},{8,12},{12,8},{16,20},{20,16},{24,28},{28,24},{1,5},{5... | collective-permute-start | bytes 3096584 | tf_op jit(solution)/shard_map/ppermute | solution.py:927
  534.6 25.6 %collective-permute-start.11 = (bf16[1296,128]{1,0:T(8,128)(2,1)S(1)}, bf16[1296,128]{1,0:T(8,128)(2,1)S(1)}, u32[]{:S(2)}, u32[]{:S(2)}) collective-permute-start(bf16[1296,128]{1,0:T(8,128)(2,1)S(1)} %constant_dynamic-slice_fusion.3), channel_id=1, source_target_pairs={{0,16},{4,20},{8,24},{12,28},{16,0},{20,4},{24,8},{28,12},{1,17},{... | collective-permute-start | bytes 995336 | tf_op jit(solution)/shard_map/ppermute | solution.py:927
  559.4 19.8 %collective-permute-start.18 = (bf16[2016,128]{1,0:T(8,128)(2,1)S(1)}, bf16[2016,128]{1,0:T(8,128)(2,1)S(1)}, u32[]{:S(2)}, u32[]{:S(2)}) collective-permute-start(bf16[2016,128]{1,0:T(8,128)(2,1)S(1)} %constant_dynamic-slice_fusion.1), channel_id=1, source_target_pairs={{0,8},{4,12},{8,0},{12,4},{16,24},{20,28},{24,16},{28,20},{1,9},{5... | collective-permute-start | bytes 1548296 | tf_op jit(solution)/shard_map/ppermute | solution.py:927
  560.3 19.1 %collective-permute-start.12 = (bf16[1296,128]{1,0:T(8,128)(2,1)S(1)}, bf16[1296,128]{1,0:T(8,128)(2,1)S(1)}, u32[]{:S(2)}, u32[]{:S(2)}) collective-permute-start(bf16[1296,128]{1,0:T(8,128)(2,1)S(1)} %add_convert_fusion.7), channel_id=1, source_target_pairs={{0,16},{4,20},{8,24},{12,28},{16,0},{20,4},{24,8},{28,12},{1,17},{... | collective-permute-start | bytes 995336 | tf_op jit(solution)/shard_map/ppermute | solution.py:927
  560.8 36.5 %copy-start.21 = (s32[96]{0:T(128)S(1)}, s32[96]{0:T(128)}, u32[]{:S(2)}) copy-start(s32[96]{0:T(128)} %param.19) | copy-start | bytes 1156
  560.8 36.5 %copy-start.22 = (s32[96]{0:T(128)S(1)}, s32[96]{0:T(128)}, u32[]{:S(2)}) copy-start(s32[96]{0:T(128)} %constant.290.clone) | copy-start | bytes 1156
  560.8 36.5 %copy-start.23 = (s32[96]{0:T(128)S(1)}, s32[96]{0:T(128)}, u32[]{:S(2)}) copy-start(s32[96]{0:T(128)} %constant.289.clone) | copy-start | bytes 1156
  560.9 18.9 %collective-permute-start.22 = (f32[24,768]{1,0:T(8,128)S(1)}, f32[24,768]{1,0:T(8,128)S(1)}, u32[]{:S(2)}, u32[]{:S(2)}) collective-permute-start(f32[24,768]{1,0:T(8,128)S(1)} %concatenate.98), channel_id=1, source_target_pairs={{0,1},{1,0},{2,3},{3,2},{4,5},{5,4},{6,7},{7,6},{8,9},{9,8},{10,11... | collective-permute-start | bytes 221192 | tf_op jit(solution)/shard_map/ppermute | solution.py:922
  579.4 10.6 %collective-permute-start.19 = (bf16[1008,128]{1,0:T(8,128)(2,1)S(1)}, bf16[1008,128]{1,0:T(8,128)(2,1)S(1)}, u32[]{:S(2)}, u32[]{:S(2)}) collective-permute-start(bf16[1008,128]{1,0:T(8,128)(2,1)S(1)} %constant_dynamic-slice_fusion), channel_id=1, source_target_pairs={{0,16},{4,20},{8,24},{12,28},{16,0},{20,4},{24,8},{28,12},{1,17},{... | collective-permute-start | bytes 774152 | tf_op jit(solution)/shard_map/ppermute | solution.py:927
  579.7 29.5 %collective-permute-start.13 = (bf16[2592,128]{1,0:T(8,128)(2,1)S(1)}, bf16[2592,128]{1,0:T(8,128)(2,1)S(1)}, u32[]{:S(2)}, u32[]{:S(2)}) collective-permute-start(bf16[2592,128]{1,0:T(8,128)(2,1)S(1)} %maximum_select_fusion.2), channel_id=1, source_target_pairs={{0,8},{4,12},{8,0},{12,4},{16,24},{20,28},{24,16},{28,20},{1,9},{5... | collective-permute-start | bytes 1990664 | tf_op jit(solution)/shard_map/ppermute | solution.py:927
  579.8 10.4 %collective-permute-start.23 = (f32[24,768]{1,0:T(8,128)S(1)}, f32[24,768]{1,0:T(8,128)S(1)}, u32[]{:S(2)}, u32[]{:S(2)}) collective-permute-start(f32[24,768]{1,0:T(8,128)S(1)} %add.288), channel_id=1, source_target_pairs={{0,2},{1,3},{2,0},{3,1},{4,6},{5,7},{6,4},{7,5},{8,10},{9,11},{10,... | collective-permute-start | bytes 221192 | tf_op jit(solution)/shard_map/ppermute | solution.py:922
  590.1 16.5 %collective-permute-start.20 = (bf16[1008,128]{1,0:T(8,128)(2,1)S(1)}, bf16[1008,128]{1,0:T(8,128)(2,1)S(1)}, u32[]{:S(2)}, u32[]{:S(2)}) collective-permute-start(bf16[1008,128]{1,0:T(8,128)(2,1)S(1)} %add_convert_fusion.8), channel_id=1, source_target_pairs={{0,16},{4,20},{8,24},{12,28},{16,0},{20,4},{24,8},{28,12},{1,17},{... | collective-permute-start | bytes 774152 | tf_op jit(solution)/shard_map/ppermute | solution.py:927
  590.2 4.4 collective-permute-start.24
  594.6 11.1 %collective-permute-start.25 = (f32[24,768]{1,0:T(8,128)S(1)}, f32[24,768]{1,0:T(8,128)S(1)}, u32[]{:S(2)}, u32[]{:S(2)}) collective-permute-start(f32[24,768]{1,0:T(8,128)S(1)} %add.290), channel_id=1, source_target_pairs={{0,8},{4,12},{8,0},{12,4},{16,24},{20,28},{24,16},{28,20},{1,9},{5... | collective-permute-start | bytes 221192 | tf_op jit(solution)/shard_map/ppermute | solution.py:927
  605.7 6.1 collective-permute-start.26
  606.7 12.5 %collective-permute-start.21 = (bf16[2016,128]{1,0:T(8,128)(2,1)S(1)}, bf16[2016,128]{1,0:T(8,128)(2,1)S(1)}, u32[]{:S(2)}, u32[]{:S(2)}) collective-permute-start(bf16[2016,128]{1,0:T(8,128)(2,1)S(1)} %maximum_select_fusion.3), channel_id=1, source_target_pairs={{0,8},{4,12},{8,0},{12,4},{16,24},{20,28},{24,16},{28,20},{1,9},{5... | collective-permute-start | bytes 1548296 | tf_op jit(solution)/shard_map/ppermute | solution.py:927
  623.2 16.6 %collective-permute-start.27 = (bf16[16,192,128]{2,1,0:T(8,128)(2,1)}, bf16[16,192,128]{2,1,0:T(8,128)(2,1)S(1)}, u32[]{:S(2)}, u32[]{:S(2)}) collective-permute-start(bf16[16,192,128]{2,1,0:T(8,128)(2,1)} %pick.1), channel_id=1, source_target_pairs={{0,4},{4,0},{8,12},{12,8},{16,20},{20,16},{24,28},{28,24},{1,5},{5... | collective-permute-start | bytes 2359304 | tf_op jit(solution)/shard_map/ppermute | solution.py:927
  (24 other events, 281.0 us)
Sparse Core Ops, SparseCore 0:
  11.4 157.3 all-gather.2

commit v3 on v2

--- a/solution.py
+++ b/solution.py
@@ -45,6 +45,10 @@
     return lax.dot_general(a, b, (((1,), (0,)), ((), ())), preferred_element_type=F32)
 
 
+def dot_tn(a, b):
+    return lax.dot_general(a, b, (((0,), (0,)), ((), ())), preferred_element_type=F32)
+
+
 def eye():
     return (
         lax.broadcasted_iota(jnp.int32, (WIDE, WIDE), 0)
@@ -98,18 +102,33 @@
     return jnp.sum(x, axis=0, keepdims=True)
 
 
-def matrix_copies(tiles, where, matrix, target, sem):
-    copies = []
+def matrix_start(tiles, where, matrix, target, sem):
+    def start(source, base, r):
+        for f in range(4):
+            pltpu.make_async_copy(
+                source.at[where[(matrix * ROWS + r) * 4 + f] - base],
+                target.at[pl.ds(f * 192, 192), pl.ds(r * PANEL, PANEL)],
+                sem,
+            ).start()
+
+    count = tiles[0].shape[0]
+    for r in range(ROWS):
+        if len(tiles) == 1:
+            start(tiles[0], 0, r)
+            continue
+        near = where[(matrix * ROWS + r) * 4] < count
+        pl.when(near)(functools.partial(start, tiles[0], 0, r))
+        pl.when(jnp.logical_not(near))(functools.partial(start, tiles[1], count, r))
+
+
+def matrix_wait(tiles, target, sem):
     for r in range(ROWS):
         for f in range(4):
-            copies.append(
-                pltpu.make_async_copy(
-                    tiles.at[where[(matrix * ROWS + r) * 4 + f]],
-                    target.at[pl.ds(f * 192, 192), pl.ds(r * PANEL, PANEL)],
-                    sem,
-                )
-            )
-    return copies
+            pltpu.make_async_copy(
+                tiles[0].at[0],
+                target.at[pl.ds(f * 192, 192), pl.ds(r * PANEL, PANEL)],
+                sem,
+            ).wait()
 
 
 def gradient_copies(staged, keep, send, slot, me, sem):
@@ -154,21 +173,18 @@
     sum_one, cross_query, query, key, value, attended, lse,
     weights, bias, sems,
 ):
-    loads = [
-        matrix_copies(tiles, where, i, weights.at[i], sems.at[i]) for i in range(5)
-    ]
-    for load in loads:
-        start_all(load)
+    for i in range(5):
+        matrix_start([tiles], where, i, weights.at[i], sems.at[i])
     unit = eye()
     count = tokens.shape[0]
     bias[...] = seen_bias(count, member_column, live_column, member_row)
     x = tokens[...].astype(F32)
     a = (norm_parts(x)[0] * vectors[0:1] + vectors[1:2]).astype(BF)
-    wait_all(loads[0])
+    matrix_wait([tiles], weights.at[0], sems.at[0])
     query[...] = (SCALE * (dot_nt(a, weights[0]) + vectors[2:3])).astype(BF)
-    wait_all(loads[1])
+    matrix_wait([tiles], weights.at[1], sems.at[1])
     key[...] = dot_nt(a, weights[1]).astype(BF)
-    wait_all(loads[2])
+    matrix_wait([tiles], weights.at[2], sems.at[2])
     value[...] = (dot_nt(a, weights[2]) + vectors[3:4]).astype(BF)
     lanes = lax.broadcasted_iota(jnp.int32, (1, WIDE), 1) >> 6
     lse[...] = jnp.zeros_like(lse)
@@ -187,11 +203,11 @@
             outs.append((out * (1.0 / total)).astype(BF))
             lse[g * 4 + h : g * 4 + h + 1] = top + jnp.log(total)
         attended[:, cols] = turned(jnp.concatenate(outs, axis=0), unit)
-    wait_all(loads[3])
+    matrix_wait([tiles], weights.at[3], sems.at[3])
     h1 = x + (dot_nt(attended[...], weights[3]) + vectors[4:5])
     sum_one[...] = h1
     c = (norm_parts(h1)[0] * vectors[5:6] + vectors[6:7]).astype(BF)
-    wait_all(loads[4])
+    matrix_wait([tiles], weights.at[4], sems.at[4])
     cross_query[...] = (SCALE * (dot_nt(c, weights[4]) + vectors[7:8])).astype(BF)
 
 
@@ -200,13 +216,10 @@
 
     @pl.when(step == 0)
     def _():
-        loads = [
-            matrix_copies(tiles, where, 5 + i, weights.at[i], sems.at[i]) for i in range(2)
-        ]
-        for load in loads:
-            start_all(load)
-        for load in loads:
-            wait_all(load)
+        for i in range(2):
+            matrix_start([tiles], where, 5 + i, weights.at[i], sems.at[i])
+        for i in range(2):
+            matrix_wait([tiles], weights.at[i], sems.at[i])
 
     @pl.when(step < act[0])
     def _():
@@ -225,16 +238,21 @@
     return jnp.concatenate(parts, axis=0)
 
 
-def each_unit(info, body):
+def units_of(info):
     step = pl.program_id(0)
-    first, mine = info[10 + step], info[18 + step]
-    rest = jnp.where(step == 0, 8 - info[1], 0)
+    first, mine, used = info[10 + step], info[18 + step], info[1]
+    rest = jnp.where(step == 0, 8 - used, 0)
+    return first, (mine + rest - 1, lambda j: jnp.where(j + 1 < mine, first + j + 1, used + j + 1 - mine))
+
+
+def each_unit(units, body):
+    count, place = units
 
     def one(j, state):
-        body(jnp.where(j < mine, first + j, info[1] + j - mine))
+        body(place(j))
         return state
 
-    lax.fori_loop(0, mine + rest, one, 0)
+    lax.fori_loop(0, count, one, 0)
 
 
 def spread_heads(x, mask):
@@ -265,7 +283,9 @@
                 out[rows, cols] = dot_nt(pick, o).astype(BF)
                 lse[pl.ds(u, 1), cols] = top + jnp.log(total)
 
-        each_unit(info, body)
+        first, others = units_of(info)
+        body(first)
+        each_unit(others, body)
 
     @pl.when(step == pl.num_programs(0) - 1)
     def _():
@@ -294,10 +314,8 @@
         for g in range(GROUPS):
             cols = pl.ds(g * WIDE, WIDE)
             key_turned[g] = turned(key_table[0, :, cols], unit)
-        key_sum[...] = jnp.zeros_like(key_sum)
-        value_sum[...] = jnp.zeros_like(value_sum)
-
-        def body(u):
+
+        def body(u, first):
             rows = pl.ds(pl.multiple_of(u * BLOCK, BLOCK), BLOCK)
             for g in range(GROUPS):
                 cols = pl.ds(g * WIDE, WIDE)
@@ -307,18 +325,23 @@
                 p = pad_rows(jnp.exp(scores - lse[pl.ds(u, 1), cols]), 0.0)
                 dp = dot_nt(value_table[0, :, cols], wide_o)
                 ds = (p * (dp - delta[pl.ds(u, 1), cols])).astype(BF)
-                value_sum[:, cols] += dot_nn(p.astype(BF), wide_o)
-                key_sum[:, cols] += dot_nn(ds, wide_q)
+                part = dot_nn(p.astype(BF), wide_o)
+                value_sum[:, cols] = part if first else value_sum[:, cols] + part
+                part = dot_nn(ds, wide_q)
+                key_sum[:, cols] = part if first else key_sum[:, cols] + part
                 dq = jnp.where(mask, dot_nn(key_turned[g], ds), 0.0).astype(BF)
                 grad_query[rows, cols] = dot_nt(pick, dq).astype(BF)
 
-        each_unit(info, body)
+        first, others = units_of(info)
+        body(first, True)
+        each_unit(others, lambda u: body(u, False))
+        ones = jnp.ones((8, key_sum.shape[0]), BF)
         for g in range(GROUPS):
             cols = pl.ds(g * WIDE, WIDE)
             low = value_sum[:, cols].astype(BF)
-            bias_grad[0:1, cols] += column_sum(low.astype(F32))
-            key_out[0, cols, :] = turned(key_sum[:, cols].astype(BF), unit)
-            value_out[0, cols, :] = turned(low, unit)
+            bias_grad[:, cols] += dot_nn(ones, low)
+            key_out[0, :, cols] = key_sum[:, cols].astype(BF)
+            value_out[0, :, cols] = low
 
 
 def table_gradient_kernel(
@@ -341,8 +364,8 @@
         @pl.when(step < info[0])
         def _():
             f = frames[0]
-            grad_key[...] += dot_nn(key[0], f)
-            grad_value[...] += dot_nn(value[0], f)
+            grad_key[...] += dot_tn(key[0], f)
+            grad_value[...] += dot_tn(value[0], f)
 
     @pl.when(step == pl.num_programs(0) - 1)
     def _():
@@ -356,16 +379,20 @@
 
 
 def middle_kernel(
+    part_count, where, me, sum_one, own, other, vectors, live, cotangent, *refs,
+):
+    tiles, refs = refs[:part_count], refs[part_count:]
+    middle_rows(where, me, sum_one, own, other, vectors, live, cotangent, tiles, *refs)
+
+
+def middle_rows(
     where, me, sum_one, own, other, vectors, live, cotangent, tiles,
     out_tokens, grad_two, packed, vector_grads, keep, send,
-    weights, hidden, act, staged, third, merged, sems, out_sem,
+    weights, slope, act, staged, third, merged, sems, out_sem,
 ):
     count = sum_one.shape[0]
-    loads = {
-        m: matrix_copies(tiles, where, m, weights.at[m - 7], sems.at[m - 7]) for m in range(7, 16)
-    }
-    for load in loads.values():
-        start_all(load)
+    for m in range(9):
+        matrix_start(tiles, where, 7 + m, weights.at[m], sems.at[m])
     unit, mask, pick = eye(), head_mask(), row_pick()
     lse_own = own[512:536].astype(F32)
     lse_other = other[512:536].astype(F32)
@@ -391,19 +418,20 @@
             first, second = own[rows, cols].astype(F32), other[rows, cols].astype(F32)
             merged[rows, cols] = second + factor * (first - second)
     cross_out = merged[...].astype(BF)
-    wait_all(loads[7])
+    matrix_wait(tiles, weights.at[0], sems.at[0])
     h2 = sum_one[...] + (dot_nt(cross_out, weights[0]) + vectors[9:10])
     unit_three, inverse_three = norm_parts(h2)
     m = (unit_three * vectors[10:11] + vectors[11:12]).astype(BF)
     third[...] = h2 + vectors[16:17]
     for c in range(4):
-        wait_all(loads[8 + c])
-        wait_all(loads[12 + c])
+        matrix_wait(tiles, weights.at[1 + c], sems.at[1 + c])
+        matrix_wait(tiles, weights.at[5 + c], sems.at[5 + c])
 
     def ahead(c, state):
         u = dot_nt(m, weights[1 + c]) + vectors[pl.ds(12 + c, 1)]
-        hidden[c] = u
-        g = (u * (0.5 * (1.0 + lax.erf(u * math.sqrt(0.5))))).astype(BF)
+        below = 0.5 * (1.0 + lax.erf(u * math.sqrt(0.5)))
+        slope[c] = below + u * (jnp.exp(-0.5 * u * u) * (1.0 / math.sqrt(2.0 * math.pi)))
+        g = (u * below).astype(BF)
         act[c] = g
         third[...] += dot_nt(g, weights[5 + c])
         return state
@@ -420,19 +448,14 @@
     third[...] = dh3
     e3 = dh3.astype(BF)
     vector_grads[7:8] = column_sum(e3.astype(F32))
-    e3_turned = turned(e3, unit)
     grad_two[...] = jnp.zeros_like(grad_two)
 
     def back(c, state):
-        staged[5 + c] = dot_nn(e3_turned, act[c]).astype(BF)
+        staged[5 + c] = dot_tn(e3, act[c]).astype(BF)
         start_all(gradient_copies(staged.at[5 + c], keep, send, 5 + c, me[0], out_sem))
-        u = hidden[c]
-        slope = 0.5 * (1.0 + lax.erf(u * math.sqrt(0.5))) + u * (
-            jnp.exp(-0.5 * u * u) * (1.0 / math.sqrt(2.0 * math.pi))
-        )
-        du = (dot_nn(e3, weights[5 + c]) * slope).astype(BF)
+        du = (dot_nn(e3, weights[5 + c]) * slope[c]).astype(BF)
         vector_grads[pl.ds(3 + c, 1)] = column_sum(du.astype(F32))
-        staged[1 + c] = dot_nn(turned(du, unit), m).astype(BF)
+        staged[1 + c] = dot_tn(du, m).astype(BF)
         start_all(gradient_copies(staged.at[1 + c], keep, send, 1 + c, me[0], out_sem))
         grad_two[...] += dot_nn(du, weights[1 + c])
         return state
@@ -445,7 +468,7 @@
     grad_two[...] = dh2
     e2 = dh2.astype(BF)
     vector_grads[0:1] = column_sum(e2.astype(F32))
-    staged[0] = dot_nn(turned(e2, unit), cross_out).astype(BF)
+    staged[0] = dot_tn(e2, cross_out).astype(BF)
     start_all(gradient_copies(staged.at[0], keep, send, 0, me[0], out_sem))
     packed[0:512] = dot_nn(e2, weights[0]).astype(BF)
     ones = jnp.ones((8, WIDE), BF)
@@ -467,13 +490,19 @@
 
 
 def cross_back_kernel(
-    where, me, sum_one, grad_two, attended, own, other, vectors, tiles, earlier, also_earlier,
+    part_count, where, me, sum_one, grad_two, attended, own, other, vectors, earlier, also_earlier, *refs,
+):
+    tiles, refs = refs[:part_count], refs[part_count:]
+    cross_back_rows(where, me, sum_one, grad_two, attended, own, other, vectors, tiles, *refs)
+
+
+def cross_back_rows(
+    where, me, sum_one, grad_two, attended, own, other, vectors, tiles,
     grad_one, grad_att, vector_grads, keep, send,
     weights, staged, sems, out_sem,
 ):
-    loads = [matrix_copies(tiles, where, m, weights.at[i], sems.at[i]) for i, m in enumerate((4, 3))]
-    for load in loads:
-        start_all(load)
+    for i, m in enumerate((4, 3)):
+        matrix_start(tiles, where, m, weights.at[i], sems.at[i])
     unit = eye()
 
     def put(slot, grad):
@@ -485,8 +514,8 @@
     vector_grads[3:4] = column_sum(ecq.astype(F32))
     unit_two, inverse_two = norm_parts(sum_one[...])
     c = (unit_two * vectors[5:6] + vectors[6:7]).astype(BF)
-    put(0, dot_nn(turned(ecq, unit), c))
-    wait_all(loads[0])
+    put(0, dot_tn(ecq, c))
+    matrix_wait(tiles, weights.at[0], sems.at[0])
     dc = dot_nn(ecq, weights[0])
     vector_grads[1:2] = column_sum(dc * unit_two)
     vector_grads[2:3] = column_sum(dc)
@@ -494,22 +523,32 @@
     grad_one[...] = dh1
     e1 = dh1.astype(BF)
     vector_grads[0:1] = column_sum(e1.astype(F32))
-    put(1, dot_nn(turned(e1, unit), attended[...]))
-    wait_all(loads[1])
+    put(1, dot_tn(e1, attended[...]))
+    matrix_wait(tiles, weights.at[1], sems.at[1])
     grad_att[...] = dot_nn(e1, weights[1]).astype(BF)
     for i in range(2):
         wait_all(gradient_copies(staged.at[i], keep, send, i, me[0], out_sem))
 
 
 def last_kernel(
+    part_count, where, me, tokens, grad_one, grad_att, query, key, value, lse, vectors,
+    member_column, live_column, member_row, earlier, *refs,
+):
+    tiles, refs = refs[:part_count], refs[part_count:]
+    last_rows(
+        where, me, tokens, grad_one, grad_att, query, key, value, lse, vectors,
+        member_column, live_column, member_row, tiles, *refs,
+    )
+
+
+def last_rows(
     where, me, tokens, grad_one, grad_att, query, key, value, lse, vectors,
-    member_column, live_column, member_row, tiles, earlier,
+    member_column, live_column, member_row, tiles,
     token_grads, vector_grads, keep, send,
     weights, staged, bias, grad_q, grad_q_turned, grad_k, grad_v, sems, out_sem,
 ):
-    loads = [matrix_copies(tiles, where, i, weights.at[i], sems.at[i]) for i in range(3)]
-    for load in loads:
-        start_all(load)
+    for i in range(3):
+        matrix_start(tiles, where, i, weights.at[i], sems.at[i])
     unit = eye()
     count = tokens.shape[0]
     bias[...] = seen_bias(count, member_column, live_column, member_row)
@@ -549,10 +588,10 @@
     vector_grads[2:3] = column_sum(grad_q[...].astype(F32))
     vector_grads[3:4] = column_sum(grad_v[...].astype(F32))
     put(0, dot_nn(grad_q_turned[...], a))
-    put(1, dot_nn(turned(grad_k[...], unit), a))
-    put(2, dot_nn(turned(grad_v[...], unit), a))
-    for load in loads:
-        wait_all(load)
+    put(1, dot_tn(grad_k[...], a))
+    put(2, dot_tn(grad_v[...], a))
+    for i in range(3):
+        matrix_wait(tiles, weights.at[i], sems.at[i])
     da = (
         dot_nn(grad_q[...], weights[0])
         + dot_nn(grad_k[...], weights[1])
@@ -711,13 +750,13 @@
     count, extent = query.shape[0], key_table.shape[1]
     slots = 8
     block = pl.BlockSpec((1, extent, D), lambda i, info: (base + info[2 + i], 0, 0))
-    block_out = pl.BlockSpec((1, D, extent), lambda i, info: (info[2 + i], 0, 0))
+    block_out = pl.BlockSpec((1, extent, D), lambda i, info: (info[2 + i], 0, 0))
     return pl.pallas_call(
         cross_backward_kernel,
         out_shape=(
             shape(count, D),
-            shape(slots, D, extent),
-            shape(slots, D, extent),
+            shape(slots, extent, D),
+            shape(slots, extent, D),
             shape(8, D, dtype=F32),
         ),
         grid_spec=pltpu.PrefetchScalarGridSpec(
@@ -747,7 +786,7 @@
 
     specs = []
     for part in range(2):
-        specs += [block(part, 0, D, extent)] * 2 + [block(part, part * slots, extent, D)]
+        specs += [block(part, 0, extent, D)] * 2 + [block(part, part * slots, extent, D)]
     part = shape(2, 2 * ROWS, 192, PANEL)
     return pl.pallas_call(
         table_gradient_kernel,
@@ -774,7 +813,7 @@
     count = sum_one.shape[0]
     part = shape(2, 9 * ROWS, 192, PANEL)
     return pl.pallas_call(
-        middle_kernel,
+        functools.partial(middle_kernel, len(tiles)),
         out_shape=(
             shape(count, D, dtype=F32),
             shape(count, D, dtype=F32),
@@ -783,7 +822,7 @@
             part,
             part,
         ),
-        in_specs=[SMEM, SMEM, WHOLE, WHOLE, WHOLE, WHOLE, WHOLE, WHOLE, AWAY],
+        in_specs=[SMEM, SMEM] + [WHOLE] * 6 + [AWAY] * len(tiles),
         out_specs=(WHOLE, WHOLE, WHOLE, WHOLE, AWAY, AWAY),
         scratch_shapes=[
             pltpu.VMEM((9, D, D), BF),
@@ -798,16 +837,16 @@
         compiler_params=PARAMS,
         cost_estimate=cost(34),
         name="middle",
-    )(where, me, sum_one, own, other, vectors, live, cotangent, tiles)
+    )(where, me, sum_one, own, other, vectors, live, cotangent, *tiles)
 
 
 def call_cross_back(where, me, sum_one, grad_two, attended, own, other, vectors, tiles, earlier):
     count = sum_one.shape[0]
     part = shape(2, 2 * ROWS, 192, PANEL)
     return pl.pallas_call(
-        cross_back_kernel,
+        functools.partial(cross_back_kernel, len(tiles)),
         out_shape=(shape(count, D, dtype=F32), shape(count, D), shape(8, D, dtype=F32), part, part),
-        in_specs=[SMEM, SMEM] + [WHOLE] * 6 + [AWAY] * 3,
+        in_specs=[SMEM, SMEM] + [WHOLE] * 6 + [AWAY] * (2 + len(tiles)),
         out_specs=(WHOLE, WHOLE, WHOLE, AWAY, AWAY),
         scratch_shapes=[
             pltpu.VMEM((2, D, D), BF),
@@ -818,16 +857,16 @@
         compiler_params=PARAMS,
         cost_estimate=cost(8),
         name="cross_back",
-    )(where, me, sum_one, grad_two, attended, own, other, vectors, tiles, *earlier)
+    )(where, me, sum_one, grad_two, attended, own, other, vectors, *earlier, *tiles)
 
 
 def call_last(where, me, tokens, grad_one, grad_att, saved, vectors, layout, tiles, earlier):
     count = tokens.shape[0]
     part = shape(2, 3 * ROWS, 192, PANEL)
     return pl.pallas_call(
-        last_kernel,
+        functools.partial(last_kernel, len(tiles)),
         out_shape=(shape(count, D, dtype=F32), shape(8, D, dtype=F32), part, part),
-        in_specs=[SMEM, SMEM] + [WHOLE] * 11 + [AWAY] * 2,
+        in_specs=[SMEM, SMEM] + [WHOLE] * 11 + [AWAY] * (1 + len(tiles)),
         out_specs=(WHOLE, WHOLE, AWAY, AWAY),
         scratch_shapes=[
             pltpu.VMEM((3, D, D), BF),
@@ -843,7 +882,7 @@
         compiler_params=PARAMS,
         cost_estimate=cost(20),
         name="last",
-    )(where, me, tokens, grad_one, grad_att, *saved, vectors, *layout, tiles, earlier)
+    )(where, me, tokens, grad_one, grad_att, *saved, vectors, *layout, earlier, *tiles)
 
 
 def call_pick(place, early, late, earlier):
@@ -967,7 +1006,38 @@
     return x
 
 
-def body(
+CAP, FIRST = 16, 10
+NEEDED = (5, 6, 0, 1, 2, 3, 4, *range(7, 16))
+SOON = 7 * ROWS
+
+
+def body(*args):
+    slot_of, master = args[5], args[6]
+    cap = master.shape[0]
+    owner = slot_of // cap
+    need = [NEEDED.index(p // ROWS) * ROWS + p % ROWS for p in range(slot_of.shape[0])]
+    need = jnp.asarray(need, jnp.int32)
+    rank = jnp.sum(
+        (owner[:, None] == owner[None, :]) & (need[None, :] < need[:, None]), axis=1, dtype=jnp.int32
+    )
+    here = (owner == lax.axis_index("dp"))[None, :] & (
+        rank[None, :] == jnp.arange(cap, dtype=jnp.int32)[:, None]
+    )
+    order = jnp.sum(jnp.where(here, (slot_of % cap)[None, :], 0), axis=1, dtype=jnp.int32)
+    ordered = master.transpose(0, 2, 1)[order].astype(BF)
+    if cap != CAP:
+        return steps(cap, owner, rank, ordered, *args)
+    soon = jnp.max(jnp.where(need < SOON, rank, 0)) < FIRST
+    return lax.cond(
+        soon,
+        functools.partial(steps, FIRST),
+        functools.partial(steps, cap),
+        owner, rank, ordered, *args,
+    )
+
+
+def steps(
+    first, owner, rank, ordered,
     tokens, frames, cotangent, buckets, lengths, slot_of, master, first_moment, second_moment,
     vectors, vector_first, vector_second,
 ):
@@ -981,14 +1051,18 @@
     slots = buckets.shape[0] // frame_count
     extent = frames.shape[1]
 
-    tiles = lax.all_gather(
-        master.astype(BF).transpose(0, 2, 1)[None], ("dp", "frame"), axis=0, tiled=True
-    )
-    tiles = tiles.reshape(group_count * frame_count * cap, master.shape[2], PANEL)
-    quarter_ids = jnp.arange(frame_count, dtype=jnp.int32)
-    where = (
-        ((slot_of // cap)[:, None] * frame_count + quarter_ids[None, :]) * cap
-        + (slot_of % cap)[:, None]
+    def gathered(part):
+        whole = lax.all_gather(part[None], ("dp", "frame"), axis=0, tiled=True)
+        return whole.reshape(-1, *part.shape[1:])
+
+    cuts = (0, first, cap) if first < cap else (0, cap)
+    tiles = [gathered(ordered[a:b]) for a, b in zip(cuts, cuts[1:])]
+    device = owner[:, None] * frame_count + jnp.arange(frame_count, dtype=jnp.int32)[None, :]
+    place_of = rank[:, None]
+    where = jnp.where(
+        place_of < first,
+        device * first + place_of,
+        group_count * frame_count * first + device * (cap - first) + place_of - first,
     ).reshape(-1)
 
     core, far = me & 1, me >> 1
@@ -1020,8 +1094,8 @@
     member, live = row_layout(own_bucket, own_length, row_count)
     layout = (member[:, None], live.astype(jnp.int32)[:, None], member[None, :])
 
-    key_table, value_table = call_tables(act, where, all_frames, vectors, tiles)
-    sum_one, cross_query, *saved = call_front(where, tokens, vectors, layout, tiles)
+    key_table, value_table = call_tables(act, where, all_frames, vectors, tiles[0])
+    sum_one, cross_query, *saved = call_front(where, tokens, vectors, layout, tiles[0])
     far_query = swap(cross_query, 2)
     own_part = call_cross_forward(infos[0], cross_query, key_table, value_table, 0)
     far_part = call_cross_forward(infos[1], far_query, key_table, value_table, slots)

time: 661 us -> 620 us (0.938)
  Pallas kernels: 276 us -> 227 us
  waiting for transfers between devices: 234 us -> 202 us
  starting transfers between devices: 19 us -> 45 us
  loops' own time: 0 us -> 8.34 us
    all_gather x1 -> x2, waiting for transfers between devices: 93.9 us -> 56.4 us  [gathered(): whole = lax.all_gather(part[None], ('dp', 'frame'), axis=0, tiled=True)]
    ppermute x14, starting transfers between devices: 8.66 us -> 29.5 us  [over_dp(): return lax.ppermute(x, 'dp', [(i, i ^ bit) for i in range(size)])]
    another operation x0 -> x2, local copies, waits for them, and re-layouts: none -> 17.8 us
    pallas_call x2, Pallas kernels: 70.9 us -> 54.4 us  [call_cross_backward(): pl.pallas_call(cross_backward_kernel, out_shape=(shape(count, D), shape(s...]
    dynamic_slice x1 -> x0, local copies, waits for them, and re-layouts: 13.6 us -> none  [halves(): first = lax.dynamic_index_in_dim(part, far, 0, False)]
    pallas_call x1, Pallas kernels: 32.2 us -> 20.2 us  [call_tables(): pl.pallas_call(tables_kernel, out_shape=(shape(slots, extent, D),) * 2, g...]
    pallas_call x1, Pallas kernels: 32.6 us -> 21.2 us  [call_table_gradient(): pl.pallas_call(table_gradient_kernel, out_shape=(part, part), grid_spec=p...]
    another operation x0 -> x1, loops' own time: none -> 8.34 us  [body(): lax.cond(soon, functools.partial(steps, FIRST), functools.partial(steps,...]
  transfers between devices with their start and end apart: 29 -> 30, of which waited for: 14 -> 18; matrix products, arithmetic and copies ran while one was open for 15% -> 16% of each run, Pallas kernels for 24% -> 25%
where the time goes in v3:
time: 620 us; the launch traced here: 613 us
  Pallas kernels  227 us (37%)
  waiting for transfers between devices  202 us (33%)
  other arithmetic  67.6 us (11%)
  local copies, waits for them, and re-layouts  47.9 us (8%)
  starting transfers between devices  45 us (7%)
  between operations  15 us (2%)
  loops' own time  8.34 us (1%)
    ppermute x14, waiting for transfers between devices, over_dp(): return lax.ppermute(x, 'dp', [(i, i ^ bit) for i in range(size)])  85.4 us
    ppermute x14, waiting for transfers between devices, swap(): return lax.ppermute(x, 'frame', [(i, i ^ bit) for i in range(4)])  60.3 us
    all_gather x2, waiting for transfers between devices, gathered(): whole = lax.all_gather(part[None], ('dp', 'frame'), axis=0, tiled=True)  56.4 us
    pallas_call x2, Pallas kernels, call_cross_backward(): pl.pallas_call(cross_backward_kernel, out_shape=(shape(count, D), shape(s...  54.4 us
    pallas_call x2, Pallas kernels, call_cross_forward(): pl.pallas_call(cross_forward_kernel, out_shape=shape(PARTIAL, D), grid_sp...  41.4 us
    pallas_call x1, Pallas kernels, call_middle(): pl.pallas_call(functools.partial(middle_kernel, len(tiles)), out_shape=(s...  32.3 us
    ppermute x14, starting transfers between devices, over_dp(): return lax.ppermute(x, 'dp', [(i, i ^ bit) for i in range(size)])  29.5 us
    convert_element_type x13, other arithmetic, added(): return (a.astype(F32) + b.astype(F32)).astype(BF)  23.1 us
  transfers between devices with their start and end apart: 30, of which 18 were waited for; matrix products, arithmetic and copies ran while one was open for 16% of the time, Pallas kernels for 25%

profile of v3, /device:TPU:0, one launch (start us, length us, event | category | flops | bytes accessed | tf_op | source)
XLA Modules:
  0.0 613.1 jit_solution(10414459364838330569)
XLA Ops:
  13.6 592.4 %conditional.1 = (f32[512,768]{1,0:T(8,128)}, f32[512,768]{1,0:T(8,128)}, f32[16,128,192]{1,2,0:T(8,128)}, f32[16,128,192]{1,2,0:T(8,128)}, f32[16,128,192]{1,2,...) conditional(s32[]{:T(128)} %convert_element_type.385, ...), branch_computations={%region_3.28_spmd, %region_28.53_spmd} | conditional | flops 263161380864 | bytes 592224960 | solution.py:1031
  20.1 17.7 %copy.88 = bf16[32,375,768]{2,1,0:T(8,128)(2,1)S(1)} copy(bf16[32,375,768]{2,0,1:T(8,128)(2,1)} %get-tuple-element.322) | data formatting | bytes 36864000 | tf_op jit(solution)/shard_map
  42.3 5.6 fusion.30
  64.7 6.0 fusion.29
  70.8 14.9 %pad_maximum_fusion.4.frames.frames_own.frames_far = bf16[16,768,768]{2,1,0:T(8,128)(2,1)} fusion(bf16[16,384,768]{2,1,0:T(8,128)(2,1)} %collective-permute-done.28, bf16[16,384,768]{2,1,0:T(8,128)(2,1)S(1)} %fusion.29), kind=kLoop, calls=%fused_computation.127 | loop fusion | flops 37748736 | bytes 37748736 | tf_op jit(solution)/shard_map/cond/branch_1_fun/concatenate | solution.py:1080
  85.7 50.6 %all-gather.9.cloned.1.call-done.tiles.refs_0_ = bf16[320,192,128]{2,1,0:T(8,128)(2,1)} async-done(((bf16[10,192,128]{2,1,0:T(8,128)(2,1)}), bf16[320,192,128]{2,1,0:T(8,128)(2,1)}) %all-gather.9.cloned.1.call-update) | async-done | bytes 15728656 | tf_op jit(solution)/shard_map/cond/branch_1_fun/all_gather | solution.py:1055
  136.3 16.0 %front.3 = (f32[512,768]{1,0:T(8,128)}, bf16[512,768]{1,0:T(8,128)(2,1)}, bf16[512,768]{1,0:T(8,128)(2,1)}, bf16[512,768]{1,0:T(8,128)(2,1)}, bf16[512,768]{1,0:...) custom-call(s32[384]{0:T(512)} %reshape.633.where, bf16[512,768]{1,0:T(8,128)(2,1)S(1)} %copy-done.54, ...), custom_call_target="tpu_custom_call" | custom-call | flops 16000000000 | bytes 1048576 | tf_op jit(solution)/shard_map/cond/branch_1_fun/front/pallas_call | solution.py:679
  153.9 20.2 %tables.3 = (bf16[16,768,768]{2,1,0:T(8,128)(2,1)}, bf16[16,768,768]{2,1,0:T(8,128)(2,1)}) custom-call(s32[17]{0:T(128)} %pad_add_fusion.1.act, s32[384]{0:T(512)} %reshape.633.where, bf16[16,768,768]{2,1,0:T(8,128)(2,1)} %pad_maximum_fusion.4.frames.frames_own.frames_far, f32[19,768]{1,0:T(8,128)S(1)} %copy-done.20, ...), custom_call_target="tpu_custom_call" | custom-call | flops 30000001024 | bytes 1048576 | tf_op jit(solution)/shard_map/cond/branch_1_fun/tables/pallas_call | solution.py:706
  179.4 20.5 %cross_forward.7 = bf16[544,768]{1,0:T(8,128)(2,1)} custom-call(s32[26]{0:T(128)} %concatenate.140.info.info_far, bf16[512,768]{1,0:T(8,128)(2,1)} %copy-done.58, bf16[16,768,768]{2,1,0:T(8,128)(2,1)} %get-tuple-element.133.key_table, bf16[16,768,768]{2,1,0:T(8,128)(2,1)} %get-tuple-element.134.value_table), custom_call_target="tpu_custom_call" | custom-call | flops 23000000512 | bytes 1048576 | tf_op jit(solution)/shard_map/cond/branch_1_fun/cross_forward/pallas_call | solution.py:730
  203.1 20.9 %cross_forward.6.own = bf16[544,768]{1,0:T(8,128)(2,1)} custom-call(s32[26]{0:T(128)} %concatenate.132.info.info_own, bf16[512,768]{1,0:T(8,128)(2,1)} %get-tuple-element.131.query, bf16[16,768,768]{2,1,0:T(8,128)(2,1)} %get-tuple-element.133.key_table, bf16[16,768,768]{2,1,0:T(8,128)(2,1)} %get-tuple-element.134.value_table), custom_call_target="tpu_custom_call" | custom-call | flops 23000000512 | bytes 1048576 | tf_op jit(solution)/shard_map/cond/branch_1_fun/cross_forward/pallas_call | solution.py:730
  224.0 5.7 all-gather.11.cloned.1.call-done.refs_1_
  230.6 32.3 %middle.3 = (f32[512,768]{1,0:T(8,128)}, f32[512,768]{1,0:T(8,128)}, bf16[560,768]{1,0:T(8,128)(2,1)}, f32[16,768]{1,0:T(8,128)}, bf16[2,54,192,128]{3,2,1,0:T(8,128)(2,1)}, /*index=5*/bf16[2,54,192,128]{3,2,1,0:T(8,128)(2,1)}) custom-call(s32[384]{0:T(512)} %reshape.633.where, s32[1]{0:T(128)} %bitcast.52.me, f32[512,768]{1,0:T(8,128)} %get-tuple-element.130.sum_one, ...), custom_call_target="tpu_custom_call" | custom-call | flops 33999998976 | bytes 1048576 | tf_op jit(solution)/shard_map/cond/branch_1_fun/middle/pallas_call | solution.py:815
  263.9 8.3 %collective-permute-done.31 = bf16[2,54,192,128]{3,2,1,0:T(8,128)(2,1)} collective-permute-done((bf16[2,54,192,128]{3,2,1,0:T(8,128)(2,1)}, bf16[2,54,192,128]{3,2,1,0:T(8,128)(2,1)}, u32[]{:S(2)}, u32[]{:S(2)}) %collective-permute-start.31) | collective-permute-done | bytes 5308448 | tf_op jit(solution)/shard_map/cond/branch_1_fun/ppermute | solution.py:961
  272.1 6.4 %add_convert_fusion.9.earlier.also_earlier = bf16[2,54,192,128]{3,2,1,0:T(8,128)(2,1)S(1)} fusion(bf16[2,54,192,128]{3,2,1,0:T(8,128)(2,1)} %collective-permute-done.31, bf16[2,54,192,128]{3,2,1,0:T(8,128)(2,1)} %get-tuple-element.140), kind=kLoop, calls=%fused_computation.128 | loop fusion | flops 10616832 | bytes 15925248 | tf_op jit(solution)/shard_map/cond/branch_1_fun/convert_element_type | solution.py:970
  282.4 28.2 %cross_backward.6 = (bf16[512,768]{1,0:T(8,128)(2,1)}, bf16[8,768,768]{2,1,0:T(8,128)(2,1)}, bf16[8,768,768]{2,1,0:T(8,128)(2,1)}, f32[8,768]{1,0:T(8,128)}) custom-call(s32[26]{0:T(128)} %concatenate.132.info.info_own, bf16[512,768]{1,0:T(8,128)(2,1)} %get-tuple-element.131.query, bf16[560,768]{1,0:T(8,128)(2,1)} %get-tuple-element.139.packed, ...), custom_call_target="tpu_custom_call" | custom-call | flops 40000000000 | bytes 1048576 | tf_op jit(solution)/shard_map/cond/branch_1_fun/cross_backward/pallas_call | solution.py:754
  314.8 26.2 %cross_backward.7 = (bf16[512,768]{1,0:T(8,128)(2,1)}, bf16[8,768,768]{2,1,0:T(8,128)(2,1)}, bf16[8,768,768]{2,1,0:T(8,128)(2,1)}, f32[8,768]{1,0:T(8,128)}) custom-call(s32[26]{0:T(128)} %concatenate.140.info.info_far, bf16[512,768]{1,0:T(8,128)(2,1)} %copy-done.58, bf16[560,768]{1,0:T(8,128)(2,1)} %collective-permute-done.32.packed, ...), custom_call_target="tpu_custom_call" | custom-call | flops 40000000000 | bytes 1048576 | tf_op jit(solution)/shard_map/cond/branch_1_fun/cross_backward/pallas_call | solution.py:754
  344.8 8.8 %collective-permute-done.35 = bf16[36,192,128]{2,1,0:T(8,128)(2,1)S(1)} collective-permute-done((bf16[36,192,128]{2,1,0:T(8,128)(2,1)S(1)}, bf16[36,192,128]{2,1,0:T(8,128)(2,1)S(1)}, u32[]{:S(2)}, u32[]{:S(2)}) %collective-permute-start.35) | collective-permute-done | bytes 1769504 | tf_op jit(solution)/shard_map/cond/branch_1_fun/ppermute | solution.py:961
  360.3 21.2 %table_gradient.3 = (bf16[2,12,192,128]{3,2,1,0:T(8,128)(2,1)}, bf16[2,12,192,128]{3,2,1,0:T(8,128)(2,1)}) custom-call(s32[26]{0:T(128)} %concatenate.132.info.info_own, s32[26]{0:T(128)} %concatenate.140.info.info_far, s32[1]{0:T(128)} %bitcast.52.me, bf16[8,768,768]{2,1,0:T(8,128)(2,1)} %get-tuple-element.144.key_own, ...), custom_call_target="tpu_custom_call" | custom-call | flops 20000000000 | bytes 1048576 | tf_op jit(solution)/shard_map/cond/branch_1_fun/table_gradient/pallas_call | solution.py:791
  381.4 7.9 %collective-permute-done.36 = bf16[5184,128]{1,0:T(8,128)(2,1)} collective-permute-done((bf16[5184,128]{1,0:T(8,128)(2,1)S(1)}, bf16[5184,128]{1,0:T(8,128)(2,1)}, u32[]{:S(2)}, u32[]{:S(2)}) %collective-permute-start.36) | collective-permute-done | bytes 1327136 | tf_op jit(solution)/shard_map/cond/branch_1_fun/ppermute | solution.py:966
  392.1 9.0 %cross_back.3 = (f32[512,768]{1,0:T(8,128)}, bf16[512,768]{1,0:T(8,128)(2,1)}, f32[8,768]{1,0:T(8,128)}, bf16[2,12,192,128]{3,2,1,0:T(8,128)(2,1)}, bf16[2,12,192,128]{3,2,1,0:T(8,128)(2,1)}) custom-call(s32[384]{0:T(512)} %reshape.633.where, s32[1]{0:T(128)} %bitcast.52.me, f32[512,768]{1,0:T(8,128)} %get-tuple-element.130.sum_one, ...), custom_call_target="tpu_custom_call" | custom-call | flops 8000000000 | bytes 1048576 | tf_op jit(solution)/shard_map/cond/branch_1_fun/cross_back/pallas_call | solution.py:846
  409.6 21.9 %last.3 = (f32[512,768]{1,0:T(8,128)}, f32[8,768]{1,0:T(8,128)}, bf16[2,18,192,128]{3,2,1,0:T(8,128)(2,1)}, bf16[2,18,192,128]{3,2,1,0:T(8,128)(2,1)}) custom-call(s32[384]{0:T(512)} %reshape.633.where, s32[1]{0:T(128)} %bitcast.52.me, bf16[512,768]{1,0:T(8,128)(2,1)S(1)} %copy-done.55, f32[512,768]{1,0:T(8,128)} %get-tuple-element.149.grad_one, ...), custom_call_target="tpu_custom_call" | custom-call | flops 20000000000 | bytes 1048576 | tf_op jit(solution)/shard_map/cond/branch_1_fun/last/pallas_call | solution.py:866
  439.5 5.6 collective-permute-start.38
  445.1 16.8 %collective-permute-done.42 = bf16[24,192,128]{2,1,0:T(8,128)(2,1)} collective-permute-done((bf16[24,192,128]{2,1,0:T(8,128)(2,1)}, bf16[24,192,128]{2,1,0:T(8,128)(2,1)}, u32[]{:S(2)}, u32[]{:S(2)}) %collective-permute-start.42) | collective-permute-done | bytes 1179680 | tf_op jit(solution)/shard_map/cond/branch_1_fun/ppermute | solution.py:961
  463.9 16.4 %collective-permute-done.44 = bf16[18,192,128]{2,1,0:T(8,128)(2,1)} collective-permute-done((bf16[18,192,128]{2,1,0:T(8,128)(2,1)}, bf16[18,192,128]{2,1,0:T(8,128)(2,1)}, u32[]{:S(2)}, u32[]{:S(2)}) %collective-permute-start.44) | collective-permute-done | bytes 884768 | tf_op jit(solution)/shard_map/cond/branch_1_fun/ppermute | solution.py:961
  490.8 16.8 %collective-permute-done.45 = bf16[4032,128]{1,0:T(8,128)(2,1)} collective-permute-done((bf16[4032,128]{1,0:T(8,128)(2,1)}, bf16[4032,128]{1,0:T(8,128)(2,1)}, u32[]{:S(2)}, u32[]{:S(2)}) %collective-permute-start.45) | collective-permute-done | bytes 1032224 | tf_op jit(solution)/shard_map/cond/branch_1_fun/ppermute | solution.py:966
  509.1 5.6 collective-permute-start.46
  517.3 15.3 %collective-permute-done.46 = bf16[2016,128]{1,0:T(8,128)(2,1)S(1)} collective-permute-done((bf16[2016,128]{1,0:T(8,128)(2,1)S(1)}, bf16[2016,128]{1,0:T(8,128)(2,1)S(1)}, u32[]{:S(2)}, u32[]{:S(2)}) %collective-permute-start.46) | collective-permute-done | bytes 516128 | tf_op jit(solution)/shard_map/cond/branch_1_fun/ppermute | solution.py:966
  537.7 8.4 %collective-permute-done.47 = bf16[1008,128]{1,0:T(8,128)(2,1)S(1)} collective-permute-done((bf16[1008,128]{1,0:T(8,128)(2,1)S(1)}, bf16[1008,128]{1,0:T(8,128)(2,1)S(1)}, u32[]{:S(2)}, u32[]{:S(2)}) %collective-permute-start.47) | collective-permute-done | bytes 258080 | tf_op jit(solution)/shard_map/cond/branch_1_fun/ppermute | solution.py:966
  553.3 8.6 %collective-permute-done.53 = f32[24,768]{1,0:T(8,128)S(1)} collective-permute-done((f32[24,768]{1,0:T(8,128)S(1)}, f32[24,768]{1,0:T(8,128)S(1)}, u32[]{:S(2)}, u32[]{:S(2)}) %collective-permute-start.53) | collective-permute-done | bytes 73760 | tf_op jit(solution)/shard_map/cond/branch_1_fun/ppermute | solution.py:966
  568.5 7.1 %collective-permute-done.49 = bf16[2016,128]{1,0:T(8,128)(2,1)S(1)} collective-permute-done((bf16[2016,128]{1,0:T(8,128)(2,1)S(1)}, bf16[2016,128]{1,0:T(8,128)(2,1)S(1)}, u32[]{:S(2)}, u32[]{:S(2)}) %collective-permute-start.49) | collective-permute-done | bytes 516128 | tf_op jit(solution)/shard_map/cond/branch_1_fun/ppermute | solution.py:966
  581.3 15.5 %collective-permute-done.55.got = bf16[16,192,128]{2,1,0:T(8,128)(2,1)S(1)} collective-permute-done((bf16[16,192,128]{2,1,0:T(8,128)(2,1)}, bf16[16,192,128]{2,1,0:T(8,128)(2,1)S(1)}, u32[]{:S(2)}, u32[]{:S(2)}) %collective-permute-start.55) | collective-permute-done | bytes 786464 | tf_op jit(solution)/shard_map/cond/branch_1_fun/ppermute | solution.py:966
  597.8 8.0 %update.3 = (f32[16,192,128]{2,1,0:T(8,128)}, f32[16,192,128]{2,1,0:T(8,128)}, f32[16,192,128]{2,1,0:T(8,128)}, f32[16,192,128]{2,1,0:T(8,128)}) custom-call(s32[16]{0:T(128)} %get-tuple-element.352.place, s32[16]{0:T(128)} %fusion.47.source, bf16[5184,128]{1,0:T(8,128)(2,1)} %maximum_select_fusion.4.early, bf16[4032,128]{1,0:T(8,128)(2,1)} %maximum_select_fusion.5.late, ...), custom_call_target="tpu_custom_call" | custom-call | flops 6000000000 | bytes 1048576 | tf_op jit(solution)/shard_map/cond/branch_1_fun/update/pallas_call | solution.py:904
  (203 shorter events, 117.1 us)
Async XLA Ops:
  19.1 117.2 %all-gather.9.cloned.1.call-start = ((), (), s32[]{:S(2)}) async-start(), calls=%async_computation.1 | async-start | bytes 16220160 | tf_op jit(solution)/shard_map/cond/branch_1_fun/all_gather | solution.py:1055
  20.0 209.7 %all-gather.11.cloned.1.call-start = ((), (), s32[]{:S(2)}) async-start(), calls=%async_computation.2 | async-start | bytes 9732096 | tf_op jit(solution)/shard_map/cond/branch_1_fun/all_gather | solution.py:1055
  47.9 22.9 %collective-permute-start.28 = (bf16[16,384,768]{2,1,0:T(8,128)(2,1)}, bf16[16,384,768]{2,1,0:T(8,128)(2,1)}, u32[]{:S(2)}, u32[]{:S(2)}) collective-permute-start(bf16[16,384,768]{2,1,0:T(8,128)(2,1)} %fusion.30), channel_id=1, source_target_pairs={{0,1},{1,0},{2,3},{3,2},{4,5},{5,4},{6,7},{7,6},{8,9},{9,8},{10,11... | collective-permute-start | bytes 28311560 | tf_op jit(solution)/shard_map/cond/branch_1_fun/ppermute | solution.py:961
  70.8 65.6 %copy-start.20 = (f32[19,768]{1,0:T(8,128)S(1)}, f32[19,768]{1,0:T(8,128)}, u32[]{:S(2)}) copy-start(f32[19,768]{1,0:T(8,128)} %get-tuple-element.126.vectors) | copy-start | bytes 175108 | tf_op jit(solution)/shard_map/cond
  70.8 65.6 %copy-start.54 = (bf16[512,768]{1,0:T(8,128)(2,1)S(1)}, bf16[512,768]{1,0:T(8,128)(2,1)}, u32[]{:S(2)}) copy-start(bf16[512,768]{1,0:T(8,128)(2,1)} %get-tuple-element.125.tokens) | copy-start | bytes 2359300 | tf_op jit(solution)/shard_map/cond
  152.4 26.1 %collective-permute-start.29 = (bf16[512,768]{1,0:T(8,128)(2,1)}, bf16[512,768]{1,0:T(8,128)(2,1)S(1)}, u32[]{:S(2)}, u32[]{:S(2)}) collective-permute-start(bf16[512,768]{1,0:T(8,128)(2,1)} %get-tuple-element.131.query), channel_id=1, source_target_pairs={{0,2},{1,3},{2,0},{3,1},{4,6},{5,7},{6,4},{7,5},{8,10},{9,11},{10,... | collective-permute-start | bytes 2359304 | tf_op jit(solution)/shard_map/cond/branch_1_fun/ppermute | solution.py:961
  199.9 29.9 %collective-permute-start.30 = (bf16[544,768]{1,0:T(8,128)(2,1)}, bf16[544,768]{1,0:T(8,128)(2,1)S(1)}, u32[]{:S(2)}, u32[]{:S(2)}) collective-permute-start(bf16[544,768]{1,0:T(8,128)(2,1)} %cross_forward.7), channel_id=1, source_target_pairs={{0,2},{1,3},{2,0},{3,1},{4,6},{5,7},{6,4},{7,5},{8,10},{9,11},{10,... | collective-permute-start | bytes 2506760 | tf_op jit(solution)/shard_map/cond/branch_1_fun/ppermute | solution.py:961
  263.0 9.2 %collective-permute-start.31 = (bf16[2,54,192,128]{3,2,1,0:T(8,128)(2,1)}, bf16[2,54,192,128]{3,2,1,0:T(8,128)(2,1)}, u32[]{:S(2)}, u32[]{:S(2)}) collective-permute-start(bf16[2,54,192,128]{3,2,1,0:T(8,128)(2,1)} %get-tuple-element.141), channel_id=1, source_target_pairs={{0,1},{1,0},{2,3},{3,2},{4,5},{5,4},{6,7},{7,6},{8,9},{9,8},{10,11... | collective-permute-start | bytes 15925256 | tf_op jit(solution)/shard_map/cond/branch_1_fun/ppermute | solution.py:961
  263.3 51.5 %collective-permute-start.32 = (bf16[560,768]{1,0:T(8,128)(2,1)}, bf16[560,768]{1,0:T(8,128)(2,1)}, u32[]{:S(2)}, u32[]{:S(2)}) collective-permute-start(bf16[560,768]{1,0:T(8,128)(2,1)} %get-tuple-element.139.packed), channel_id=1, source_target_pairs={{0,2},{1,3},{2,0},{3,1},{4,6},{5,7},{6,4},{7,5},{8,10},{9,11},{10,... | collective-permute-start | bytes 2580488 | tf_op jit(solution)/shard_map/cond/branch_1_fun/ppermute | solution.py:961
  281.8 30.4 %collective-permute-start.33 = (bf16[18,192,128]{2,1,0:T(8,128)(2,1)}, bf16[18,192,128]{2,1,0:T(8,128)(2,1)}, u32[]{:S(2)}, u32[]{:S(2)}) collective-permute-start(bf16[18,192,128]{2,1,0:T(8,128)(2,1)} %slice_bitcast_fusion.14), channel_id=1, source_target_pairs={{0,2},{1,3},{2,0},{3,1},{4,6},{5,7},{6,4},{7,5},{8,10},{9,11},{10,... | collective-permute-start | bytes 2654216 | tf_op jit(solution)/shard_map/cond/branch_1_fun/ppermute | solution.py:961
  312.1 41.5 %collective-permute-start.35 = (bf16[36,192,128]{2,1,0:T(8,128)(2,1)S(1)}, bf16[36,192,128]{2,1,0:T(8,128)(2,1)S(1)}, u32[]{:S(2)}, u32[]{:S(2)}) collective-permute-start(bf16[36,192,128]{2,1,0:T(8,128)(2,1)S(1)} %slice_bitcast_fusion.8), channel_id=1, source_target_pairs={{0,2},{1,3},{2,0},{3,1},{4,6},{5,7},{6,4},{7,5},{8,10},{9,11},{10,... | collective-permute-start | bytes 5308424 | tf_op jit(solution)/shard_map/cond/branch_1_fun/ppermute | solution.py:961
  341.1 51.0 %collective-permute-start.34 = (bf16[512,768]{1,0:T(8,128)(2,1)}, bf16[512,768]{1,0:T(8,128)(2,1)}, u32[]{:S(2)}, u32[]{:S(2)}) collective-permute-start(bf16[512,768]{1,0:T(8,128)(2,1)} %get-tuple-element.143), channel_id=1, source_target_pairs={{0,2},{1,3},{2,0},{3,1},{4,6},{5,7},{6,4},{7,5},{8,10},{9,11},{10,... | collective-permute-start | bytes 2359304 | tf_op jit(solution)/shard_map/cond/branch_1_fun/ppermute | solution.py:961
  358.6 30.8 %collective-permute-start.36 = (bf16[5184,128]{1,0:T(8,128)(2,1)S(1)}, bf16[5184,128]{1,0:T(8,128)(2,1)}, u32[]{:S(2)}, u32[]{:S(2)}) collective-permute-start(bf16[5184,128]{1,0:T(8,128)(2,1)S(1)} %constant_dynamic-slice_fusion.14), channel_id=1, source_target_pairs={{0,4},{4,0},{8,12},{12,8},{16,20},{20,16},{24,28},{28,24},{1,5},{5... | collective-permute-start | bytes 3981320 | tf_op jit(solution)/shard_map/cond/branch_1_fun/ppermute | solution.py:966
  402.8 4.6 collective-permute-start.37
  431.5 4.0 collective-permute-start.43
  432.8 29.1 %collective-permute-start.42 = (bf16[24,192,128]{2,1,0:T(8,128)(2,1)}, bf16[24,192,128]{2,1,0:T(8,128)(2,1)}, u32[]{:S(2)}, u32[]{:S(2)}) collective-permute-start(bf16[24,192,128]{2,1,0:T(8,128)(2,1)} %slice_bitcast_fusion.10), channel_id=1, source_target_pairs={{0,2},{1,3},{2,0},{3,1},{4,6},{5,7},{6,4},{7,5},{8,10},{9,11},{10,... | collective-permute-start | bytes 3538952 | tf_op jit(solution)/shard_map/cond/branch_1_fun/ppermute | solution.py:961
  437.1 43.2 %collective-permute-start.44 = (bf16[18,192,128]{2,1,0:T(8,128)(2,1)}, bf16[18,192,128]{2,1,0:T(8,128)(2,1)}, u32[]{:S(2)}, u32[]{:S(2)}) collective-permute-start(bf16[18,192,128]{2,1,0:T(8,128)(2,1)} %slice_bitcast_fusion.12), channel_id=1, source_target_pairs={{0,2},{1,3},{2,0},{3,1},{4,6},{5,7},{6,4},{7,5},{8,10},{9,11},{10,... | collective-permute-start | bytes 2654216 | tf_op jit(solution)/shard_map/cond/branch_1_fun/ppermute | solution.py:961
  439.5 45.2 %collective-permute-start.38 = (bf16[2592,128]{1,0:T(8,128)(2,1)}, bf16[2592,128]{1,0:T(8,128)(2,1)}, u32[]{:S(2)}, u32[]{:S(2)}) collective-permute-start(bf16[2592,128]{1,0:T(8,128)(2,1)} %constant_dynamic-slice_fusion.13), channel_id=1, source_target_pairs={{0,8},{4,12},{8,0},{12,4},{16,24},{20,28},{24,16},{28,20},{1,9},{5... | collective-permute-start | bytes 1990664 | tf_op jit(solution)/shard_map/cond/branch_1_fun/ppermute | solution.py:966
  483.0 24.6 %collective-permute-start.45 = (bf16[4032,128]{1,0:T(8,128)(2,1)}, bf16[4032,128]{1,0:T(8,128)(2,1)}, u32[]{:S(2)}, u32[]{:S(2)}) collective-permute-start(bf16[4032,128]{1,0:T(8,128)(2,1)} %constant_dynamic-slice_fusion.11), channel_id=1, source_target_pairs={{0,4},{4,0},{8,12},{12,8},{16,20},{20,16},{24,28},{28,24},{1,5},{5... | collective-permute-start | bytes 3096584 | tf_op jit(solution)/shard_map/cond/branch_1_fun/ppermute | solution.py:966
  486.1 29.5 %collective-permute-start.39 = (bf16[1296,128]{1,0:T(8,128)(2,1)S(1)}, bf16[1296,128]{1,0:T(8,128)(2,1)S(1)}, u32[]{:S(2)}, u32[]{:S(2)}) collective-permute-start(bf16[1296,128]{1,0:T(8,128)(2,1)S(1)} %constant_dynamic-slice_fusion.12), channel_id=1, source_target_pairs={{0,16},{4,20},{8,24},{12,28},{16,0},{20,4},{24,8},{28,12},{1,17},{... | collective-permute-start | bytes 995336 | tf_op jit(solution)/shard_map/cond/branch_1_fun/ppermute | solution.py:966
  509.1 23.5 %collective-permute-start.46 = (bf16[2016,128]{1,0:T(8,128)(2,1)S(1)}, bf16[2016,128]{1,0:T(8,128)(2,1)S(1)}, u32[]{:S(2)}, u32[]{:S(2)}) collective-permute-start(bf16[2016,128]{1,0:T(8,128)(2,1)S(1)} %constant_dynamic-slice_fusion.10), channel_id=1, source_target_pairs={{0,8},{4,12},{8,0},{12,4},{16,24},{20,28},{24,16},{28,20},{1,9},{5... | collective-permute-start | bytes 1548296 | tf_op jit(solution)/shard_map/cond/branch_1_fun/ppermute | solution.py:966
  515.6 17.9 %collective-permute-start.40 = (bf16[1296,128]{1,0:T(8,128)(2,1)S(1)}, bf16[1296,128]{1,0:T(8,128)(2,1)S(1)}, u32[]{:S(2)}, u32[]{:S(2)}) collective-permute-start(bf16[1296,128]{1,0:T(8,128)(2,1)S(1)} %add_convert_fusion.16), channel_id=1, source_target_pairs={{0,16},{4,20},{8,24},{12,28},{16,0},{20,4},{24,8},{28,12},{1,17},{... | collective-permute-start | bytes 995336 | tf_op jit(solution)/shard_map/cond/branch_1_fun/ppermute | solution.py:966
  517.2 19.1 %collective-permute-start.50 = (f32[24,768]{1,0:T(8,128)S(1)}, f32[24,768]{1,0:T(8,128)S(1)}, u32[]{:S(2)}, u32[]{:S(2)}) collective-permute-start(f32[24,768]{1,0:T(8,128)S(1)} %concatenate.153), channel_id=1, source_target_pairs={{0,1},{1,0},{2,3},{3,2},{4,5},{5,4},{6,7},{7,6},{8,9},{9,8},{10,11... | collective-permute-start | bytes 221192 | tf_op jit(solution)/shard_map/cond/branch_1_fun/ppermute | solution.py:961
  532.8 13.3 %collective-permute-start.47 = (bf16[1008,128]{1,0:T(8,128)(2,1)S(1)}, bf16[1008,128]{1,0:T(8,128)(2,1)S(1)}, u32[]{:S(2)}, u32[]{:S(2)}) collective-permute-start(bf16[1008,128]{1,0:T(8,128)(2,1)S(1)} %constant_dynamic-slice_fusion.9), channel_id=1, source_target_pairs={{0,16},{4,20},{8,24},{12,28},{16,0},{20,4},{24,8},{28,12},{1,17},{... | collective-permute-start | bytes 774152 | tf_op jit(solution)/shard_map/cond/branch_1_fun/ppermute | solution.py:966
  533.8 30.6 %collective-permute-start.41 = (bf16[2592,128]{1,0:T(8,128)(2,1)S(1)}, bf16[2592,128]{1,0:T(8,128)(2,1)S(1)}, u32[]{:S(2)}, u32[]{:S(2)}) collective-permute-start(bf16[2592,128]{1,0:T(8,128)(2,1)S(1)} %maximum_select_fusion.6), channel_id=1, source_target_pairs={{0,8},{4,12},{8,0},{12,4},{16,24},{20,28},{24,16},{28,20},{1,9},{5... | collective-permute-start | bytes 1990664 | tf_op jit(solution)/shard_map/cond/branch_1_fun/ppermute | solution.py:966
  536.3 10.0 %collective-permute-start.51 = (f32[24,768]{1,0:T(8,128)S(1)}, f32[24,768]{1,0:T(8,128)S(1)}, u32[]{:S(2)}, u32[]{:S(2)}) collective-permute-start(f32[24,768]{1,0:T(8,128)S(1)} %add.497), channel_id=1, source_target_pairs={{0,2},{1,3},{2,0},{3,1},{4,6},{5,7},{6,4},{7,5},{8,10},{9,11},{10,... | collective-permute-start | bytes 221192 | tf_op jit(solution)/shard_map/cond/branch_1_fun/ppermute | solution.py:961
  546.2 16.3 %collective-permute-start.48 = (bf16[1008,128]{1,0:T(8,128)(2,1)S(1)}, bf16[1008,128]{1,0:T(8,128)(2,1)S(1)}, u32[]{:S(2)}, u32[]{:S(2)}) collective-permute-start(bf16[1008,128]{1,0:T(8,128)(2,1)S(1)} %add_convert_fusion.17), channel_id=1, source_target_pairs={{0,16},{4,20},{8,24},{12,28},{16,0},{20,4},{24,8},{28,12},{1,17},{... | collective-permute-start | bytes 774152 | tf_op jit(solution)/shard_map/cond/branch_1_fun/ppermute | solution.py:966
  546.3 4.4 collective-permute-start.52
  550.8 11.2 %collective-permute-start.53 = (f32[24,768]{1,0:T(8,128)S(1)}, f32[24,768]{1,0:T(8,128)S(1)}, u32[]{:S(2)}, u32[]{:S(2)}) collective-permute-start(f32[24,768]{1,0:T(8,128)S(1)} %add.499), channel_id=1, source_target_pairs={{0,8},{4,12},{8,0},{12,4},{16,24},{20,28},{24,16},{28,20},{1,9},{5... | collective-permute-start | bytes 221192 | tf_op jit(solution)/shard_map/cond/branch_1_fun/ppermute | solution.py:966
  562.0 5.7 collective-permute-start.54
  562.7 12.9 %collective-permute-start.49 = (bf16[2016,128]{1,0:T(8,128)(2,1)S(1)}, bf16[2016,128]{1,0:T(8,128)(2,1)S(1)}, u32[]{:S(2)}, u32[]{:S(2)}) collective-permute-start(bf16[2016,128]{1,0:T(8,128)(2,1)S(1)} %maximum_select_fusion.7), channel_id=1, source_target_pairs={{0,8},{4,12},{8,0},{12,4},{16,24},{20,28},{24,16},{28,20},{1,9},{5... | collective-permute-start | bytes 1548296 | tf_op jit(solution)/shard_map/cond/branch_1_fun/ppermute | solution.py:966
  579.7 17.2 %collective-permute-start.55 = (bf16[16,192,128]{2,1,0:T(8,128)(2,1)}, bf16[16,192,128]{2,1,0:T(8,128)(2,1)S(1)}, u32[]{:S(2)}, u32[]{:S(2)}) collective-permute-start(bf16[16,192,128]{2,1,0:T(8,128)(2,1)} %pick.3), channel_id=1, source_target_pairs={{0,4},{4,0},{8,12},{12,8},{16,20},{20,16},{24,28},{28,24},{1,5},{5... | collective-permute-start | bytes 2359304 | tf_op jit(solution)/shard_map/cond/branch_1_fun/ppermute | solution.py:966
  (28 other events, 423.5 us)
Sparse Core Ops, SparseCore 0:
  23.5 112.8 all-gather.8
  139.8 89.8 all-gather.10
